TPU v7x, 128 devices: a whole 4x4x4 slice. The times are simulated.
128 devices in a mesh: gx: 16 (over z_hi, y, core), ta: 8 (over z_lo, x).
Axes of the slice: x: 4, y: 4, z: 4 (z_hi: 2, z_lo: 2; z = z_hi * 2 + z_lo), core: 2. Of those that a mesh axis runs over, the one named last changes fastest.
Arguments:
- initial_state: float32 [128, 256, 128], P('gx'), may hold values from -10 to 10
- reaction: float32 [128, 256, 128], P('gx'), may hold values from 0.02 to 0.1
- source: float32 [128, 256, 128], P('gx'), may hold values from -4 to 4
Outputs:
- interval_ends: float32 [8, 128, 256, 128], P('ta', 'gx')
All inputs are finite; a program needn't handle non-finite values.
Results may differ from a plain program's by a relative error of at most 0.00002.
Values sent between devices are 32-bit elements; how exact they have to be, the bound alone decides.
No kernel may reach another device: no remote copies, remote signals or barrier semaphores. Data moves between devices by JAX's collectives and lax.ppermute only.
A program may use at most 64 MiB of HBM per device.

v0:
```python
import jax
import jax.numpy as jnp
from jax import lax
from jax.sharding import PartitionSpec as P

STEPS = 8
ITERS = 2


robin_weight = 0.5
diffusion = 0.1
speed_x = 0.2
speed_y = 0.1
speed_z = 0.1


def from_behind(block, axis, distance):
    devices = range(lax.axis_size(axis))
    route = [(i - distance, i) for i in devices if i - distance in devices]
    return lax.ppermute(block, axis, route)


def advance_field(field, lower_ghost, upper_ghost, reaction, source):
    stacked = jnp.concatenate([lower_ghost[None], field, upper_ghost[None]], axis=0)
    padded = jnp.pad(stacked, ((0, 0), (1, 1), (1, 1)))
    x_below = padded[:-2, 1:-1, 1:-1]
    x_above = padded[2:, 1:-1, 1:-1]
    y_below = padded[1:-1, :-2, 1:-1]
    y_above = padded[1:-1, 2:, 1:-1]
    z_below = padded[1:-1, 1:-1, :-2]
    z_above = padded[1:-1, 1:-1, 2:]
    laplace = x_below + x_above + y_below + y_above + z_below + z_above - 6.0 * field
    advect = speed_x * (field - x_below) + speed_y * (field - y_below) + speed_z * (field - z_below)
    return (field + diffusion * laplace - advect + source) / (1.0 + reaction)


def down_trace(first_plane, second_plane):
    return second_plane - first_plane + robin_weight * (first_plane + second_plane) / 2.0


def up_trace(last_plane, before_last):
    return before_last - last_plane + robin_weight * (last_plane + before_last) / 2.0


def run_interval(field, lower_series, upper_series, reaction, source, is_first, is_last):
    low_edges = []
    high_edges = []
    for moment in range(STEPS):
        first_plane = field[0]
        last_plane = field[-1]
        low_edges.append(field[0:2])
        high_edges.append(jnp.stack([field[-1], field[-2]]))
        lower_ghost = (lower_series[moment] + (1.0 - robin_weight / 2.0) * first_plane) / (
            1.0 + robin_weight / 2.0
        )
        upper_ghost = (upper_series[moment] + (1.0 - robin_weight / 2.0) * last_plane) / (
            1.0 + robin_weight / 2.0
        )
        lower_ghost = jnp.where(is_first, 0.0, lower_ghost)
        upper_ghost = jnp.where(is_last, 0.0, upper_ghost)
        field = advance_field(field, lower_ghost, upper_ghost, reaction, source)
    return (field, jnp.stack(low_edges), jnp.stack(high_edges))


def local(initial_state, reaction, source):
    interval = lax.axis_index("ta")
    intervals = lax.axis_size("ta")
    slab_index = lax.axis_index("gx")
    slab_count = lax.axis_size("gx")
    is_first = slab_index == 0
    is_last = slab_index == slab_count - 1
    rows_y = initial_state.shape[1]
    rows_z = initial_state.shape[2]
    zero_series = jnp.zeros((STEPS, rows_y, rows_z), jnp.float32)

    def slot(slot_index, carry):
        incoming, kept_lower, kept_upper, result = carry
        level = slot_index - interval
        start = jnp.where(interval == 0, initial_state, incoming)
        lower_series = jnp.where(level >= 1, kept_lower, 0.0)
        upper_series = jnp.where(level >= 1, kept_upper, 0.0)
        final_state, low_edges, high_edges = run_interval(
            start, lower_series, upper_series, reaction, source, is_first, is_last
        )
        from_below = from_behind(high_edges, "gx", 1)
        from_above = from_behind(low_edges, "gx", -1)
        new_lower = up_trace(from_below[:, 0], from_below[:, 1])
        new_upper = down_trace(from_above[:, 0], from_above[:, 1])
        valid = jnp.logical_and(level >= 0, level < ITERS)
        kept_lower = jnp.where(valid, new_lower, kept_lower)
        kept_upper = jnp.where(valid, new_upper, kept_upper)
        result = jnp.where(level == ITERS - 1, final_state, result)
        incoming = from_behind(final_state, "ta", 1)
        return (incoming, kept_lower, kept_upper, result)

    start_carry = (
        jnp.zeros_like(initial_state),
        zero_series,
        zero_series,
        jnp.zeros_like(initial_state),
    )
    carry = lax.fori_loop(0, intervals + ITERS - 1, slot, start_carry)
    return carry[3][None]


def solution(mesh):
    return jax.shard_map(
        local,
        mesh=mesh,
        in_specs=(P("gx", None, None), P("gx", None, None), P("gx", None, None)),
        out_specs=P("ta", "gx", None, None),
        check_vma=False,
    )
```

profile of v0, /device:TPU:32, one launch (start us, length us, event | category | flops | bytes accessed | tf_op | source)
XLA Modules:
  0.0 682.3 jit_solution(3930378736437492307)
XLA Ops:
  1.1 681.2 %while.23 = (s32[]{:T(128)}, f32[8,256,128]{2,1,0:T(8,128)}, f32[8,256,128]{2,1,0:T(8,128)S(1)}, f32[8,256,128]{2,1,0:T(8,128)S(1)}, f32[8,256,128]{2,1,0:T(8,12...) while((s32[]{:T(128)}, f32[8,256,128]{2,1,0:T(8,128)}, ...), condition=%wide.region_1.2_spmd.clone, body=%wide.region_0.1_spmd.clone.sunk | while | flops 96084672 | bytes 184797040 | solution.py:102
  1.1 2.1 broadcast_select_fusion.2
  31.8 4.3 collective-permute-start.1
  37.3 2.3 select_select_fusion.6
  40.6 3.5 collective-permute-start
  44.2 2.7 bitcast_select_fusion.5
  46.9 2.1 bitcast_select_fusion.4
  49.0 39.0 %collective-permute-done = f32[8,256,128]{2,1,0:T(8,128)S(1)} collective-permute-done((f32[8,256,128]{2,1,0:T(8,128)}, f32[8,256,128]{2,1,0:T(8,128)S(1)}, u32[]{:S(2)}, u32[]{:S(2)}) %collective-permute-start) | collective-permute-done | bytes 1048608 | tf_op jit(solution)/shard_map/while/body/eval_jaxpr/ppermute | solution.py:20
  89.1 2.1 broadcast_select_fusion.2
  119.7 4.3 collective-permute-start.1
  125.3 2.3 select_select_fusion.6
  128.6 2.0 collective-permute-start
  130.6 3.1 bitcast_select_fusion.5
  133.7 2.1 bitcast_select_fusion.4
  135.8 35.9 %collective-permute-done = f32[8,256,128]{2,1,0:T(8,128)S(1)} collective-permute-done((f32[8,256,128]{2,1,0:T(8,128)}, f32[8,256,128]{2,1,0:T(8,128)S(1)}, u32[]{:S(2)}, u32[]{:S(2)}) %collective-permute-start) | collective-permute-done | bytes 1048608 | tf_op jit(solution)/shard_map/while/body/eval_jaxpr/ppermute | solution.py:20
  172.8 2.1 broadcast_select_fusion.2
  203.4 4.3 collective-permute-start.1
  209.0 2.3 select_select_fusion.6
  212.3 2.0 collective-permute-start
  214.3 3.1 bitcast_select_fusion.5
  217.4 2.1 bitcast_select_fusion.4
  219.5 32.7 %collective-permute-done = f32[8,256,128]{2,1,0:T(8,128)S(1)} collective-permute-done((f32[8,256,128]{2,1,0:T(8,128)}, f32[8,256,128]{2,1,0:T(8,128)S(1)}, u32[]{:S(2)}, u32[]{:S(2)}) %collective-permute-start) | collective-permute-done | bytes 1048608 | tf_op jit(solution)/shard_map/while/body/eval_jaxpr/ppermute | solution.py:20
  253.2 2.1 broadcast_select_fusion.2
  283.9 4.3 collective-permute-start.1
  289.4 2.3 select_select_fusion.6
  292.7 2.0 collective-permute-start
  294.8 3.1 bitcast_select_fusion.5
  297.8 2.1 bitcast_select_fusion.4
  300.0 29.6 %collective-permute-done = f32[8,256,128]{2,1,0:T(8,128)S(1)} collective-permute-done((f32[8,256,128]{2,1,0:T(8,128)}, f32[8,256,128]{2,1,0:T(8,128)S(1)}, u32[]{:S(2)}, u32[]{:S(2)}) %collective-permute-start) | collective-permute-done | bytes 1048608 | tf_op jit(solution)/shard_map/while/body/eval_jaxpr/ppermute | solution.py:20
  330.7 2.1 broadcast_select_fusion.2
  361.3 4.3 collective-permute-start.1
  366.8 2.3 select_select_fusion.6
  370.1 2.0 collective-permute-start
  372.2 3.1 bitcast_select_fusion.5
  375.3 2.1 bitcast_select_fusion.4
  377.4 26.6 %collective-permute-done = f32[8,256,128]{2,1,0:T(8,128)S(1)} collective-permute-done((f32[8,256,128]{2,1,0:T(8,128)}, f32[8,256,128]{2,1,0:T(8,128)S(1)}, u32[]{:S(2)}, u32[]{:S(2)}) %collective-permute-start) | collective-permute-done | bytes 1048608 | tf_op jit(solution)/shard_map/while/body/eval_jaxpr/ppermute | solution.py:20
  405.0 2.1 broadcast_select_fusion.2
  435.6 4.3 collective-permute-start.1
  441.2 2.3 select_select_fusion.6
  444.5 2.0 collective-permute-start
  446.6 3.1 bitcast_select_fusion.5
  449.6 2.1 bitcast_select_fusion.4
  451.7 23.5 %collective-permute-done = f32[8,256,128]{2,1,0:T(8,128)S(1)} collective-permute-done((f32[8,256,128]{2,1,0:T(8,128)}, f32[8,256,128]{2,1,0:T(8,128)S(1)}, u32[]{:S(2)}, u32[]{:S(2)}) %collective-permute-start) | collective-permute-done | bytes 1048608 | tf_op jit(solution)/shard_map/while/body/eval_jaxpr/ppermute | solution.py:20
  476.3 2.1 broadcast_select_fusion.2
  507.0 4.3 collective-permute-start.1
  512.5 2.3 select_select_fusion.6
  515.8 2.0 collective-permute-start
  517.9 3.1 bitcast_select_fusion.5
  520.9 2.1 bitcast_select_fusion.4
  523.1 20.9 %collective-permute-done = f32[8,256,128]{2,1,0:T(8,128)S(1)} collective-permute-done((f32[8,256,128]{2,1,0:T(8,128)}, f32[8,256,128]{2,1,0:T(8,128)S(1)}, u32[]{:S(2)}, u32[]{:S(2)}) %collective-permute-start) | collective-permute-done | bytes 1048608 | tf_op jit(solution)/shard_map/while/body/eval_jaxpr/ppermute | solution.py:20
  545.0 2.1 broadcast_select_fusion.2
  575.6 4.3 collective-permute-start.1
  581.2 2.3 select_select_fusion.6
  584.5 2.0 collective-permute-start
  586.5 3.1 bitcast_select_fusion.5
  589.6 2.1 bitcast_select_fusion.4
  591.7 20.9 %collective-permute-done = f32[8,256,128]{2,1,0:T(8,128)S(1)} collective-permute-done((f32[8,256,128]{2,1,0:T(8,128)}, f32[8,256,128]{2,1,0:T(8,128)S(1)}, u32[]{:S(2)}, u32[]{:S(2)}) %collective-permute-start) | collective-permute-done | bytes 1048608 | tf_op jit(solution)/shard_map/while/body/eval_jaxpr/ppermute | solution.py:20
  613.7 2.1 broadcast_select_fusion.2
  644.3 4.3 collective-permute-start.1
  649.8 2.3 select_select_fusion.6
  653.1 2.0 collective-permute-start
  655.2 3.1 bitcast_select_fusion.5
  658.3 2.1 bitcast_select_fusion.4
  660.4 20.9 %collective-permute-done = f32[8,256,128]{2,1,0:T(8,128)S(1)} collective-permute-done((f32[8,256,128]{2,1,0:T(8,128)}, f32[8,256,128]{2,1,0:T(8,128)S(1)}, u32[]{:S(2)}, u32[]{:S(2)}) %collective-permute-start) | collective-permute-done | bytes 1048608 | tf_op jit(solution)/shard_map/while/body/eval_jaxpr/ppermute | solution.py:20
  (553 shorter events, 285.7 us)
Async XLA Ops:
  1.1 2.8 copy-start.2
  1.1 2.8 copy-start.4
  4.2 1.5 copy-start.1
  24.6 19.5 %collective-permute-start.2 = (f32[8,2,256,128]{3,2,1,0:T(8,128)}, f32[8,2,256,128]{3,2,1,0:T(8,128)}, u32[]{:S(2)}, u32[]{:S(2)}) collective-permute-start(f32[8,2,256,128]{3,2,1,0:T(8,128)} %fusion.233), channel_id=1, source_target_pairs={{8,0},{16,8},{24,16},{32,24},{40,32},{48,40},{56,48},{64,56},{72,6... | collective-permute-start | bytes 6291464 | tf_op jit(solution)/shard_map/while/body/eval_jaxpr/ppermute | solution.py:20
  31.8 15.1 %collective-permute-start.1 = (f32[8,2,256,128]{3,2,1,0:T(8,128)}, f32[8,2,256,128]{3,2,1,0:T(8,128)}, u32[]{:S(2)}, u32[]{:S(2)}) collective-permute-start(f32[8,2,256,128]{3,2,1,0:T(8,128)} %fusion.225), channel_id=1, source_target_pairs={{0,8},{8,16},{16,24},{24,32},{32,40},{40,48},{48,56},{56,64},{64,7... | collective-permute-start | bytes 6291464 | tf_op jit(solution)/shard_map/while/body/eval_jaxpr/ppermute | solution.py:20
  40.6 6.3 copy-start.3
  40.6 47.4 %collective-permute-start = (f32[8,256,128]{2,1,0:T(8,128)}, f32[8,256,128]{2,1,0:T(8,128)S(1)}, u32[]{:S(2)}, u32[]{:S(2)}) collective-permute-start(f32[8,256,128]{2,1,0:T(8,128)} %get-tuple-element.535), channel_id=1, source_target_pairs={{0,1},{1,2},{2,3},{3,4},{4,5},{5,6},{6,7},{8,9},{9,10},{10,11},{11... | collective-permute-start | bytes 3145736 | tf_op jit(solution)/shard_map/while/body/eval_jaxpr/ppermute | solution.py:20
  46.9 42.2 %copy-start.5 = (f32[8,256,128]{2,1,0:T(8,128)S(1)}, f32[8,256,128]{2,1,0:T(8,128)}, u32[]{:S(2)}) copy-start(f32[8,256,128]{2,1,0:T(8,128)} %bitcast_select_fusion.5) | copy-start | bytes 3145732 | tf_op jit(solution)/shard_map/while
  89.1 2.9 copy-start.2
  89.1 2.9 copy-start.4
  112.5 18.1 %collective-permute-start.2 = (f32[8,2,256,128]{3,2,1,0:T(8,128)}, f32[8,2,256,128]{3,2,1,0:T(8,128)}, u32[]{:S(2)}, u32[]{:S(2)}) collective-permute-start(f32[8,2,256,128]{3,2,1,0:T(8,128)} %fusion.233), channel_id=1, source_target_pairs={{8,0},{16,8},{24,16},{32,24},{40,32},{48,40},{56,48},{64,56},{72,6... | collective-permute-start | bytes 6291464 | tf_op jit(solution)/shard_map/while/body/eval_jaxpr/ppermute | solution.py:20
  119.7 14.0 %collective-permute-start.1 = (f32[8,2,256,128]{3,2,1,0:T(8,128)}, f32[8,2,256,128]{3,2,1,0:T(8,128)}, u32[]{:S(2)}, u32[]{:S(2)}) collective-permute-start(f32[8,2,256,128]{3,2,1,0:T(8,128)} %fusion.225), channel_id=1, source_target_pairs={{0,8},{8,16},{16,24},{24,32},{32,40},{40,48},{48,56},{56,64},{64,7... | collective-permute-start | bytes 6291464 | tf_op jit(solution)/shard_map/while/body/eval_jaxpr/ppermute | solution.py:20
  128.5 5.1 copy-start.3
  128.6 43.2 %collective-permute-start = (f32[8,256,128]{2,1,0:T(8,128)}, f32[8,256,128]{2,1,0:T(8,128)S(1)}, u32[]{:S(2)}, u32[]{:S(2)}) collective-permute-start(f32[8,256,128]{2,1,0:T(8,128)} %get-tuple-element.535), channel_id=1, source_target_pairs={{0,1},{1,2},{2,3},{3,4},{4,5},{5,6},{6,7},{8,9},{9,10},{10,11},{11... | collective-permute-start | bytes 3145736 | tf_op jit(solution)/shard_map/while/body/eval_jaxpr/ppermute | solution.py:20
  133.7 39.1 %copy-start.5 = (f32[8,256,128]{2,1,0:T(8,128)S(1)}, f32[8,256,128]{2,1,0:T(8,128)}, u32[]{:S(2)}) copy-start(f32[8,256,128]{2,1,0:T(8,128)} %bitcast_select_fusion.5) | copy-start | bytes 3145732 | tf_op jit(solution)/shard_map/while
  172.8 2.9 copy-start.2
  172.8 2.9 copy-start.4
  196.2 18.1 %collective-permute-start.2 = (f32[8,2,256,128]{3,2,1,0:T(8,128)}, f32[8,2,256,128]{3,2,1,0:T(8,128)}, u32[]{:S(2)}, u32[]{:S(2)}) collective-permute-start(f32[8,2,256,128]{3,2,1,0:T(8,128)} %fusion.233), channel_id=1, source_target_pairs={{8,0},{16,8},{24,16},{32,24},{40,32},{48,40},{56,48},{64,56},{72,6... | collective-permute-start | bytes 6291464 | tf_op jit(solution)/shard_map/while/body/eval_jaxpr/ppermute | solution.py:20
  203.4 14.0 %collective-permute-start.1 = (f32[8,2,256,128]{3,2,1,0:T(8,128)}, f32[8,2,256,128]{3,2,1,0:T(8,128)}, u32[]{:S(2)}, u32[]{:S(2)}) collective-permute-start(f32[8,2,256,128]{3,2,1,0:T(8,128)} %fusion.225), channel_id=1, source_target_pairs={{0,8},{8,16},{16,24},{24,32},{32,40},{40,48},{48,56},{56,64},{64,7... | collective-permute-start | bytes 6291464 | tf_op jit(solution)/shard_map/while/body/eval_jaxpr/ppermute | solution.py:20
  212.3 5.1 copy-start.3
  212.3 39.9 %collective-permute-start = (f32[8,256,128]{2,1,0:T(8,128)}, f32[8,256,128]{2,1,0:T(8,128)S(1)}, u32[]{:S(2)}, u32[]{:S(2)}) collective-permute-start(f32[8,256,128]{2,1,0:T(8,128)} %get-tuple-element.535), channel_id=1, source_target_pairs={{0,1},{1,2},{2,3},{3,4},{4,5},{5,6},{6,7},{8,9},{9,10},{10,11},{11... | collective-permute-start | bytes 3145736 | tf_op jit(solution)/shard_map/while/body/eval_jaxpr/ppermute | solution.py:20
  217.4 35.9 %copy-start.5 = (f32[8,256,128]{2,1,0:T(8,128)S(1)}, f32[8,256,128]{2,1,0:T(8,128)}, u32[]{:S(2)}) copy-start(f32[8,256,128]{2,1,0:T(8,128)} %bitcast_select_fusion.5) | copy-start | bytes 3145732 | tf_op jit(solution)/shard_map/while
  253.2 2.9 copy-start.2
  253.2 2.9 copy-start.4
  276.7 18.1 %collective-permute-start.2 = (f32[8,2,256,128]{3,2,1,0:T(8,128)}, f32[8,2,256,128]{3,2,1,0:T(8,128)}, u32[]{:S(2)}, u32[]{:S(2)}) collective-permute-start(f32[8,2,256,128]{3,2,1,0:T(8,128)} %fusion.233), channel_id=1, source_target_pairs={{8,0},{16,8},{24,16},{32,24},{40,32},{48,40},{56,48},{64,56},{72,6... | collective-permute-start | bytes 6291464 | tf_op jit(solution)/shard_map/while/body/eval_jaxpr/ppermute | solution.py:20
  283.9 14.0 %collective-permute-start.1 = (f32[8,2,256,128]{3,2,1,0:T(8,128)}, f32[8,2,256,128]{3,2,1,0:T(8,128)}, u32[]{:S(2)}, u32[]{:S(2)}) collective-permute-start(f32[8,2,256,128]{3,2,1,0:T(8,128)} %fusion.225), channel_id=1, source_target_pairs={{0,8},{8,16},{16,24},{24,32},{32,40},{40,48},{48,56},{56,64},{64,7... | collective-permute-start | bytes 6291464 | tf_op jit(solution)/shard_map/while/body/eval_jaxpr/ppermute | solution.py:20
  292.7 5.1 copy-start.3
  292.7 36.9 %collective-permute-start = (f32[8,256,128]{2,1,0:T(8,128)}, f32[8,256,128]{2,1,0:T(8,128)S(1)}, u32[]{:S(2)}, u32[]{:S(2)}) collective-permute-start(f32[8,256,128]{2,1,0:T(8,128)} %get-tuple-element.535), channel_id=1, source_target_pairs={{0,1},{1,2},{2,3},{3,4},{4,5},{5,6},{6,7},{8,9},{9,10},{10,11},{11... | collective-permute-start | bytes 3145736 | tf_op jit(solution)/shard_map/while/body/eval_jaxpr/ppermute | solution.py:20
  297.8 32.8 %copy-start.5 = (f32[8,256,128]{2,1,0:T(8,128)S(1)}, f32[8,256,128]{2,1,0:T(8,128)}, u32[]{:S(2)}) copy-start(f32[8,256,128]{2,1,0:T(8,128)} %bitcast_select_fusion.5) | copy-start | bytes 3145732 | tf_op jit(solution)/shard_map/while
  330.7 2.9 copy-start.2
  330.7 2.9 copy-start.4
  354.1 18.1 %collective-permute-start.2 = (f32[8,2,256,128]{3,2,1,0:T(8,128)}, f32[8,2,256,128]{3,2,1,0:T(8,128)}, u32[]{:S(2)}, u32[]{:S(2)}) collective-permute-start(f32[8,2,256,128]{3,2,1,0:T(8,128)} %fusion.233), channel_id=1, source_target_pairs={{8,0},{16,8},{24,16},{32,24},{40,32},{48,40},{56,48},{64,56},{72,6... | collective-permute-start | bytes 6291464 | tf_op jit(solution)/shard_map/while/body/eval_jaxpr/ppermute | solution.py:20
  361.3 14.0 %collective-permute-start.1 = (f32[8,2,256,128]{3,2,1,0:T(8,128)}, f32[8,2,256,128]{3,2,1,0:T(8,128)}, u32[]{:S(2)}, u32[]{:S(2)}) collective-permute-start(f32[8,2,256,128]{3,2,1,0:T(8,128)} %fusion.225), channel_id=1, source_target_pairs={{0,8},{8,16},{16,24},{24,32},{32,40},{40,48},{48,56},{56,64},{64,7... | collective-permute-start | bytes 6291464 | tf_op jit(solution)/shard_map/while/body/eval_jaxpr/ppermute | solution.py:20
  370.1 5.1 copy-start.3
  370.1 33.8 %collective-permute-start = (f32[8,256,128]{2,1,0:T(8,128)}, f32[8,256,128]{2,1,0:T(8,128)S(1)}, u32[]{:S(2)}, u32[]{:S(2)}) collective-permute-start(f32[8,256,128]{2,1,0:T(8,128)} %get-tuple-element.535), channel_id=1, source_target_pairs={{0,1},{1,2},{2,3},{3,4},{4,5},{5,6},{6,7},{8,9},{9,10},{10,11},{11... | collective-permute-start | bytes 3145736 | tf_op jit(solution)/shard_map/while/body/eval_jaxpr/ppermute | solution.py:20
  375.2 29.8 %copy-start.5 = (f32[8,256,128]{2,1,0:T(8,128)S(1)}, f32[8,256,128]{2,1,0:T(8,128)}, u32[]{:S(2)}) copy-start(f32[8,256,128]{2,1,0:T(8,128)} %bitcast_select_fusion.5) | copy-start | bytes 3145732 | tf_op jit(solution)/shard_map/while
  405.0 2.9 copy-start.2
  405.0 2.9 copy-start.4
  428.5 18.1 %collective-permute-start.2 = (f32[8,2,256,128]{3,2,1,0:T(8,128)}, f32[8,2,256,128]{3,2,1,0:T(8,128)}, u32[]{:S(2)}, u32[]{:S(2)}) collective-permute-start(f32[8,2,256,128]{3,2,1,0:T(8,128)} %fusion.233), channel_id=1, source_target_pairs={{8,0},{16,8},{24,16},{32,24},{40,32},{48,40},{56,48},{64,56},{72,6... | collective-permute-start | bytes 6291464 | tf_op jit(solution)/shard_map/while/body/eval_jaxpr/ppermute | solution.py:20
  435.6 14.0 %collective-permute-start.1 = (f32[8,2,256,128]{3,2,1,0:T(8,128)}, f32[8,2,256,128]{3,2,1,0:T(8,128)}, u32[]{:S(2)}, u32[]{:S(2)}) collective-permute-start(f32[8,2,256,128]{3,2,1,0:T(8,128)} %fusion.225), channel_id=1, source_target_pairs={{0,8},{8,16},{16,24},{24,32},{32,40},{40,48},{48,56},{56,64},{64,7... | collective-permute-start | bytes 6291464 | tf_op jit(solution)/shard_map/while/body/eval_jaxpr/ppermute | solution.py:20
  444.5 5.1 copy-start.3
  444.5 30.8 %collective-permute-start = (f32[8,256,128]{2,1,0:T(8,128)}, f32[8,256,128]{2,1,0:T(8,128)S(1)}, u32[]{:S(2)}, u32[]{:S(2)}) collective-permute-start(f32[8,256,128]{2,1,0:T(8,128)} %get-tuple-element.535), channel_id=1, source_target_pairs={{0,1},{1,2},{2,3},{3,4},{4,5},{5,6},{6,7},{8,9},{9,10},{10,11},{11... | collective-permute-start | bytes 3145736 | tf_op jit(solution)/shard_map/while/body/eval_jaxpr/ppermute | solution.py:20
  449.6 26.7 %copy-start.5 = (f32[8,256,128]{2,1,0:T(8,128)S(1)}, f32[8,256,128]{2,1,0:T(8,128)}, u32[]{:S(2)}) copy-start(f32[8,256,128]{2,1,0:T(8,128)} %bitcast_select_fusion.5) | copy-start | bytes 3145732 | tf_op jit(solution)/shard_map/while
  476.3 2.9 copy-start.2
  476.3 2.9 copy-start.4
  499.8 18.1 %collective-permute-start.2 = (f32[8,2,256,128]{3,2,1,0:T(8,128)}, f32[8,2,256,128]{3,2,1,0:T(8,128)}, u32[]{:S(2)}, u32[]{:S(2)}) collective-permute-start(f32[8,2,256,128]{3,2,1,0:T(8,128)} %fusion.233), channel_id=1, source_target_pairs={{8,0},{16,8},{24,16},{32,24},{40,32},{48,40},{56,48},{64,56},{72,6... | collective-permute-start | bytes 6291464 | tf_op jit(solution)/shard_map/while/body/eval_jaxpr/ppermute | solution.py:20
  507.0 14.0 %collective-permute-start.1 = (f32[8,2,256,128]{3,2,1,0:T(8,128)}, f32[8,2,256,128]{3,2,1,0:T(8,128)}, u32[]{:S(2)}, u32[]{:S(2)}) collective-permute-start(f32[8,2,256,128]{3,2,1,0:T(8,128)} %fusion.225), channel_id=1, source_target_pairs={{0,8},{8,16},{16,24},{24,32},{32,40},{40,48},{48,56},{56,64},{64,7... | collective-permute-start | bytes 6291464 | tf_op jit(solution)/shard_map/while/body/eval_jaxpr/ppermute | solution.py:20
  515.8 5.1 copy-start.3
  515.8 28.1 %collective-permute-start = (f32[8,256,128]{2,1,0:T(8,128)}, f32[8,256,128]{2,1,0:T(8,128)S(1)}, u32[]{:S(2)}, u32[]{:S(2)}) collective-permute-start(f32[8,256,128]{2,1,0:T(8,128)} %get-tuple-element.535), channel_id=1, source_target_pairs={{0,1},{1,2},{2,3},{3,4},{4,5},{5,6},{6,7},{8,9},{9,10},{10,11},{11... | collective-permute-start | bytes 3145736 | tf_op jit(solution)/shard_map/while/body/eval_jaxpr/ppermute | solution.py:20
  520.9 24.1 %copy-start.5 = (f32[8,256,128]{2,1,0:T(8,128)S(1)}, f32[8,256,128]{2,1,0:T(8,128)}, u32[]{:S(2)}) copy-start(f32[8,256,128]{2,1,0:T(8,128)} %bitcast_select_fusion.5) | copy-start | bytes 3145732 | tf_op jit(solution)/shard_map/while
  545.0 2.9 copy-start.2
  545.0 2.9 copy-start.4
  568.5 18.1 %collective-permute-start.2 = (f32[8,2,256,128]{3,2,1,0:T(8,128)}, f32[8,2,256,128]{3,2,1,0:T(8,128)}, u32[]{:S(2)}, u32[]{:S(2)}) collective-permute-start(f32[8,2,256,128]{3,2,1,0:T(8,128)} %fusion.233), channel_id=1, source_target_pairs={{8,0},{16,8},{24,16},{32,24},{40,32},{48,40},{56,48},{64,56},{72,6... | collective-permute-start | bytes 6291464 | tf_op jit(solution)/shard_map/while/body/eval_jaxpr/ppermute | solution.py:20
  575.6 14.0 %collective-permute-start.1 = (f32[8,2,256,128]{3,2,1,0:T(8,128)}, f32[8,2,256,128]{3,2,1,0:T(8,128)}, u32[]{:S(2)}, u32[]{:S(2)}) collective-permute-start(f32[8,2,256,128]{3,2,1,0:T(8,128)} %fusion.225), channel_id=1, source_target_pairs={{0,8},{8,16},{16,24},{24,32},{32,40},{40,48},{48,56},{56,64},{64,7... | collective-permute-start | bytes 6291464 | tf_op jit(solution)/shard_map/while/body/eval_jaxpr/ppermute | solution.py:20
  584.5 5.1 copy-start.3
  584.5 28.1 %collective-permute-start = (f32[8,256,128]{2,1,0:T(8,128)}, f32[8,256,128]{2,1,0:T(8,128)S(1)}, u32[]{:S(2)}, u32[]{:S(2)}) collective-permute-start(f32[8,256,128]{2,1,0:T(8,128)} %get-tuple-element.535), channel_id=1, source_target_pairs={{0,1},{1,2},{2,3},{3,4},{4,5},{5,6},{6,7},{8,9},{9,10},{10,11},{11... | collective-permute-start | bytes 3145736 | tf_op jit(solution)/shard_map/while/body/eval_jaxpr/ppermute | solution.py:20
  589.6 24.1 %copy-start.5 = (f32[8,256,128]{2,1,0:T(8,128)S(1)}, f32[8,256,128]{2,1,0:T(8,128)}, u32[]{:S(2)}) copy-start(f32[8,256,128]{2,1,0:T(8,128)} %bitcast_select_fusion.5) | copy-start | bytes 3145732 | tf_op jit(solution)/shard_map/while
  613.7 2.9 copy-start.2
  613.7 2.9 copy-start.4
  637.1 18.1 %collective-permute-start.2 = (f32[8,2,256,128]{3,2,1,0:T(8,128)}, f32[8,2,256,128]{3,2,1,0:T(8,128)}, u32[]{:S(2)}, u32[]{:S(2)}) collective-permute-start(f32[8,2,256,128]{3,2,1,0:T(8,128)} %fusion.233), channel_id=1, source_target_pairs={{8,0},{16,8},{24,16},{32,24},{40,32},{48,40},{56,48},{64,56},{72,6... | collective-permute-start | bytes 6291464 | tf_op jit(solution)/shard_map/while/body/eval_jaxpr/ppermute | solution.py:20
  644.3 14.0 %collective-permute-start.1 = (f32[8,2,256,128]{3,2,1,0:T(8,128)}, f32[8,2,256,128]{3,2,1,0:T(8,128)}, u32[]{:S(2)}, u32[]{:S(2)}) collective-permute-start(f32[8,2,256,128]{3,2,1,0:T(8,128)} %fusion.225), channel_id=1, source_target_pairs={{0,8},{8,16},{16,24},{24,32},{32,40},{40,48},{48,56},{56,64},{64,7... | collective-permute-start | bytes 6291464 | tf_op jit(solution)/shard_map/while/body/eval_jaxpr/ppermute | solution.py:20
  653.1 5.1 copy-start.3
  653.1 28.1 %collective-permute-start = (f32[8,256,128]{2,1,0:T(8,128)}, f32[8,256,128]{2,1,0:T(8,128)S(1)}, u32[]{:S(2)}, u32[]{:S(2)}) collective-permute-start(f32[8,256,128]{2,1,0:T(8,128)} %get-tuple-element.535), channel_id=1, source_target_pairs={{0,1},{1,2},{2,3},{3,4},{4,5},{5,6},{6,7},{8,9},{9,10},{10,11},{11... | collective-permute-start | bytes 3145736 | tf_op jit(solution)/shard_map/while/body/eval_jaxpr/ppermute | solution.py:20
  658.2 24.1 %copy-start.5 = (f32[8,256,128]{2,1,0:T(8,128)S(1)}, f32[8,256,128]{2,1,0:T(8,128)}, u32[]{:S(2)}) copy-start(f32[8,256,128]{2,1,0:T(8,128)} %bitcast_select_fusion.5) | copy-start | bytes 3145732 | tf_op jit(solution)/shard_map/while
  (44 other events, 52.5 us)
where the time goes:
time: 685 us; the launch traced here: 682 us
  other arithmetic  278 us (41%)
  waiting for transfers between devices  250 us (36%)
  local copies, waits for them, and re-layouts  82.5 us (12%)
  starting transfers between devices  70.3 us (10%)
    ppermute x27, waiting for transfers between devices, from_behind(): return lax.ppermute(block, axis, route)  250 us
    div x63, other arithmetic, advance_field(): return (field + diffusion * laplace - advect + source) / (1.0 + reaction)  78.4 us
    while x225, local copies, waits for them, and re-layouts  74.6 us
    ppermute x27, starting transfers between devices, from_behind(): return lax.ppermute(block, axis, route)  70.3 us
    concatenate x72, other arithmetic, advance_field(): jnp.concatenate([lower_ghost[None], field, upper_ghost[None]], axis=0)  54.9 us
    while x63, other arithmetic  45.9 us
    select_n x9, other arithmetic, slot(): kept_upper = jnp.where(valid, new_upper, kept_upper)  27.1 us
    select_n x9, other arithmetic, slot(): result = jnp.where(level == ITERS - 1, final_state, result)  20.9 us
  transfers between devices with their start and end apart: 27, of which 9 were waited for; matrix products, arithmetic and copies ran while one was open for 19% of the time, Pallas kernels for 0%

commit v1 on v0

v1 whole, which is shorter than its diff:
```python
import functools

import jax
import jax.numpy as jnp
from jax import lax
from jax.experimental import pallas as pl
from jax.experimental.pallas import tpu as pltpu
from jax.sharding import PartitionSpec as P

CX = 8
NZ = 128
STRIP = 32
HALO = 32
WINDOW = STRIP + 2 * HALO
WIDE = STRIP + 4 * HALO
PHASE = 32
STEPS = 8
PAD = 8
GROUP = 4
BY_MATRIX = 4

VMEM = pl.BlockSpec(memory_space=pltpu.VMEM)
SMEM = pl.BlockSpec(memory_space=pltpu.SMEM)
HBM = pl.BlockSpec(memory_space=pl.ANY)
PARAMS = pltpu.CompilerParams(vmem_limit_bytes=48 << 20)


def z_matrix():
    row = lax.broadcasted_iota(jnp.int32, (2 * NZ, NZ), 0) % NZ
    col = lax.broadcasted_iota(jnp.int32, (2 * NZ, NZ), 1)
    taps = jnp.where(row == col - 1, 2.0, 0.0) + jnp.where(row == col + 1, 1.0, 0.0)
    return taps.astype(jnp.bfloat16)


def z_sum(planes, taps):
    high = planes.astype(jnp.bfloat16)
    low = (planes - high.astype(jnp.float32)).astype(jnp.bfloat16)
    return jnp.dot(jnp.concatenate([high, low], 1), taps, preferred_element_type=jnp.float32)


def advance(src, dst, m, q, ghosts, edge, tiles, taps):
    lane = lax.broadcasted_iota(jnp.int32, (8, NZ), 1)
    not_first, not_last = lane != 0, lane != NZ - 1
    tiles = list(tiles)
    for begin in range(0, len(tiles), GROUP):
        group = tiles[begin : begin + GROUP]
        cells = [[src[x, PAD + 8 * t : PAD + 8 * t + 8, :] for x in range(CX)] for t in group]
        z_all = z_sum(jnp.concatenate([c[x] for c in cells for x in range(BY_MATRIX)], 0), taps)
        for at, t in enumerate(group):
            c = cells[at]
            low, high = ghosts(t)
            low = edge[0] * c[0] if low is None else edge[0] * c[0] + low
            high = edge[1] * c[-1] if high is None else edge[1] * c[-1] + high
            below = [low] + c[:-1]
            above = c[1:] + [high]
            for x in range(CX):
                y_below = src[x, PAD + 8 * t - 1 : PAD + 8 * t + 7, :]
                y_above = src[x, PAD + 8 * t + 1 : PAD + 8 * t + 9, :]
                if x < BY_MATRIX:
                    row = (at * BY_MATRIX + x) * 8
                    twice = below[x] + y_below
                    total = (twice + twice) + ((below[x] + above[x]) + y_above) + z_all[row : row + 8]
                else:
                    z_below = jnp.where(not_first, pltpu.roll(c[x], 1, 1), 0.0)
                    z_above = jnp.where(not_last, pltpu.roll(c[x], NZ - 1, 1), 0.0)
                    twice = below[x] + y_below + z_below
                    total = (twice + twice) + ((below[x] + above[x]) + (y_above + z_above))
                rows = slice(8 * t, 8 * t + 8)
                dst[x, PAD + 8 * t : PAD + 8 * t + 8, :] = total * m[x, rows, :] + q[x, rows, :]


def clear_pads(buffers, rows):
    for b in buffers:
        b[:, :PAD, :] = jnp.zeros((CX, PAD, NZ), jnp.float32)
        b[:, PAD + rows :, :] = jnp.zeros((CX, PAD, NZ), jnp.float32)


def no_ghosts(t):
    return None, None


def trace(src, place, t):
    rows = slice(PAD + 8 * t, PAD + 8 * t + 8)
    return src[place[2], rows, :] - 0.6 * src[place[1], rows, :]


def window_copies(arrays, bufs, sems, strip, blocks, start):
    for b in range(blocks):
        at = strip + start + b
        inside = jnp.logical_and(at >= 0, at < 8)
        row = pl.multiple_of(jnp.clip(at, 0, 7) * STRIP, STRIP)
        copies = [
            pltpu.make_async_copy(a.at[:, pl.ds(row, STRIP), :], v.at[:, pl.ds(b * STRIP, STRIP), :], sems.at[n, b])
            for n, (a, v) in enumerate(zip(arrays, bufs))
        ]
        yield b, inside, copies


def load_window(arrays, bufs, sems, strip, blocks, start, u_out, m_out, q_out, u_pad):
    for b, inside, copies in window_copies(arrays, bufs, sems, strip, blocks, start):
        for copy in copies:
            copy.start()
    for b, inside, copies in window_copies(arrays, bufs, sems, strip, blocks, start):
        for copy in copies:
            copy.wait()
        keep = jnp.where(inside, 1.0, 0.0)
        rows = slice(b * STRIP, (b + 1) * STRIP)
        scale = keep / (1.0 + bufs[1][:, rows, :])
        m_out[:, rows, :] = 0.1 * scale
        q_out[:, rows, :] = bufs[2][:, rows, :] * scale
        u_out[:, u_pad + b * STRIP : u_pad + (b + 1) * STRIP, :] = bufs[0][:, rows, :] * keep


def pack_kernel(place, u, r, s, out, ubuf, rbuf, sbuf, sems):
    load_window((u, r, s), (ubuf, rbuf, sbuf), sems, place[0], 3, -1, out.at[0], out.at[1], out.at[2], 0)


def first_a_kernel(place, edge, taps, u, r, s, trace_out, last, ubuf, rbuf, sbuf, ua, ub, m, q, sems):
    load_window((u, r, s), (ubuf, rbuf, sbuf), sems, place[0], 5, -2, ua, m, q, PAD)
    clear_pads((ua, ub), WIDE)
    edges = (edge[0], edge[1])
    t_matrix = taps[...]
    for k in range(PHASE // STEPS):
        def pair(p, _):
            for n, (src, dst) in enumerate(((ua, ub), (ub, ua))):
                step = k * STEPS + 2 * p + n
                for t in range(4 + k, 16 - k):
                    trace_out[step, 8 * (t - 4) : 8 * (t - 4) + 8, :] = trace(src, place, t)
                advance(src, dst, m, q, no_ghosts, edges, range(k, 20 - k), t_matrix)
            return 0
        lax.fori_loop(0, STEPS // 2, pair, 0)
    last[...] = ua[:, PAD + HALO : PAD + HALO + WINDOW, :]


def first_b_kernel(place, edge, taps, u, mine, trace_out, ua, ub):
    clear_pads((ua, ub), WINDOW)
    ua[:, PAD : PAD + WINDOW, :] = u[...]
    edges = (edge[0], edge[1])
    t_matrix = taps[...]
    for k in range(PHASE // STEPS):
        def pair(p, _):
            for n, (src, dst) in enumerate(((ua, ub), (ub, ua))):
                step = k * STEPS + 2 * p + n
                for t in range(k, 12 - k):
                    trace_out[step, 8 * t : 8 * t + 8, :] = trace(src, place, t)
                advance(src, dst, mine.at[1], mine.at[2], no_ghosts, edges, range(k, 12 - k), t_matrix)
            return 0
        lax.fori_loop(0, STEPS // 2, pair, 0)


def two_slabs(place, edge, taps, mine, other, series, ends, ua, ub, va, vb):
    odd = place[3] == 1
    own_edges = (edge[0], edge[1])
    other_edges = (edge[2], edge[3])
    t_matrix = taps[...]
    for k in range(PHASE // STEPS):
        def pair(p, _):
            for src, dst, osrc, odst, n in ((ua, ub, va, vb, 0), (ub, ua, vb, va, 1)):
                step = k * STEPS + 2 * p + n
                tiles = range(k, 12 - k)

                def ghosts(t):
                    far = trace(osrc, place, t)
                    near = series[step, 8 * t : 8 * t + 8, :]
                    return jnp.where(odd, near, far), jnp.where(odd, far, near)

                advance(src, dst, mine.at[1], mine.at[2], ghosts, own_edges, tiles, t_matrix)
                advance(osrc, odst, other.at[1], other.at[2], no_ghosts, other_edges, tiles, t_matrix)
            return 0
        lax.fori_loop(0, STEPS // 2, pair, 0)
        ends[k] = ua[:, PAD + HALO : PAD + HALO + STRIP, :]


def second_a_kernel(place, edge, taps, mine, other, series, ends, last, ua, ub, va, vb):
    clear_pads((ua, ub, va, vb), WINDOW)
    ua[:, PAD : PAD + WINDOW, :] = mine[0]
    va[:, PAD : PAD + WINDOW, :] = other[0]
    two_slabs(place, edge, taps, mine, other, series, ends, ua, ub, va, vb)
    last[0] = ua[:, PAD + HALO : PAD + HALO + STRIP, :]
    last[1] = va[:, PAD + HALO : PAD + HALO + STRIP, :]


def second_b_kernel(place, edge, taps, mine, other, series, left, mid, right, ends, ua, ub, va, vb):
    clear_pads((ua, ub, va, vb), WINDOW)
    for at, part in enumerate((left, mid, right)):
        rows = slice(PAD + at * STRIP, PAD + (at + 1) * STRIP)
        ua[:, rows, :] = part[0]
        va[:, rows, :] = part[1]
    two_slabs(place, edge, taps, mine, other, series, ends, ua, ub, va, vb)


def f32(*shape):
    return jax.ShapeDtypeStruct(shape, jnp.float32)


def buffer(rows):
    return pltpu.VMEM((CX, rows, NZ), jnp.float32)


def local(u, r, s):
    strip = lax.axis_index("ta")
    slab = lax.axis_index("gx")
    slabs = lax.axis_size("gx")
    strips = lax.axis_size("ta")
    odd = slab % 2
    other = slab - 1 + 2 * odd
    place = jnp.stack([strip, 7 - 7 * odd, 6 - 5 * odd, odd]).astype(jnp.int32)

    def weight(inside):
        return jnp.where(inside, 0.6, 0.0).astype(jnp.float32)

    edge = jnp.stack([weight(slab > 0), weight(slab < slabs - 1), weight(other > 0), weight(other < slabs - 1)])
    taps = z_matrix()

    mine = pl.pallas_call(
        pack_kernel,
        out_shape=f32(3, CX, WINDOW, NZ),
        in_specs=[SMEM, HBM, HBM, HBM],
        out_specs=VMEM,
        scratch_shapes=[buffer(WINDOW)] * 3 + [pltpu.SemaphoreType.DMA((3, 3))],
        compiler_params=PARAMS,
        name="pack_window",
    )(place, u, r, s)
    inter = [(i, i + 1) for i in range(1, slabs - 1, 2)]
    theirs = lax.ppermute(mine, "gx", inter + [(b, a) for a, b in inter])

    series_a, state = pl.pallas_call(
        first_a_kernel,
        out_shape=(f32(PHASE, WINDOW, NZ), f32(CX, WINDOW, NZ)),
        in_specs=[SMEM, SMEM, VMEM, HBM, HBM, HBM],
        out_specs=(VMEM, VMEM),
        scratch_shapes=[buffer(WIDE)] * 3 + [buffer(WIDE + 2 * PAD)] * 2 + [buffer(WIDE)] * 2 + [pltpu.SemaphoreType.DMA((3, 5))],
        compiler_params=PARAMS,
        name="first_iteration_a",
    )(place, edge, taps, u, r, s)
    intra = [(i, i + 1) for i in range(0, slabs, 2)]
    intra = intra + [(b, a) for a, b in intra]
    series_a = lax.ppermute(series_a, "gx", intra)
    series_b = pl.pallas_call(
        first_b_kernel,
        out_shape=f32(PHASE, WINDOW, NZ),
        in_specs=[SMEM, SMEM, VMEM, VMEM, VMEM],
        out_specs=VMEM,
        scratch_shapes=[buffer(WINDOW + 2 * PAD)] * 2,
        compiler_params=PARAMS,
        name="first_iteration_b",
    )(place, edge, taps, state, mine)
    series_b = lax.ppermute(series_b, "gx", intra)

    work = [buffer(WINDOW + 2 * PAD)] * 4
    ends_a, last = pl.pallas_call(
        second_a_kernel,
        out_shape=(f32(4, CX, STRIP, NZ), f32(2, CX, STRIP, NZ)),
        in_specs=[SMEM, SMEM] + [VMEM] * 4,
        out_specs=(VMEM, VMEM),
        scratch_shapes=work,
        compiler_params=PARAMS,
        name="second_iteration_a",
    )(place, edge, taps, mine, theirs, series_a)
    left = lax.ppermute(last, "ta", [(i, i + 1) for i in range(strips - 1)])
    right = lax.ppermute(last, "ta", [(i + 1, i) for i in range(strips - 1)])
    ends_b = pl.pallas_call(
        second_b_kernel,
        out_shape=f32(4, CX, STRIP, NZ),
        in_specs=[SMEM, SMEM] + [VMEM] * 7,
        out_specs=VMEM,
        scratch_shapes=work,
        compiler_params=PARAMS,
        name="second_iteration_b",
    )(place, edge, taps, mine, theirs, series_b, left, last, right)
    ends = jnp.concatenate([ends_a, ends_b], 0)
    return lax.all_to_all(ends, "ta", 0, 2, tiled=True)


def solution(mesh):
    return jax.shard_map(
        local,
        mesh=mesh,
        in_specs=(P("gx", None, None), P("gx", None, None), P("gx", None, None)),
        out_specs=P("ta", "gx", None, None),
        check_vma=False,
    )
```

time: 685 us -> 102 us (0.15)
  the two profiles are of different devices: /device:TPU:32 before, /device:TPU:24 now
where the time goes in v1:
time: 102 us
  Pallas kernels  43.2 us (42%)
  blocking collectives  23 us (23%)
  waiting for transfers between devices  22.6 us (22%)
  starting transfers between devices  7.62 us (7%)
  local copies, waits for them, and re-layouts  4.73 us (5%)
    all_to_all x1, blocking collectives, local(): return lax.all_to_all(ends, 'ta', 0, 2, tiled=True)  23 us
    ppermute x1, waiting for transfers between devices, local(): theirs = lax.ppermute(mine, 'gx', inter + [(b, a) for a, b in inter])  15.2 us
    pallas_call x1, Pallas kernels, local(): pl.pallas_call(second_a_kernel, out_shape=(f32(4, CX, STRIP, NZ), f32(2,...  12.4 us
    pallas_call x1, Pallas kernels, local(): pl.pallas_call(second_b_kernel, out_shape=f32(4, CX, STRIP, NZ), in_specs...  12.4 us
    pallas_call x1, Pallas kernels, local(): pl.pallas_call(first_a_kernel, out_shape=(f32(PHASE, WINDOW, NZ), f32(CX,...  10.2 us
    pallas_call x1, Pallas kernels, local(): pl.pallas_call(first_b_kernel, out_shape=f32(PHASE, WINDOW, NZ), in_specs...  7.28 us
    ppermute x1, waiting for transfers between devices, local(): right = lax.ppermute(last, 'ta', [(i + 1, i) for i in range(strips - 1)])  4.69 us
    unnamed x6, local copies, waits for them, and re-layouts  3.67 us
  transfers between devices with their start and end apart: 5, of which 3 were waited for; matrix products, arithmetic and copies ran while one was open for 0% of the time, Pallas kernels for 20%

profile of v1, /device:TPU:24, one launch (start us, length us, event | category | flops | bytes accessed | tf_op | source)
XLA Modules:
  0.0 101.7 jit_solution(8114923398188804390)
XLA Ops:
  0.0 0.1 pad_maximum_fusion.1.edge
  0.1 0.1 pad_add_fusion.place
  0.2 0.2 add_convert_fusion.taps
  0.4 0.0 copy-start
  0.4 1.2 %copy-done = f32[8,256,128]{2,1,0:T(8,128)S(1)} copy-done((f32[8,256,128]{2,1,0:T(8,128)S(1)}, f32[8,256,128]{2,1,0:T(8,128)}, u32[]{:S(2)}) %copy-start) | copy-done | bytes 1048600
  1.6 0.0 copy-start.1
  1.6 1.2 %copy-done.1 = f32[8,256,128]{2,1,0:T(8,128)S(1)} copy-done((f32[8,256,128]{2,1,0:T(8,128)S(1)}, f32[8,256,128]{2,1,0:T(8,128)}, u32[]{:S(2)}) %copy-start.1) | copy-done | bytes 1048600
  2.8 0.0 copy-start.2
  2.8 1.2 %copy-done.2 = f32[8,256,128]{2,1,0:T(8,128)S(1)} copy-done((f32[8,256,128]{2,1,0:T(8,128)S(1)}, f32[8,256,128]{2,1,0:T(8,128)}, u32[]{:S(2)}) %copy-start.2) | copy-done | bytes 1048600
  4.1 10.2 %first_iteration_a.1 = (f32[32,96,128]{2,1,0:T(8,128)S(1)}, f32[8,96,128]{2,1,0:T(8,128)S(1)}) custom-call(s32[4]{0:T(128)S(1)} %pad_add_fusion.place, f32[4]{0:T(128)S(1)} %pad_maximum_fusion.1.edge, bf16[256,128]{1,0:T(8,128)(2,1)S(1)} %add_convert_fusion.taps, f32[8,256,128]{2,1,0:T(8,128)S(1)} %copy-done, f32[8,256,128]{2,1,0:T(8,128)S(1)} %copy-done.1, ...), custom_call_target="tpu_custom_call" | custom-call | tf_op jit(solution)/shard_map/first_iteration_a/pallas_call | solution.py:227
  14.2 0.1 collective-permute-start.1
  14.3 1.0 pack_window.1.mine
  15.3 7.3 %first_iteration_b.1 = f32[32,96,128]{2,1,0:T(8,128)S(1)} custom-call(s32[4]{0:T(128)S(1)} %pad_add_fusion.place, f32[4]{0:T(128)S(1)} %pad_maximum_fusion.1.edge, bf16[256,128]{1,0:T(8,128)(2,1)S(1)} %add_convert_fusion.taps, f32[8,96,128]{2,1,0:T(8,128)S(1)} %get-tuple-element.11.u, f32[3,8,96,128]{3,2,1,0:T(8,128)S(1)} %pack_window.1.mine), custom_call_target="tpu_custom_call" | custom-call | tf_op jit(solution)/shard_map/first_iteration_b/pallas_call | solution.py:239
  22.6 0.6 collective-permute-start.2
  23.1 2.3 %collective-permute-start = (f32[3,8,96,128]{3,2,1,0:T(8,128)S(1)}, f32[3,8,96,128]{3,2,1,0:T(8,128)S(1)}, u32[]{:S(2)}, u32[]{:S(2)}) collective-permute-start(f32[3,8,96,128]{3,2,1,0:T(8,128)S(1)} %pack_window.1.mine), channel_id=1, source_target_pairs={{8,16},{24,32},{40,48},{56,64},{72,80},{88,96},{104,112},{16,8},{3... | collective-permute-start | bytes 3538952 | tf_op jit(solution)/shard_map/ppermute | solution.py:225
  25.4 15.2 %collective-permute-done.other = f32[3,8,96,128]{3,2,1,0:T(8,128)S(1)} collective-permute-done((f32[3,8,96,128]{3,2,1,0:T(8,128)S(1)}, f32[3,8,96,128]{3,2,1,0:T(8,128)S(1)}, u32[]{:S(2)}, u32[]{:S(2)}) %collective-permute-start) | collective-permute-done | bytes 1179680 | tf_op jit(solution)/shard_map/ppermute | solution.py:225
  40.6 0.0 collective-permute-done.1.series
  40.6 12.4 %second_iteration_a.1 = (f32[4,8,32,128]{3,2,1,0:T(8,128)S(1)}, f32[2,8,32,128]{3,2,1,0:T(8,128)S(1)}) custom-call(s32[4]{0:T(128)S(1)} %pad_add_fusion.place, f32[4]{0:T(128)S(1)} %pad_maximum_fusion.1.edge, bf16[256,128]{1,0:T(8,128)(2,1)S(1)} %add_convert_fusion.taps, f32[3,8,96,128]{3,2,1,0:T(8,128)S(1)} %pack_window.1.mine, ...), custom_call_target="tpu_custom_call" | custom-call | tf_op jit(solution)/shard_map/second_iteration_a/pallas_call | solution.py:251
  53.1 3.4 %collective-permute-start.3 = (f32[2,8,32,128]{3,2,1,0:T(8,128)S(1)}, f32[2,8,32,128]{3,2,1,0:T(8,128)S(1)}, u32[]{:S(2)}, u32[]{:S(2)}) collective-permute-start(f32[2,8,32,128]{3,2,1,0:T(8,128)S(1)} %get-tuple-element.12.mid), channel_id=1, source_target_pairs={{0,1},{1,2},{2,3},{3,4},{4,5},{5,6},{6,7},{8,9},{9,10},{10,11},{11... | collective-permute-start | bytes 786440 | tf_op jit(solution)/shard_map/ppermute | solution.py:260
  56.5 1.3 %collective-permute-start.4 = (f32[2,8,32,128]{3,2,1,0:T(8,128)S(1)}, f32[2,8,32,128]{3,2,1,0:T(8,128)S(1)}, u32[]{:S(2)}, u32[]{:S(2)}) collective-permute-start(f32[2,8,32,128]{3,2,1,0:T(8,128)S(1)} %get-tuple-element.12.mid), channel_id=1, source_target_pairs={{1,0},{2,1},{3,2},{4,3},{5,4},{6,5},{7,6},{9,8},{10,9},{11,10},{12... | collective-permute-start | bytes 786440 | tf_op jit(solution)/shard_map/ppermute | solution.py:261
  57.8 0.0 collective-permute-done.2.series
  57.8 2.6 %collective-permute-done.3.left = f32[2,8,32,128]{3,2,1,0:T(8,128)S(1)} collective-permute-done((f32[2,8,32,128]{3,2,1,0:T(8,128)S(1)}, f32[2,8,32,128]{3,2,1,0:T(8,128)S(1)}, u32[]{:S(2)}, u32[]{:S(2)}) %collective-permute-start.3) | collective-permute-done | bytes 262176 | tf_op jit(solution)/shard_map/ppermute | solution.py:260
  60.4 4.7 %collective-permute-done.4.right = f32[2,8,32,128]{3,2,1,0:T(8,128)S(1)} collective-permute-done((f32[2,8,32,128]{3,2,1,0:T(8,128)S(1)}, f32[2,8,32,128]{3,2,1,0:T(8,128)S(1)}, u32[]{:S(2)}, u32[]{:S(2)}) %collective-permute-start.4) | collective-permute-done | bytes 262176 | tf_op jit(solution)/shard_map/ppermute | solution.py:261
  65.1 12.4 %second_iteration_b.1 = f32[4,8,32,128]{3,2,1,0:T(8,128)S(1)} custom-call(s32[4]{0:T(128)S(1)} %pad_add_fusion.place, f32[4]{0:T(128)S(1)} %pad_maximum_fusion.1.edge, bf16[256,128]{1,0:T(8,128)(2,1)S(1)} %add_convert_fusion.taps, f32[3,8,96,128]{3,2,1,0:T(8,128)S(1)} %pack_window.1.mine, f32[3,8,96,128]{3,2,1,0:T(8,128)S(1)} %collective-permute-done.other, ...), custom_call_target="tpu_custom_call" | custom-call | tf_op jit(solution)/shard_map/second_iteration_b/pallas_call | solution.py:262
  77.6 0.1 pad_maximum_fusion
  77.6 23.0 %all_to_all.18 = f32[8,8,32,128]{3,2,1,0:T(8,128)S(1)} all-to-all(f32[8,8,32,128]{3,2,1,0:T(8,128)S(1)} %pad_maximum_fusion), channel_id=1, replica_groups=mesh['gx'=16,'ta'=8] {'ta'}, dimensions={0} | all-to-all | bytes 2097152 | tf_op jit(solution)/shard_map/all_to_all | solution.py:272
  100.6 1.1 %copy.4 = f32[1,8,8,32,128]{4,3,2,1,0:T(8,128)} copy(f32[1,8,8,32,128]{4,3,1,2,0:T(8,128)S(1)} %bitcast.12) | data formatting | bytes 2097152 | tf_op jit(solution)/shard_map/all_to_all | solution.py:272
  (3 shorter events, 0.0 us)
Async XLA Ops:
  0.4 1.2 %copy-start = (f32[8,256,128]{2,1,0:T(8,128)S(1)}, f32[8,256,128]{2,1,0:T(8,128)}, u32[]{:S(2)}) copy-start(f32[8,256,128]{2,1,0:T(8,128)} %u.3) | copy-start | bytes 3145732
  1.6 1.2 %copy-start.1 = (f32[8,256,128]{2,1,0:T(8,128)S(1)}, f32[8,256,128]{2,1,0:T(8,128)}, u32[]{:S(2)}) copy-start(f32[8,256,128]{2,1,0:T(8,128)} %r.3) | copy-start | bytes 3145732
  2.8 1.2 %copy-start.2 = (f32[8,256,128]{2,1,0:T(8,128)S(1)}, f32[8,256,128]{2,1,0:T(8,128)}, u32[]{:S(2)}) copy-start(f32[8,256,128]{2,1,0:T(8,128)} %s.3) | copy-start | bytes 3145732
  14.2 26.4 %collective-permute-start.1 = (f32[32,96,128]{2,1,0:T(8,128)S(1)}, f32[32,96,128]{2,1,0:T(8,128)S(1)}, u32[]{:S(2)}, u32[]{:S(2)}) collective-permute-start(f32[32,96,128]{2,1,0:T(8,128)S(1)} %get-tuple-element.9), channel_id=1, source_target_pairs={{0,8},{16,24},{32,40},{48,56},{64,72},{80,88},{96,104},{112,120},{... | collective-permute-start | bytes 4718600 | tf_op jit(solution)/shard_map/ppermute | solution.py:238
  22.6 35.2 %collective-permute-start.2 = (f32[32,96,128]{2,1,0:T(8,128)S(1)}, f32[32,96,128]{2,1,0:T(8,128)S(1)}, u32[]{:S(2)}, u32[]{:S(2)}) collective-permute-start(f32[32,96,128]{2,1,0:T(8,128)S(1)} %first_iteration_b.1), channel_id=1, source_target_pairs={{0,8},{16,24},{32,40},{48,56},{64,72},{80,88},{96,104},{112,120},{... | collective-permute-start | bytes 4718600 | tf_op jit(solution)/shard_map/ppermute | solution.py:248
  23.1 17.5 %collective-permute-start = (f32[3,8,96,128]{3,2,1,0:T(8,128)S(1)}, f32[3,8,96,128]{3,2,1,0:T(8,128)S(1)}, u32[]{:S(2)}, u32[]{:S(2)}) collective-permute-start(f32[3,8,96,128]{3,2,1,0:T(8,128)S(1)} %pack_window.1.mine), channel_id=1, source_target_pairs={{8,16},{24,32},{40,48},{56,64},{72,80},{88,96},{104,112},{16,8},{3... | collective-permute-start | bytes 3538952 | tf_op jit(solution)/shard_map/ppermute | solution.py:225
  53.1 7.4 %collective-permute-start.3 = (f32[2,8,32,128]{3,2,1,0:T(8,128)S(1)}, f32[2,8,32,128]{3,2,1,0:T(8,128)S(1)}, u32[]{:S(2)}, u32[]{:S(2)}) collective-permute-start(f32[2,8,32,128]{3,2,1,0:T(8,128)S(1)} %get-tuple-element.12.mid), channel_id=1, source_target_pairs={{0,1},{1,2},{2,3},{3,4},{4,5},{5,6},{6,7},{8,9},{9,10},{10,11},{11... | collective-permute-start | bytes 786440 | tf_op jit(solution)/shard_map/ppermute | solution.py:260
  56.5 8.6 %collective-permute-start.4 = (f32[2,8,32,128]{3,2,1,0:T(8,128)S(1)}, f32[2,8,32,128]{3,2,1,0:T(8,128)S(1)}, u32[]{:S(2)}, u32[]{:S(2)}) collective-permute-start(f32[2,8,32,128]{3,2,1,0:T(8,128)S(1)} %get-tuple-element.12.mid), channel_id=1, source_target_pairs={{1,0},{2,1},{3,2},{4,3},{5,4},{6,5},{7,6},{9,8},{10,9},{11,10},{12... | collective-permute-start | bytes 786440 | tf_op jit(solution)/shard_map/ppermute | solution.py:261

commit v2 on v0

v2 whole, which is shorter than its diff:
```python
import jax
import jax.numpy as jnp
from jax import lax
from jax.experimental import pallas as pl
from jax.experimental.pallas import tpu as pltpu
from jax.sharding import PartitionSpec as P

CX = 8
NZ = 128
STRIP = 32
HALO = 32
WINDOW = STRIP + 2 * HALO
WIDE = STRIP + 4 * HALO
PHASE = 32
STEPS = 8
PAD = 8
SERIES = STEPS * sum(range(WINDOW, STRIP, -16))
GROUP = 4
SNAKE = (0, 1, 2, 3, 7, 6, 5, 4)
BY_MATRIX = 4

VMEM = pl.BlockSpec(memory_space=pltpu.VMEM)
HBM = pl.BlockSpec(memory_space=pltpu.HBM)
ANY = pl.BlockSpec(memory_space=pl.ANY)


def z_matrix(taps):
    row = lax.broadcasted_iota(jnp.int32, (NZ, NZ), 0)
    col = lax.broadcasted_iota(jnp.int32, (NZ, NZ), 1)
    half = jnp.where(row == col - 1, 2.0, 0.0) + jnp.where(row == col + 1, 1.0, 0.0)
    taps[:NZ, :] = half.astype(jnp.bfloat16)
    taps[NZ:, :] = half.astype(jnp.bfloat16)
    return taps[...]


def position():
    interval = lax.axis_index("ta")
    slab = lax.axis_index("gx")
    slabs = lax.axis_size("gx")
    strip = jnp.where(interval < 4, interval, 11 - interval)
    odd = lax.rem(slab, 2) == 1

    def edges(at):
        return jnp.where(at > 0, 0.6, 0.0), jnp.where(at < slabs - 1, 0.6, 0.0)

    return strip, odd, edges(slab), edges(jnp.where(odd, slab + 1, slab - 1))


def z_sum(planes, taps):
    high = planes.astype(jnp.bfloat16)
    low = (planes - high.astype(jnp.float32)).astype(jnp.bfloat16)
    return jnp.dot(jnp.concatenate([high, low], 1), taps, preferred_element_type=jnp.float32)


def advance(src, dst, m, q, ghosts, edge, tiles, taps):
    lane = lax.broadcasted_iota(jnp.int32, (8, NZ), 1)
    not_first, not_last = lane != 0, lane != NZ - 1
    tiles = list(tiles)
    for begin in range(0, len(tiles), GROUP):
        group = tiles[begin : begin + GROUP]
        cells = [[src[x, PAD + 8 * t : PAD + 8 * t + 8, :] for x in range(CX)] for t in group]
        z_all = z_sum(jnp.concatenate([c[x] for c in cells for x in range(BY_MATRIX)], 0), taps)
        for at, t in enumerate(group):
            c = cells[at]
            low, high = ghosts(t, c)
            low = edge[0] * c[0] if low is None else edge[0] * c[0] + low
            high = edge[1] * c[-1] if high is None else edge[1] * c[-1] + high
            below = [low] + c[:-1]
            above = c[1:] + [high]
            for x in range(CX):
                y_below = src[x, PAD + 8 * t - 1 : PAD + 8 * t + 7, :]
                y_above = src[x, PAD + 8 * t + 1 : PAD + 8 * t + 9, :]
                if x < BY_MATRIX:
                    row = (at * BY_MATRIX + x) * 8
                    twice = below[x] + y_below
                    total = (twice + twice) + ((below[x] + above[x]) + y_above) + z_all[row : row + 8]
                else:
                    z_below = jnp.where(not_first, pltpu.roll(c[x], 1, 1), 0.0)
                    z_above = jnp.where(not_last, pltpu.roll(c[x], NZ - 1, 1), 0.0)
                    twice = below[x] + y_below + z_below
                    total = (twice + twice) + ((below[x] + above[x]) + (y_above + z_above))
                rows = slice(8 * t, 8 * t + 8)
                dst[x, PAD + 8 * t : PAD + 8 * t + 8, :] = total * m[x, rows, :] + q[x, rows, :]


def clear_pads(buffers, rows):
    for b in buffers:
        b[:, :PAD, :] = jnp.zeros((CX, PAD, NZ), jnp.float32)
        b[:, PAD + rows :, :] = jnp.zeros((CX, PAD, NZ), jnp.float32)


def traces(c):
    return c[CX - 2] - 0.6 * c[CX - 1], c[1] - 0.6 * c[0]


def series_rows(k, step, t):
    base = STEPS * sum(WINDOW - 16 * before for before in range(k))
    return pl.ds(pl.multiple_of(base + step * (WINDOW - 16 * k) + 8 * (t - k), 8), 8)


def window_blocks(strip, blocks, start):
    for b in range(blocks):
        at = strip + start + b
        inside = jnp.logical_and(at >= 0, at < 8)
        yield b, pl.multiple_of(jnp.clip(at, 0, 7) * STRIP, STRIP), jnp.where(inside, 1.0, 0.0)


def pack_kernel(u, r, s, out, ubuf, rbuf, sbuf, sems):
    strip, _, _, _ = position()
    copies = []
    for b, row, keep in window_blocks(strip, 3, -1):
        rows = pl.ds(b * STRIP, STRIP)
        for n, (a, v) in enumerate(((u, ubuf), (r, rbuf), (s, sbuf))):
            copies.append(pltpu.make_async_copy(a.at[:, pl.ds(row, STRIP), :], v.at[:, rows, :], sems.at[n, b]))
    for copy in copies:
        copy.start()
    for b, row, keep in window_blocks(strip, 3, -1):
        for copy in copies[3 * b : 3 * b + 3]:
            copy.wait()
        rows = slice(b * STRIP, (b + 1) * STRIP)
        scale = keep / (1.0 + rbuf[:, rows, :])
        out[0, :, rows, :] = ubuf[:, rows, :] * keep
        out[1, :, rows, :] = 0.1 * scale
        out[2, :, rows, :] = sbuf[:, rows, :] * scale


def phase(body):
    for k in range(PHASE // STEPS):
        def pair(p, _):
            for n in range(2):
                body(k, 2 * p + n, n)
            return 0
        lax.fori_loop(0, STEPS // 2, pair, 0)
        yield k


def first_a_kernel(u, r, s, packed, near_out, last, taps, ua, ub, m, q):
    strip, odd, edges, _ = position()
    for b, row, keep in window_blocks(strip, 5, -2):
        rows = slice(b * STRIP, (b + 1) * STRIP)
        scale = keep / (1.0 + r[:, pl.ds(row, STRIP), :])
        m[:, rows, :] = 0.1 * scale
        q[:, rows, :] = s[:, pl.ds(row, STRIP), :] * scale
        ua[:, PAD + b * STRIP : PAD + (b + 1) * STRIP, :] = u[:, pl.ds(row, STRIP), :] * keep
    clear_pads((ua, ub), WIDE)
    t_matrix = z_matrix(taps)

    def step(k, at, n):
        def ghosts(t, c):
            if 4 + k <= t < 16 - k:
                up, down = traces(c)
                near_out[series_rows(k, at, t - 4), :] = jnp.where(odd, down, up)
            return None, None

        src, dst = ((ua, ub), (ub, ua))[n]
        advance(src, dst, m, q, ghosts, edges, range(k, 20 - k), t_matrix)

    for _ in phase(step):
        pass
    last[...] = ua[:, PAD + HALO : PAD + HALO + WINDOW, :]


def first_b_kernel(u, mine, near_out, far_out, taps, ua, ub):
    _, odd, edges, _ = position()
    clear_pads((ua, ub), WINDOW)
    ua[:, PAD : PAD + WINDOW, :] = u[...]
    t_matrix = z_matrix(taps)

    def step(k, at, n):
        def ghosts(t, c):
            up, down = traces(c)
            rows = series_rows(k, at, t)
            near_out[rows, :] = jnp.where(odd, down, up)
            far_out[rows, :] = jnp.where(odd, up, down)
            return None, None

        src, dst = ((ua, ub), (ub, ua))[n]
        advance(src, dst, mine.at[1], mine.at[2], ghosts, edges, range(k, 12 - k), t_matrix)

    for _ in phase(step):
        pass


def second_a_kernel(mine, other, near_series, ends, taps, ua, ub, va, vb):
    _, odd, own_edges, other_edges = position()
    clear_pads((ua, ub, va, vb), WINDOW)
    ua[:, PAD : PAD + WINDOW, :] = mine[0]
    va[:, PAD : PAD + WINDOW, :] = other[0]
    t_matrix = z_matrix(taps)

    def step(k, at, n):
        src, dst, osrc, odst = ((ua, ub, va, vb), (ub, ua, vb, va))[n]

        def ghosts(t, c):
            rows = slice(PAD + 8 * t, PAD + 8 * t + 8)
            up, down = traces({x: osrc[x, rows, :] for x in (0, 1, CX - 2, CX - 1)})
            near = near_series[series_rows(k, at, t), :]
            return jnp.where(odd, near, up), jnp.where(odd, down, near)

        tiles = range(k, 12 - k)
        advance(src, dst, mine.at[1], mine.at[2], ghosts, own_edges, tiles, t_matrix)
        advance(osrc, odst, other.at[1], other.at[2], lambda t, c: (None, None), other_edges, tiles, t_matrix)

    for k in phase(step):
        ends[k] = ua[:, PAD + HALO : PAD + HALO + STRIP, :]


def second_b_kernel(mine, near_series, far_series, even_swap, mid, odd_swap, ends, taps, ua, ub):
    strip, odd, edges, _ = position()
    clear_pads((ua, ub), WINDOW)
    odd_strip = lax.rem(strip, 2) == 1

    def put(left, right):
        for at, part in enumerate((left, mid, right)):
            ua[:, PAD + at * STRIP : PAD + (at + 1) * STRIP, :] = part[...]

    pl.when(odd_strip)(lambda: put(even_swap, odd_swap))
    pl.when(jnp.logical_not(odd_strip))(lambda: put(odd_swap, even_swap))
    t_matrix = z_matrix(taps)

    def step(k, at, n):
        def ghosts(t, c):
            rows = series_rows(k, at, t)
            near, far = near_series[rows, :], far_series[rows, :]
            return jnp.where(odd, near, far), jnp.where(odd, far, near)

        src, dst = ((ua, ub), (ub, ua))[n]
        advance(src, dst, mine.at[1], mine.at[2], ghosts, edges, range(k, 12 - k), t_matrix)

    for k in phase(step):
        ends[k] = ua[:, PAD + HALO : PAD + HALO + STRIP, :]


def swaps(some, others):
    pairs = list(zip(some, others))
    return pairs + [(b, a) for a, b in pairs]


def f32(*shape):
    return jax.ShapeDtypeStruct(shape, jnp.float32)


def buffer(rows):
    return pltpu.VMEM((CX, rows, NZ), jnp.float32)


def local(u, r, s):
    slabs = lax.axis_size("gx")

    def kernel(body, outs, ins, scratch, name, micros, vmem=48):
        return pl.pallas_call(
            body,
            out_shape=outs,
            in_specs=ins,
            out_specs=jax.tree.map(lambda _: VMEM, outs),
            scratch_shapes=scratch,
            compiler_params=pltpu.CompilerParams(vmem_limit_bytes=vmem << 20),
            cost_estimate=pl.CostEstimate(flops=0, transcendentals=0, bytes_accessed=int(micros * 3.6e6)),
            name=name,
        )

    taps = pltpu.VMEM((2 * NZ, NZ), jnp.bfloat16)
    padded = buffer(WINDOW + 2 * PAD)
    mine = kernel(
        pack_kernel, f32(3, CX, WINDOW, NZ), [HBM, HBM, HBM],
        [buffer(WINDOW)] * 3 + [pltpu.SemaphoreType.DMA((3, 3))], "pack_window", 2.0, 62,
    )(u, r, s)
    far_swap = swaps(range(1, slabs - 1, 2), range(2, slabs, 2))
    near_swap = swaps(range(0, slabs, 2), range(1, slabs, 2))
    theirs = lax.ppermute(mine, "gx", far_swap)

    series = f32(SERIES, NZ)
    near_a, state = kernel(
        first_a_kernel, (series, f32(CX, WINDOW, NZ)), [VMEM, VMEM, VMEM, ANY],
        [taps] + [buffer(WIDE + 2 * PAD)] * 2 + [buffer(WIDE)] * 2,
        "first_iteration_a", 11.0,
    )(u, r, s, mine)
    near_a = lax.ppermute(near_a, "gx", near_swap)
    near_b, far_b = kernel(
        first_b_kernel, (series, series), [VMEM, VMEM], [taps] + [padded] * 2, "first_iteration_b", 6.0
    )(state, mine)
    near_b = lax.ppermute(near_b, "gx", near_swap)
    far_b = lax.ppermute(far_b, "gx", far_swap)

    ends_a = kernel(
        second_a_kernel, f32(4, CX, STRIP, NZ), [VMEM] * 3, [taps] + [padded] * 4, "second_iteration_a", 12.0
    )(mine, theirs, near_a)
    last = ends_a[3]
    even_swap = lax.ppermute(last, "ta", swaps(SNAKE[0::2], SNAKE[1::2]))
    odd_swap = lax.ppermute(last, "ta", swaps(SNAKE[1:-1:2], SNAKE[2::2]))
    ends_b = kernel(
        second_b_kernel, f32(4, CX, STRIP, NZ), [VMEM] * 6, [taps] + [padded] * 2, "second_iteration_b", 7.0
    )(mine, near_b, far_b, even_swap, last, odd_swap)
    ends = jnp.concatenate([ends_a, ends_b], 0)
    strips = lax.all_to_all(ends, "ta", 0, 0, tiled=True)
    return jnp.concatenate([strips[i] for i in SNAKE], 1)[None]


def solution(mesh):
    return jax.shard_map(
        local,
        mesh=mesh,
        in_specs=(P("gx", None, None), P("gx", None, None), P("gx", None, None)),
        out_specs=P("ta", "gx", None, None),
        check_vma=False,
    )
```

time: 685 us -> 78.7 us (0.11)
  the two profiles are of different devices: /device:TPU:32 before, /device:TPU:0 now
where the time goes in v2:
time: 78.7 us; the launch traced here: 78.4 us
  Pallas kernels  32.9 us (42%)
  blocking collectives  27.9 us (35%)
  starting transfers between devices  9.56 us (12%)
  local copies, waits for them, and re-layouts  4.79 us (6%)
  waiting for transfers between devices  2.95 us (4%)
    all_to_all x1, blocking collectives, local(): strips = lax.all_to_all(ends, 'ta', 0, 0, tiled=True)  27.9 us
    pallas_call x1, Pallas kernels, local(): kernel(second_a_kernel, f32(4, CX, STRIP, NZ), [VMEM] * 3, [taps] + [padd...  9.65 us
    pallas_call x1, Pallas kernels, local(): kernel(first_a_kernel, (series, f32(CX, WINDOW, NZ)), [VMEM, VMEM, VMEM,...  8.9 us
    pallas_call x1, Pallas kernels, local(): kernel(second_b_kernel, f32(4, CX, STRIP, NZ), [VMEM] * 6, [taps] + [padd...  5.99 us
    pallas_call x1, Pallas kernels, local(): kernel(first_b_kernel, (series, series), [VMEM, VMEM], [taps] + [padded]...  5.86 us
    unnamed x19, local copies, waits for them, and re-layouts  4.76 us
    ppermute x1, starting transfers between devices, local(): even_swap = lax.ppermute(last, 'ta', swaps(SNAKE[0::2], SNAKE[1::2]))  4.3 us
    ppermute x1, starting transfers between devices, local(): near_a = lax.ppermute(near_a, 'gx', near_swap)  3.02 us
  transfers between devices with their start and end apart: 6, of which 1 were waited for; matrix products, arithmetic and copies ran while one was open for 0% of the time, Pallas kernels for 31%

profile of v2, /device:TPU:0, one launch (start us, length us, event | category | flops | bytes accessed | tf_op | source)
XLA Modules:
  0.0 78.4 jit_solution(6672511738544715238)
XLA Ops:
  0.0 0.0 copy-start.2
  0.0 2.5 %pack_window.1.packed.mine = f32[3,8,96,128]{3,2,1,0:T(8,128)} custom-call(f32[8,256,128]{2,1,0:T(8,128)} %u.3, f32[8,256,128]{2,1,0:T(8,128)} %r.3, f32[8,256,128]{2,1,0:T(8,128)} %s.3), custom_call_target="tpu_custom_call" | custom-call | bytes 7200000 | tf_op jit(solution)/shard_map/pack_window/pallas_call | solution.py:264
  2.6 0.7 collective-permute-start
  3.3 0.0 copy-done.2
  3.3 0.0 copy-start
  3.3 1.3 %copy-done = f32[3,8,96,128]{3,2,1,0:T(8,128)S(1)} copy-done((f32[3,8,96,128]{3,2,1,0:T(8,128)S(1)}, f32[3,8,96,128]{3,2,1,0:T(8,128)}, u32[]{:S(2)}) %copy-start) | copy-done | bytes 1179672
  4.6 0.0 copy-start.3
  4.6 1.2 %copy-done.3 = f32[8,256,128]{2,1,0:T(8,128)S(1)} copy-done((f32[8,256,128]{2,1,0:T(8,128)S(1)}, f32[8,256,128]{2,1,0:T(8,128)}, u32[]{:S(2)}) %copy-start.3) | copy-done | bytes 1048600
  5.8 0.0 copy-start.4
  5.8 1.2 %copy-done.4 = f32[8,256,128]{2,1,0:T(8,128)S(1)} copy-done((f32[8,256,128]{2,1,0:T(8,128)S(1)}, f32[8,256,128]{2,1,0:T(8,128)}, u32[]{:S(2)}) %copy-start.4) | copy-done | bytes 1048600
  7.0 0.0 copy-start.1
  7.0 8.9 %first_iteration_a.1 = (f32[2304,128]{1,0:T(8,128)S(1)}, f32[8,96,128]{2,1,0:T(8,128)S(1)}) custom-call(f32[8,256,128]{2,1,0:T(8,128)S(1)} %copy-done.2, f32[8,256,128]{2,1,0:T(8,128)S(1)} %copy-done.3, f32[8,256,128]{2,1,0:T(8,128)S(1)} %copy-done.4, f32[3,8,96,128]{3,2,1,0:T(8,128)S(1)} %copy-done), custom_call_target="tpu_custom_call" | custom-call | bytes 39600000 | tf_op jit(solution)/shard_map/first_iteration_a/pallas_call | solution.py:273
  15.9 3.0 %collective-permute-start.1 = (f32[2304,128]{1,0:T(8,128)S(1)}, f32[2304,128]{1,0:T(8,128)S(1)}, u32[]{:S(2)}, u32[]{:S(2)}) collective-permute-start(f32[2304,128]{1,0:T(8,128)S(1)} %get-tuple-element.9), channel_id=1, source_target_pairs={{0,8},{16,24},{32,40},{48,56},{64,72},{80,88},{96,104},{112,120},{... | collective-permute-start | bytes 3538952 | tf_op jit(solution)/shard_map/ppermute | solution.py:278
  19.0 0.0 copy-done.1
  19.0 5.9 %first_iteration_b.1 = (f32[2304,128]{1,0:T(8,128)S(1)}, f32[2304,128]{1,0:T(8,128)S(1)}) custom-call(f32[8,96,128]{2,1,0:T(8,128)S(1)} %get-tuple-element.10.u, f32[3,8,96,128]{3,2,1,0:T(8,128)S(1)} %copy-done.1), custom_call_target="tpu_custom_call" | custom-call | bytes 21600000 | tf_op jit(solution)/shard_map/first_iteration_b/pallas_call | solution.py:279
  24.8 0.1 collective-permute-start.2
  24.9 0.7 collective-permute-start.3
  25.7 0.0 collective-permute-done.other
  25.7 0.0 collective-permute-done.1.near_series
  25.7 9.6 %second_iteration_a.1 = f32[4,8,32,128]{3,2,1,0:T(8,128)S(1)} custom-call(f32[3,8,96,128]{3,2,1,0:T(8,128)S(1)} %copy-done.1, f32[3,8,96,128]{3,2,1,0:T(8,128)S(1)} %collective-permute-done.other, f32[2304,128]{1,0:T(8,128)S(1)} %collective-permute-done.1.near_series), custom_call_target="tpu_custom_call" | custom-call | bytes 43200000 | tf_op jit(solution)/shard_map/second_iteration_a/pallas_call | solution.py:285
  35.4 0.7 collective-permute-start.5
  36.0 4.3 %collective-permute-start.4 = (f32[8,32,128]{2,1,0:T(8,128)S(1)}, f32[8,32,128]{2,1,0:T(8,128)S(1)}, u32[]{:S(2)}, u32[]{:S(2)}) collective-permute-start(f32[8,32,128]{2,1,0:T(8,128)S(1)} %slice_bitcast_fusion.8.mid), channel_id=1, source_target_pairs={{0,1},{2,3},{7,6},{5,4},{1,0},{3,2},{6,7},{4,5},{8,9},{10,11},{15,... | collective-permute-start | bytes 393224 | tf_op jit(solution)/shard_map/ppermute | solution.py:289
  40.3 0.0 collective-permute-done.2.near_series
  40.3 0.0 collective-permute-done.3.far_series
  40.3 0.0 collective-permute-done.5.odd_swap
  40.4 2.9 %collective-permute-done.4.even_swap = f32[8,32,128]{2,1,0:T(8,128)S(1)} collective-permute-done((f32[8,32,128]{2,1,0:T(8,128)S(1)}, f32[8,32,128]{2,1,0:T(8,128)S(1)}, u32[]{:S(2)}, u32[]{:S(2)}) %collective-permute-start.4) | collective-permute-done | bytes 131104 | tf_op jit(solution)/shard_map/ppermute | solution.py:289
  43.3 6.0 %second_iteration_b.1 = f32[4,8,32,128]{3,2,1,0:T(8,128)S(1)} custom-call(f32[3,8,96,128]{3,2,1,0:T(8,128)S(1)} %copy-done.1, f32[2304,128]{1,0:T(8,128)S(1)} %collective-permute-done.2.near_series, f32[2304,128]{1,0:T(8,128)S(1)} %collective-permute-done.3.far_series, f32[8,32,128]{2,1,0:T(8,128)S(1)} %collective-permute-done.4.even_swap, ...), custom_call_target="tpu_custom_call" | custom-call | bytes 25200000 | tf_op jit(solution)/shard_map/second_iteration_b/pallas_call | solution.py:291
  49.3 0.1 pad_maximum_fusion
  49.4 27.9 %all_to_all.5 = f32[8,8,32,128]{3,2,1,0:T(8,128)S(1)} all-to-all(f32[8,8,32,128]{3,2,1,0:T(8,128)S(1)} %pad_maximum_fusion), channel_id=1, replica_groups=mesh['gx'=16,'ta'=8] {'ta'}, dimensions={0} | all-to-all | bytes 2097152 | tf_op jit(solution)/shard_map/all_to_all | solution.py:295
  77.4 0.0 copy-start.5
  77.5 1.0 %copy-done.5 = f32[8,256,128]{2,1,0:T(8,128)} copy-done((f32[8,256,128]{2,1,0:T(8,128)}, f32[8,256,128]{2,1,0:T(8,128)S(1)}, u32[]{:S(2)}) %copy-start.5) | copy-done | bytes 1048600
  (9 shorter events, 0.1 us)
Async XLA Ops:
  0.0 3.3 %copy-start.2 = (f32[8,256,128]{2,1,0:T(8,128)S(1)}, f32[8,256,128]{2,1,0:T(8,128)}, u32[]{:S(2)}) copy-start(f32[8,256,128]{2,1,0:T(8,128)} %u.3) | copy-start | bytes 3145732
  2.6 23.1 %collective-permute-start = (f32[3,8,96,128]{3,2,1,0:T(8,128)}, f32[3,8,96,128]{3,2,1,0:T(8,128)S(1)}, u32[]{:S(2)}, u32[]{:S(2)}) collective-permute-start(f32[3,8,96,128]{3,2,1,0:T(8,128)} %pack_window.1.packed.mine), channel_id=1, source_target_pairs={{8,16},{24,32},{40,48},{56,64},{72,80},{88,96},{104,112},{16,8},{3... | collective-permute-start | bytes 3538952 | tf_op jit(solution)/shard_map/ppermute | solution.py:270
  3.3 1.3 %copy-start = (f32[3,8,96,128]{3,2,1,0:T(8,128)S(1)}, f32[3,8,96,128]{3,2,1,0:T(8,128)}, u32[]{:S(2)}) copy-start(f32[3,8,96,128]{3,2,1,0:T(8,128)} %pack_window.1.packed.mine) | copy-start | bytes 3538948
  4.6 1.2 %copy-start.3 = (f32[8,256,128]{2,1,0:T(8,128)S(1)}, f32[8,256,128]{2,1,0:T(8,128)}, u32[]{:S(2)}) copy-start(f32[8,256,128]{2,1,0:T(8,128)} %r.3) | copy-start | bytes 3145732
  5.8 1.2 %copy-start.4 = (f32[8,256,128]{2,1,0:T(8,128)S(1)}, f32[8,256,128]{2,1,0:T(8,128)}, u32[]{:S(2)}) copy-start(f32[8,256,128]{2,1,0:T(8,128)} %s.3) | copy-start | bytes 3145732
  7.0 11.9 %copy-start.1 = (f32[3,8,96,128]{3,2,1,0:T(8,128)S(1)}, f32[3,8,96,128]{3,2,1,0:T(8,128)}, u32[]{:S(2)}) copy-start(f32[3,8,96,128]{3,2,1,0:T(8,128)} %pack_window.1.packed.mine) | copy-start | bytes 3538948
  15.9 9.7 %collective-permute-start.1 = (f32[2304,128]{1,0:T(8,128)S(1)}, f32[2304,128]{1,0:T(8,128)S(1)}, u32[]{:S(2)}, u32[]{:S(2)}) collective-permute-start(f32[2304,128]{1,0:T(8,128)S(1)} %get-tuple-element.9), channel_id=1, source_target_pairs={{0,8},{16,24},{32,40},{48,56},{64,72},{80,88},{96,104},{112,120},{... | collective-permute-start | bytes 3538952 | tf_op jit(solution)/shard_map/ppermute | solution.py:278
  24.8 15.5 %collective-permute-start.2 = (f32[2304,128]{1,0:T(8,128)S(1)}, f32[2304,128]{1,0:T(8,128)S(1)}, u32[]{:S(2)}, u32[]{:S(2)}) collective-permute-start(f32[2304,128]{1,0:T(8,128)S(1)} %get-tuple-element.11), channel_id=1, source_target_pairs={{0,8},{16,24},{32,40},{48,56},{64,72},{80,88},{96,104},{112,120},{... | collective-permute-start | bytes 3538952 | tf_op jit(solution)/shard_map/ppermute | solution.py:282
  24.9 15.4 %collective-permute-start.3 = (f32[2304,128]{1,0:T(8,128)S(1)}, f32[2304,128]{1,0:T(8,128)S(1)}, u32[]{:S(2)}, u32[]{:S(2)}) collective-permute-start(f32[2304,128]{1,0:T(8,128)S(1)} %get-tuple-element.12), channel_id=1, source_target_pairs={{8,16},{24,32},{40,48},{56,64},{72,80},{88,96},{104,112},{16,8},{3... | collective-permute-start | bytes 3538952 | tf_op jit(solution)/shard_map/ppermute | solution.py:283
  35.4 5.0 %collective-permute-start.5 = (f32[8,32,128]{2,1,0:T(8,128)S(1)}, f32[8,32,128]{2,1,0:T(8,128)S(1)}, u32[]{:S(2)}, u32[]{:S(2)}) collective-permute-start(f32[8,32,128]{2,1,0:T(8,128)S(1)} %slice_bitcast_fusion.8.mid), channel_id=1, source_target_pairs={{1,2},{3,7},{6,5},{2,1},{7,3},{5,6},{9,10},{11,15},{14,13},{10,9},... | collective-permute-start | bytes 393224 | tf_op jit(solution)/shard_map/ppermute | solution.py:290
  36.0 7.2 %collective-permute-start.4 = (f32[8,32,128]{2,1,0:T(8,128)S(1)}, f32[8,32,128]{2,1,0:T(8,128)S(1)}, u32[]{:S(2)}, u32[]{:S(2)}) collective-permute-start(f32[8,32,128]{2,1,0:T(8,128)S(1)} %slice_bitcast_fusion.8.mid), channel_id=1, source_target_pairs={{0,1},{2,3},{7,6},{5,4},{1,0},{3,2},{6,7},{4,5},{8,9},{10,11},{15,... | collective-permute-start | bytes 393224 | tf_op jit(solution)/shard_map/ppermute | solution.py:289
  77.4 1.0 %copy-start.5 = (f32[8,256,128]{2,1,0:T(8,128)}, f32[8,256,128]{2,1,0:T(8,128)S(1)}, u32[]{:S(2)}) copy-start(f32[8,256,128]{2,1,0:T(8,128)S(1)} %fusion) | copy-start | bytes 3145732

commit v3 on v2

v3 whole, which is shorter than its diff:
```python
import jax
import jax.numpy as jnp
from jax import lax
from jax.experimental import pallas as pl
from jax.experimental.pallas import tpu as pltpu
from jax.sharding import PartitionSpec as P

CX = 8
NZ = 128
STRIP = 32
HALO = 32
WINDOW = STRIP + 2 * HALO
WIDE = STRIP + 4 * HALO
PHASE = 32
STEPS = 8
PAD = 8
MIDDLE = WIDE - 32
GROUP = 4
SNAKE = (0, 1, 2, 3, 7, 6, 5, 4)
BY_MATRIX = 4

VMEM = pl.BlockSpec(memory_space=pltpu.VMEM)
ANY = pl.BlockSpec(memory_space=pl.ANY)
HBM = pl.BlockSpec(memory_space=pltpu.HBM)


def z_matrix(taps):
    row = lax.broadcasted_iota(jnp.int32, (NZ, NZ), 0)
    col = lax.broadcasted_iota(jnp.int32, (NZ, NZ), 1)
    half = jnp.where(row == col - 1, 2.0, 0.0) + jnp.where(row == col + 1, 1.0, 0.0)
    taps[:NZ, :] = half.astype(jnp.bfloat16)
    taps[NZ:, :] = half.astype(jnp.bfloat16)
    return taps[...]


def position():
    interval = lax.axis_index("ta")
    slab = lax.axis_index("gx")
    slabs = lax.axis_size("gx")
    strip = jnp.where(interval < 4, interval, 11 - interval)
    edges = jnp.where(slab > 0, 0.6, 0.0), jnp.where(slab < slabs - 1, 0.6, 0.0)
    return strip, lax.rem(slab, 2) == 1, edges


def z_sum(planes, taps):
    high = planes.astype(jnp.bfloat16)
    low = (planes - high.astype(jnp.float32)).astype(jnp.bfloat16)
    return jnp.dot(jnp.concatenate([high, low], 1), taps, preferred_element_type=jnp.float32)


def advance(src, dst, m, q, ghosts, edge, tiles, taps):
    lane = lax.broadcasted_iota(jnp.int32, (8, NZ), 1)
    not_first, not_last = lane != 0, lane != NZ - 1
    tiles = list(tiles)
    for begin in range(0, len(tiles), GROUP):
        group = tiles[begin : begin + GROUP]
        cells = [[src[x, PAD + 8 * t : PAD + 8 * t + 8, :] for x in range(CX)] for t in group]
        z_all = z_sum(jnp.concatenate([c[x] for c in cells for x in range(BY_MATRIX)], 0), taps)
        for at, t in enumerate(group):
            c = cells[at]
            low, high = ghosts(t, c)
            low = edge[0] * c[0] if low is None else edge[0] * c[0] + low
            high = edge[1] * c[-1] if high is None else edge[1] * c[-1] + high
            below = [low] + c[:-1]
            above = c[1:] + [high]
            for x in range(CX):
                y_below = src[x, PAD + 8 * t - 1 : PAD + 8 * t + 7, :]
                y_above = src[x, PAD + 8 * t + 1 : PAD + 8 * t + 9, :]
                if x < BY_MATRIX:
                    row = (at * BY_MATRIX + x) * 8
                    twice = below[x] + y_below
                    total = (twice + twice) + ((below[x] + above[x]) + y_above) + z_all[row : row + 8]
                else:
                    z_below = jnp.where(not_first, pltpu.roll(c[x], 1, 1), 0.0)
                    z_above = jnp.where(not_last, pltpu.roll(c[x], NZ - 1, 1), 0.0)
                    twice = below[x] + y_below + z_below
                    total = (twice + twice) + ((below[x] + above[x]) + (y_above + z_above))
                rows = slice(8 * t, 8 * t + 8)
                dst[x, PAD + 8 * t : PAD + 8 * t + 8, :] = total * m[x, rows, :] + q[x, rows, :]


def clear_pads(buffers, rows):
    for b in buffers:
        b[:, :PAD, :] = jnp.zeros((CX, PAD, NZ), jnp.float32)
        b[:, PAD + rows :, :] = jnp.zeros((CX, PAD, NZ), jnp.float32)


def traces(c):
    return c[CX - 2] - 0.6 * c[CX - 1], c[1] - 0.6 * c[0]


def series_rows(k, step, t, first=0):
    base = STEPS * sum(WINDOW - 16 * before for before in range(first, k))
    return pl.ds(pl.multiple_of(base + step * (WINDOW - 16 * k) + 8 * (t - k), 8), 8)


def load_window(u, r, s, ubuf, rbuf, sbuf, sems, strip, height, put):
    halo = (height - STRIP) // 2
    first = strip * STRIP - halo
    start = pl.multiple_of(jnp.clip(first, 0, u.shape[1] - height), STRIP)
    landing = pl.multiple_of(halo + start - first, STRIP)
    copies = [
        pltpu.make_async_copy(a.at[:, pl.ds(start, height), :], v.at[:, pl.ds(landing, height), :], sems.at[n])
        for n, (a, v) in enumerate(((u, ubuf), (r, rbuf), (s, sbuf)))
    ]
    for copy in copies:
        copy.start()
    for copy in copies:
        copy.wait()
    for b in range(height // STRIP):
        at = strip + b - halo // STRIP
        keep = jnp.logical_and(at >= 0, at < u.shape[1] // STRIP)
        here = slice(halo + b * STRIP, halo + (b + 1) * STRIP)
        scale = 1.0 / (1.0 + rbuf[:, here, :])
        parts = ubuf[:, here, :], 0.1 * scale, sbuf[:, here, :] * scale
        put(slice(b * STRIP, (b + 1) * STRIP), [jnp.where(keep, part, 0.0) for part in parts])


def phase(body, intervals=range(PHASE // STEPS)):
    for k in intervals:
        def pair(p, _):
            for n in range(2):
                body(k, 2 * p + n, n)
            return 0
        lax.fori_loop(0, STEPS // 2, pair, 0)
        yield k


def first_iteration(m, q, near_out, far_out, taps, ua, ub, odd, edges, intervals, margin):
    t_matrix = z_matrix(taps)
    begin = intervals[0]

    def step(k, at, n):
        def ghosts(t, c):
            t = t - margin
            if k <= t < WINDOW // 8 - k:
                up, down = traces(c)
                rows = series_rows(k, at, t, begin)
                near_out[rows, :] = jnp.where(odd, down, up)
                far_out[rows, :] = jnp.where(odd, up, down)
            return None, None

        src, dst = ((ua, ub), (ub, ua))[n]
        tiles = m.shape[1] // 8
        advance(src, dst, m, q, ghosts, edges, range(k - begin, tiles - k + begin), t_matrix)

    for _ in phase(step, intervals):
        pass


def first_a_kernel(u, r, s, near_out, far_out, kept, start, taps, ubuf, rbuf, sbuf, ua, ub, m, q, sems):
    strip, odd, edges = position()

    def put(rows, parts):
        ua[:, PAD + rows.start : PAD + rows.stop, :], m[:, rows, :], q[:, rows, :] = parts

    clear_pads((ua, ub), WIDE)
    load_window(u, r, s, ubuf, rbuf, sbuf, sems, strip, WIDE, put)
    start[...] = ua[:, PAD + HALO : PAD + HALO + WINDOW, :]
    first_iteration(m, q, near_out, far_out, taps, ua, ub, odd, edges, (0, 1), 4)
    kept[0] = ua[:, PAD + 16 : PAD + 16 + MIDDLE, :]
    kept[1] = m[:, 16 : 16 + MIDDLE, :]
    kept[2] = q[:, 16 : 16 + MIDDLE, :]


def first_b_kernel(kept, near_in, far_in, near_out, far_out, last, taps, ua, ub):
    _, odd, edges = position()
    clear_pads((ua, ub), MIDDLE)
    ua[:, PAD : PAD + MIDDLE, :] = kept[0]
    before = near_in.shape[0]
    near_out[:before, :] = near_in[...]
    far_out[:before, :] = far_in[...]
    rest = pl.ds(before, near_out.shape[0] - before)
    first_iteration(
        kept.at[1], kept.at[2], near_out.at[rest, :], far_out.at[rest, :], taps, ua, ub, odd, edges, (2, 3), 2
    )
    last[...] = ua[:, PAD + 16 : PAD + 16 + WINDOW, :]


def inner(kept):
    return [kept.at[n, :, pl.ds(16, WINDOW), :] for n in (1, 2)]


def first_c_kernel(u, kept, near_out, far_out, taps, ua, ub):
    _, odd, edges = position()
    clear_pads((ua, ub), WINDOW)
    ua[:, PAD : PAD + WINDOW, :] = u[...]
    first_iteration(*inner(kept), near_out, far_out, taps, ua, ub, odd, edges, range(4), 0)


def second_iteration(kept, near, far, ends, taps, ua, ub, odd, edges):
    t_matrix = z_matrix(taps)
    m, q = inner(kept)

    def step(k, at, n):
        def ghosts(t, c):
            rows = series_rows(k, at, t)
            near_trace, far_trace = near[rows, :], far[rows, :]
            return jnp.where(odd, near_trace, far_trace), jnp.where(odd, far_trace, near_trace)

        src, dst = ((ua, ub), (ub, ua))[n]
        advance(src, dst, m, q, ghosts, edges, range(k, WINDOW // 8 - k), t_matrix)

    for k in phase(step):
        ends[k] = ua[:, PAD + HALO : PAD + HALO + STRIP, :]


def second_a_kernel(start, kept, near, far, ends, taps, ua, ub):
    _, odd, edges = position()
    clear_pads((ua, ub), WINDOW)
    ua[:, PAD : PAD + WINDOW, :] = start[...]
    second_iteration(kept, near, far, ends, taps, ua, ub, odd, edges)


def second_b_kernel(kept, near, far, even_swap, mid, odd_swap, ends, taps, ua, ub):
    strip, odd, edges = position()
    clear_pads((ua, ub), WINDOW)
    odd_strip = lax.rem(strip, 2) == 1

    def put(left, right):
        for at, part in enumerate((left, mid, right)):
            ua[:, PAD + at * STRIP : PAD + (at + 1) * STRIP, :] = part[...]

    pl.when(odd_strip)(lambda: put(even_swap, odd_swap))
    pl.when(jnp.logical_not(odd_strip))(lambda: put(odd_swap, even_swap))
    second_iteration(kept, near, far, ends, taps, ua, ub, odd, edges)


def swaps(some, others):
    pairs = list(zip(some, others))
    return pairs + [(b, a) for a, b in pairs]


def buffer(rows):
    return pltpu.VMEM((CX, rows, NZ), jnp.float32)


def local(u, r, s):
    slabs = lax.axis_size("gx")
    taps = pltpu.VMEM((2 * NZ, NZ), jnp.bfloat16)
    padded = buffer(WINDOW + 2 * PAD)

    def out(*shape):
        return pltpu.VMEM(shape, jnp.float32)

    def kernel(body, outs, ins, scratch, name, micros, after=0):
        def run(*refs):
            body(*refs[: len(ins)], *refs[len(ins) + after :])

        return pl.pallas_call(
            run,
            out_shape=outs,
            in_specs=ins + [ANY] * after,
            out_specs=jax.tree.map(lambda _: VMEM, outs),
            scratch_shapes=scratch,
            compiler_params=pltpu.CompilerParams(vmem_limit_bytes=40 << 20),
            cost_estimate=pl.CostEstimate(flops=0, transcendentals=0, bytes_accessed=int(micros * 3.6e6)),
            name=name,
        )

    far_swap = swaps(range(1, slabs - 1, 2), range(2, slabs, 2))
    near_swap = swaps(range(0, slabs, 2), range(1, slabs, 2))
    early, late = (STEPS * (2 * WINDOW - 16 - 64 * n) for n in range(2))

    u, r, s = (pltpu.with_memory_space_constraint(a, pltpu.HBM) for a in (u, r, s))
    wide_work = [buffer(WIDE + 4 * HALO)] * 3 + [buffer(WIDE + 2 * PAD)] * 2 + [buffer(WIDE)] * 2
    near_a, far_a, kept, start = kernel(
        first_a_kernel,
        (out(early, NZ), out(early, NZ), out(3, CX, MIDDLE, NZ), out(CX, WINDOW, NZ)),
        [HBM] * 3, [taps] + wide_work + [pltpu.SemaphoreType.DMA((3,))], "first_iteration_a", 0.01,
    )(u, r, s)
    series = out(early + late, NZ)
    near_b, far_b, state = kernel(
        first_b_kernel, (series, series, out(CX, WINDOW, NZ)),
        [VMEM] * 3, [taps] + [buffer(MIDDLE + 2 * PAD)] * 2, "first_iteration_b", 3.0,
    )(kept, near_a, far_a)
    near_c, far_c = kernel(
        first_c_kernel, (series, series), [VMEM, VMEM], [taps] + [padded] * 2, "first_iteration_c", 3.0, 2
    )(state, kept, near_b, far_b)
    theirs = [
        (lax.ppermute(near, "gx", near_swap), lax.ppermute(far, "gx", far_swap))
        for near, far in ((near_b, far_b), (near_c, far_c))
    ]
    ends_a = kernel(
        second_a_kernel, out(4, CX, STRIP, NZ), [VMEM] * 4, [taps] + [padded] * 2, "second_iteration_a", 12.0, 2
    )(start, kept, *theirs[0], near_c, far_c)
    last = ends_a[3]
    even_swap = lax.ppermute(last, "ta", swaps(SNAKE[0::2], SNAKE[1::2]))
    odd_swap = lax.ppermute(last, "ta", swaps(SNAKE[1:-1:2], SNAKE[2::2]))
    ends_b = kernel(
        second_b_kernel, out(4, CX, STRIP, NZ), [VMEM] * 6, [taps] + [padded] * 2, "second_iteration_b", 3.0
    )(kept, *theirs[1], even_swap, last, odd_swap)
    ends = jnp.concatenate([ends_a, ends_b], 0)
    strips = lax.all_to_all(ends, "ta", 0, 0, tiled=True)
    return jnp.concatenate([strips[i] for i in SNAKE], 1)[None]


def solution(mesh):
    return jax.shard_map(
        local,
        mesh=mesh,
        in_specs=(P("gx", None, None), P("gx", None, None), P("gx", None, None)),
        out_specs=P("ta", "gx", None, None),
        check_vma=False,
    )
```

time: 78.7 us -> 76.5 us (0.972)
  blocking collectives: 27.9 us -> 36.8 us
  Pallas kernels: 32.9 us -> 28.6 us
  local copies, waits for them, and re-layouts: 4.79 us -> 1.07 us
  starting transfers between devices: 9.56 us -> 6.8 us
    all_to_all x1, blocking collectives: 27.9 us -> 36.8 us  [local(): strips = lax.all_to_all(ends, 'ta', 0, 0, tiled=True)]
    pallas_call x5, Pallas kernels: 32.9 us -> 28.6 us  [the longest x1 6.66 us: local(): kernel(first_a_kernel, (out(early, NZ), out(early, NZ), out(3, CX, MIDDLE...]
    unnamed x19 -> x9, local copies, waits for them, and re-layouts: 4.76 us -> 1.04 us
    ppermute x1, starting transfers between devices: 4.3 us -> 1.57 us  [local(): even_swap = lax.ppermute(last, 'ta', swaps(SNAKE[0::2], SNAKE[1::2]))]
  transfers between devices with their start and end apart: 6 -> 6, of which waited for: 1 -> 1; matrix products, arithmetic and copies ran while one was open for 0% -> 0% of each run, Pallas kernels for 31% -> 16%
where the time goes in v3:
time: 76.5 us; the launch traced here: 76.3 us
  blocking collectives  36.8 us (48%)
  Pallas kernels  28.6 us (37%)
  starting transfers between devices  6.8 us (9%)
  waiting for transfers between devices  2.81 us (4%)
  local copies, waits for them, and re-layouts  1.07 us (1%)
    all_to_all x1, blocking collectives, local(): strips = lax.all_to_all(ends, 'ta', 0, 0, tiled=True)  36.8 us
    pallas_call x1, Pallas kernels, local(): kernel(first_a_kernel, (out(early, NZ), out(early, NZ), out(3, CX, MIDDLE...  6.66 us
    pallas_call x1, Pallas kernels, local(): kernel(second_b_kernel, out(4, CX, STRIP, NZ), [VMEM] * 6, [taps] + [padd...  6.01 us
    pallas_call x1, Pallas kernels, local(): kernel(second_a_kernel, out(4, CX, STRIP, NZ), [VMEM] * 4, [taps] + [padd...  5.99 us
    pallas_call x1, Pallas kernels, local(): kernel(first_c_kernel, (series, series), [VMEM, VMEM], [taps] + [padded]...  5.84 us
    pallas_call x1, Pallas kernels, local(): kernel(first_b_kernel, (series, series, out(CX, WINDOW, NZ)), [VMEM] * 3,...  4.11 us
    ppermute x2, starting transfers between devices, local(): lax.ppermute(near, 'gx', near_swap)  3.12 us
    ppermute x1, waiting for transfers between devices, local(): even_swap = lax.ppermute(last, 'ta', swaps(SNAKE[0::2], SNAKE[1::2]))  2.79 us
  transfers between devices with their start and end apart: 6, of which 1 were waited for; matrix products, arithmetic and copies ran while one was open for 0% of the time, Pallas kernels for 16%

profile of v3, /device:TPU:0, one launch (start us, length us, event | category | flops | bytes accessed | tf_op | source)
XLA Modules:
  0.0 76.3 jit_solution(5470854773114085390)
XLA Ops:
  0.0 6.7 %first_iteration_a.1 = (f32[1408,128]{1,0:T(8,128)S(1)}, f32[1408,128]{1,0:T(8,128)S(1)}, f32[3,8,128,128]{3,2,1,0:T(8,128)S(1)}, f32[8,96,128]{2,1,0:T(8,128)S(1)}) custom-call(f32[8,256,128]{2,1,0:T(8,128)} %refs_0_.1, f32[8,256,128]{2,1,0:T(8,128)} %refs_1_.1, f32[8,256,128]{2,1,0:T(8,128)} %refs_2_.1), custom_call_target="tpu_custom_call" | custom-call | bytes 36000 | tf_op jit(solution)/shard_map/first_iteration_a/pallas_call | solution.py:267
  6.7 4.1 %first_iteration_b.1 = (f32[2304,128]{1,0:T(8,128)S(1)}, f32[2304,128]{1,0:T(8,128)S(1)}, f32[8,96,128]{2,1,0:T(8,128)S(1)}) custom-call(f32[3,8,128,128]{3,2,1,0:T(8,128)S(1)} %get-tuple-element.15.refs_0_.refs_1_, f32[1408,128]{1,0:T(8,128)S(1)} %get-tuple-element.16.refs_1_, f32[1408,128]{1,0:T(8,128)S(1)} %get-tuple-element.17.refs_2_), custom_call_target="tpu_custom_call" | custom-call | bytes 10800000 | tf_op jit(solution)/shard_map/first_iteration_b/pallas_call | solution.py:273
  10.8 0.1 collective-permute-start
  10.9 0.7 collective-permute-start.1
  11.6 5.8 %first_iteration_c.1 = (f32[2304,128]{1,0:T(8,128)S(1)}, f32[2304,128]{1,0:T(8,128)S(1)}) custom-call(f32[8,96,128]{2,1,0:T(8,128)S(1)} %get-tuple-element.20.refs_0_, f32[3,8,128,128]{3,2,1,0:T(8,128)S(1)} %get-tuple-element.15.refs_0_.refs_1_, f32[2304,128]{1,0:T(8,128)S(1)} %get-tuple-element.18.refs_2_, f32[2304,128]{1,0:T(8,128)S(1)} %get-tuple-element.19.refs_3_), custom_call_target="tpu_custom_call" | custom-call | bytes 10800000 | tf_op jit(solution)/shard_map/first_iteration_c/pallas_call | solution.py:277
  17.5 3.0 %collective-permute-start.2 = (f32[2304,128]{1,0:T(8,128)S(1)}, f32[2304,128]{1,0:T(8,128)S(1)}, u32[]{:S(2)}, u32[]{:S(2)}) collective-permute-start(f32[2304,128]{1,0:T(8,128)S(1)} %get-tuple-element.21.refs_4_), channel_id=1, source_target_pairs={{0,8},{16,24},{32,40},{48,56},{64,72},{80,88},{96,104},{112,120},{... | collective-permute-start | bytes 3538952 | tf_op jit(solution)/shard_map/ppermute | solution.py:281
  20.5 0.7 collective-permute-start.3
  21.2 0.0 collective-permute-done.refs_2_
  21.2 0.0 collective-permute-done.1.refs_3_
  21.3 6.0 %second_iteration_a.1 = f32[4,8,32,128]{3,2,1,0:T(8,128)S(1)} custom-call(f32[8,96,128]{2,1,0:T(8,128)S(1)} %get-tuple-element.14.refs_0_, f32[3,8,128,128]{3,2,1,0:T(8,128)S(1)} %get-tuple-element.15.refs_0_.refs_1_, f32[2304,128]{1,0:T(8,128)S(1)} %collective-permute-done.refs_2_, f32[2304,128]{1,0:T(8,128)S(1)} %collective-permute-done.1.refs_3_, ...), custom_call_target="tpu_custom_call" | custom-call | bytes 43200000 | tf_op jit(solution)/shard_map/second_iteration_a/pallas_call | solution.py:284
  27.3 1.6 %collective-permute-start.4 = (f32[8,32,128]{2,1,0:T(8,128)S(1)}, f32[8,32,128]{2,1,0:T(8,128)S(1)}, u32[]{:S(2)}, u32[]{:S(2)}) collective-permute-start(f32[8,32,128]{2,1,0:T(8,128)S(1)} %slice_bitcast_fusion.8.refs_4_), channel_id=1, source_target_pairs={{0,1},{2,3},{7,6},{5,4},{1,0},{3,2},{6,7},{4,5},{8,9},{10,11},{15,... | collective-permute-start | bytes 393224 | tf_op jit(solution)/shard_map/ppermute | solution.py:288
  28.8 0.7 collective-permute-start.5
  29.5 0.0 collective-permute-done.2.refs_1_
  29.5 0.0 collective-permute-done.3.refs_2_
  29.5 2.8 %collective-permute-done.4.refs_3_ = f32[8,32,128]{2,1,0:T(8,128)S(1)} collective-permute-done((f32[8,32,128]{2,1,0:T(8,128)S(1)}, f32[8,32,128]{2,1,0:T(8,128)S(1)}, u32[]{:S(2)}, u32[]{:S(2)}) %collective-permute-start.4) | collective-permute-done | bytes 131104 | tf_op jit(solution)/shard_map/ppermute | solution.py:288
  32.3 0.0 collective-permute-done.5.refs_5_
  32.3 6.0 %second_iteration_b.1 = f32[4,8,32,128]{3,2,1,0:T(8,128)S(1)} custom-call(f32[3,8,128,128]{3,2,1,0:T(8,128)S(1)} %get-tuple-element.15.refs_0_.refs_1_, f32[2304,128]{1,0:T(8,128)S(1)} %collective-permute-done.2.refs_1_, f32[2304,128]{1,0:T(8,128)S(1)} %collective-permute-done.3.refs_2_, f32[8,32,128]{2,1,0:T(8,128)S(1)} %collective-permute-done.4.refs_3_, ...), custom_call_target="tpu_custom_call" | custom-call | bytes 10800000 | tf_op jit(solution)/shard_map/second_iteration_b/pallas_call | solution.py:290
  38.3 0.1 pad_maximum_fusion
  38.4 36.8 %all_to_all.5 = f32[8,8,32,128]{3,2,1,0:T(8,128)S(1)} all-to-all(f32[8,8,32,128]{3,2,1,0:T(8,128)S(1)} %pad_maximum_fusion), channel_id=1, replica_groups=mesh['gx'=16,'ta'=8] {'ta'}, dimensions={0} | all-to-all | bytes 2097152 | tf_op jit(solution)/shard_map/all_to_all | solution.py:294
  75.3 0.0 copy-start
  75.3 1.0 %copy-done = f32[8,256,128]{2,1,0:T(8,128)} copy-done((f32[8,256,128]{2,1,0:T(8,128)}, f32[8,256,128]{2,1,0:T(8,128)S(1)}, u32[]{:S(2)}) %copy-start) | copy-done | bytes 1048600
  (9 shorter events, 0.1 us)
Async XLA Ops:
  10.8 10.5 %collective-permute-start = (f32[2304,128]{1,0:T(8,128)S(1)}, f32[2304,128]{1,0:T(8,128)S(1)}, u32[]{:S(2)}, u32[]{:S(2)}) collective-permute-start(f32[2304,128]{1,0:T(8,128)S(1)} %get-tuple-element.18.refs_2_), channel_id=1, source_target_pairs={{0,8},{16,24},{32,40},{48,56},{64,72},{80,88},{96,104},{112,120},{... | collective-permute-start | bytes 3538952 | tf_op jit(solution)/shard_map/ppermute | solution.py:281
  10.9 10.4 %collective-permute-start.1 = (f32[2304,128]{1,0:T(8,128)S(1)}, f32[2304,128]{1,0:T(8,128)S(1)}, u32[]{:S(2)}, u32[]{:S(2)}) collective-permute-start(f32[2304,128]{1,0:T(8,128)S(1)} %get-tuple-element.19.refs_3_), channel_id=1, source_target_pairs={{8,16},{24,32},{40,48},{56,64},{72,80},{88,96},{104,112},{16,8},{3... | collective-permute-start | bytes 3538952 | tf_op jit(solution)/shard_map/ppermute | solution.py:281
  17.5 12.0 %collective-permute-start.2 = (f32[2304,128]{1,0:T(8,128)S(1)}, f32[2304,128]{1,0:T(8,128)S(1)}, u32[]{:S(2)}, u32[]{:S(2)}) collective-permute-start(f32[2304,128]{1,0:T(8,128)S(1)} %get-tuple-element.21.refs_4_), channel_id=1, source_target_pairs={{0,8},{16,24},{32,40},{48,56},{64,72},{80,88},{96,104},{112,120},{... | collective-permute-start | bytes 3538952 | tf_op jit(solution)/shard_map/ppermute | solution.py:281
  20.5 9.0 %collective-permute-start.3 = (f32[2304,128]{1,0:T(8,128)S(1)}, f32[2304,128]{1,0:T(8,128)S(1)}, u32[]{:S(2)}, u32[]{:S(2)}) collective-permute-start(f32[2304,128]{1,0:T(8,128)S(1)} %get-tuple-element.22.refs_5_), channel_id=1, source_target_pairs={{8,16},{24,32},{40,48},{56,64},{72,80},{88,96},{104,112},{16,8},{3... | collective-permute-start | bytes 3538952 | tf_op jit(solution)/shard_map/ppermute | solution.py:281
  27.3 5.0 %collective-permute-start.4 = (f32[8,32,128]{2,1,0:T(8,128)S(1)}, f32[8,32,128]{2,1,0:T(8,128)S(1)}, u32[]{:S(2)}, u32[]{:S(2)}) collective-permute-start(f32[8,32,128]{2,1,0:T(8,128)S(1)} %slice_bitcast_fusion.8.refs_4_), channel_id=1, source_target_pairs={{0,1},{2,3},{7,6},{5,4},{1,0},{3,2},{6,7},{4,5},{8,9},{10,11},{15,... | collective-permute-start | bytes 393224 | tf_op jit(solution)/shard_map/ppermute | solution.py:288
  28.8 3.5 %collective-permute-start.5 = (f32[8,32,128]{2,1,0:T(8,128)S(1)}, f32[8,32,128]{2,1,0:T(8,128)S(1)}, u32[]{:S(2)}, u32[]{:S(2)}) collective-permute-start(f32[8,32,128]{2,1,0:T(8,128)S(1)} %slice_bitcast_fusion.8.refs_4_), channel_id=1, source_target_pairs={{1,2},{3,7},{6,5},{2,1},{7,3},{5,6},{9,10},{11,15},{14,13},{10,9},... | collective-permute-start | bytes 393224 | tf_op jit(solution)/shard_map/ppermute | solution.py:289
  75.3 1.0 %copy-start = (f32[8,256,128]{2,1,0:T(8,128)}, f32[8,256,128]{2,1,0:T(8,128)S(1)}, u32[]{:S(2)}) copy-start(f32[8,256,128]{2,1,0:T(8,128)S(1)} %fusion) | copy-start | bytes 3145732

commit v4 on v3

--- a/solution.py
+++ b/solution.py
@@ -10,11 +10,10 @@
 STRIP = 32
 HALO = 32
 WINDOW = STRIP + 2 * HALO
-WIDE = STRIP + 4 * HALO
 PHASE = 32
 STEPS = 8
 PAD = 8
-MIDDLE = WIDE - 32
+SERIES = STEPS * sum(range(WINDOW, STRIP, -16))
 GROUP = 4
 SNAKE = (0, 1, 2, 3, 7, 6, 5, 4)
 BY_MATRIX = 4
@@ -38,6 +37,7 @@
     slab = lax.axis_index("gx")
     slabs = lax.axis_size("gx")
     strip = jnp.where(interval < 4, interval, 11 - interval)
+    strip = jnp.where(slab < slabs // 2, strip, 7 - strip)
     edges = jnp.where(slab > 0, 0.6, 0.0), jnp.where(slab < slabs - 1, 0.6, 0.0)
     return strip, lax.rem(slab, 2) == 1, edges
 
@@ -89,8 +89,8 @@
     return c[CX - 2] - 0.6 * c[CX - 1], c[1] - 0.6 * c[0]
 
 
-def series_rows(k, step, t, first=0):
-    base = STEPS * sum(WINDOW - 16 * before for before in range(first, k))
+def series_rows(k, step, t):
+    base = STEPS * sum(WINDOW - 16 * before for before in range(k))
     return pl.ds(pl.multiple_of(base + step * (WINDOW - 16 * k) + 8 * (t - k), 8), 8)
 
 
@@ -126,71 +126,57 @@
         yield k
 
 
-def first_iteration(m, q, near_out, far_out, taps, ua, ub, odd, edges, intervals, margin):
+def first_iteration(m, q, near_out, far_out, taps, ua, ub, odd, edges):
     t_matrix = z_matrix(taps)
-    begin = intervals[0]
 
     def step(k, at, n):
         def ghosts(t, c):
-            t = t - margin
-            if k <= t < WINDOW // 8 - k:
-                up, down = traces(c)
-                rows = series_rows(k, at, t, begin)
-                near_out[rows, :] = jnp.where(odd, down, up)
-                far_out[rows, :] = jnp.where(odd, up, down)
+            up, down = traces(c)
+            rows = series_rows(k, at, t)
+            near_out[rows, :] = jnp.where(odd, down, up)
+            far_out[rows, :] = jnp.where(odd, up, down)
             return None, None
 
         src, dst = ((ua, ub), (ub, ua))[n]
-        tiles = m.shape[1] // 8
-        advance(src, dst, m, q, ghosts, edges, range(k - begin, tiles - k + begin), t_matrix)
-
-    for _ in phase(step, intervals):
+        advance(src, dst, m, q, ghosts, edges, range(k, WINDOW // 8 - k), t_matrix)
+
+    for _ in phase(step):
         pass
 
 
-def first_a_kernel(u, r, s, near_out, far_out, kept, start, taps, ubuf, rbuf, sbuf, ua, ub, m, q, sems):
+def first_a_kernel(u, r, s, near_out, far_out, start, m, q, last, taps, ubuf, rbuf, sbuf, ua, ub, sems):
     strip, odd, edges = position()
 
     def put(rows, parts):
-        ua[:, PAD + rows.start : PAD + rows.stop, :], m[:, rows, :], q[:, rows, :] = parts
-
-    clear_pads((ua, ub), WIDE)
-    load_window(u, r, s, ubuf, rbuf, sbuf, sems, strip, WIDE, put)
-    start[...] = ua[:, PAD + HALO : PAD + HALO + WINDOW, :]
-    first_iteration(m, q, near_out, far_out, taps, ua, ub, odd, edges, (0, 1), 4)
-    kept[0] = ua[:, PAD + 16 : PAD + 16 + MIDDLE, :]
-    kept[1] = m[:, 16 : 16 + MIDDLE, :]
-    kept[2] = q[:, 16 : 16 + MIDDLE, :]
-
-
-def first_b_kernel(kept, near_in, far_in, near_out, far_out, last, taps, ua, ub):
-    _, odd, edges = position()
-    clear_pads((ua, ub), MIDDLE)
-    ua[:, PAD : PAD + MIDDLE, :] = kept[0]
-    before = near_in.shape[0]
-    near_out[:before, :] = near_in[...]
-    far_out[:before, :] = far_in[...]
-    rest = pl.ds(before, near_out.shape[0] - before)
-    first_iteration(
-        kept.at[1], kept.at[2], near_out.at[rest, :], far_out.at[rest, :], taps, ua, ub, odd, edges, (2, 3), 2
-    )
-    last[...] = ua[:, PAD + 16 : PAD + 16 + WINDOW, :]
-
-
-def inner(kept):
-    return [kept.at[n, :, pl.ds(16, WINDOW), :] for n in (1, 2)]
-
-
-def first_c_kernel(u, kept, near_out, far_out, taps, ua, ub):
-    _, odd, edges = position()
-    clear_pads((ua, ub), WINDOW)
-    ua[:, PAD : PAD + WINDOW, :] = u[...]
-    first_iteration(*inner(kept), near_out, far_out, taps, ua, ub, odd, edges, range(4), 0)
-
-
-def second_iteration(kept, near, far, ends, taps, ua, ub, odd, edges):
+        start[:, rows, :], m[:, rows, :], q[:, rows, :] = parts
+        ua[:, PAD + rows.start : PAD + rows.stop, :] = parts[0]
+
+    clear_pads((ua, ub), WINDOW)
+    load_window(u, r, s, ubuf, rbuf, sbuf, sems, strip, WINDOW, put)
+    first_iteration(m, q, near_out, far_out, taps, ua, ub, odd, edges)
+    last[...] = ua[:, PAD + HALO : PAD + HALO + STRIP, :]
+
+
+def join(strip, even_swap, mid, odd_swap, ua):
+    odd_strip = lax.rem(strip, 2) == 1
+
+    def put(left, right):
+        for at, part in enumerate((left, mid, right)):
+            ua[:, PAD + at * STRIP : PAD + (at + 1) * STRIP, :] = part[...]
+
+    pl.when(odd_strip)(lambda: put(even_swap, odd_swap))
+    pl.when(jnp.logical_not(odd_strip))(lambda: put(odd_swap, even_swap))
+
+
+def first_b_kernel(m, q, even_swap, mid, odd_swap, near_out, far_out, taps, ua, ub):
+    strip, odd, edges = position()
+    clear_pads((ua, ub), WINDOW)
+    join(strip, even_swap, mid, odd_swap, ua)
+    first_iteration(m, q, near_out, far_out, taps, ua, ub, odd, edges)
+
+
+def second_iteration(m, q, near, far, ends, taps, ua, ub, odd, edges):
     t_matrix = z_matrix(taps)
-    m, q = inner(kept)
 
     def step(k, at, n):
         def ghosts(t, c):
@@ -205,25 +191,25 @@
         ends[k] = ua[:, PAD + HALO : PAD + HALO + STRIP, :]
 
 
-def second_a_kernel(start, kept, near, far, ends, taps, ua, ub):
+def second_a_kernel(start, m, q, near, far, ends, taps, ua, ub):
     _, odd, edges = position()
     clear_pads((ua, ub), WINDOW)
     ua[:, PAD : PAD + WINDOW, :] = start[...]
-    second_iteration(kept, near, far, ends, taps, ua, ub, odd, edges)
-
-
-def second_b_kernel(kept, near, far, even_swap, mid, odd_swap, ends, taps, ua, ub):
+    second_iteration(m, q, near, far, ends, taps, ua, ub, odd, edges)
+
+
+def second_b_kernel(m, q, near, far, even_swap, mid, odd_swap, ends, taps, ua, ub):
     strip, odd, edges = position()
     clear_pads((ua, ub), WINDOW)
-    odd_strip = lax.rem(strip, 2) == 1
-
-    def put(left, right):
-        for at, part in enumerate((left, mid, right)):
-            ua[:, PAD + at * STRIP : PAD + (at + 1) * STRIP, :] = part[...]
-
-    pl.when(odd_strip)(lambda: put(even_swap, odd_swap))
-    pl.when(jnp.logical_not(odd_strip))(lambda: put(odd_swap, even_swap))
-    second_iteration(kept, near, far, ends, taps, ua, ub, odd, edges)
+    join(strip, even_swap, mid, odd_swap, ua)
+    second_iteration(m, q, near, far, ends, taps, ua, ub, odd, edges)
+
+
+def far_partners(slabs):
+    for low in range(1, slabs - 1, 2):
+        flip = 4 if low + 1 == slabs // 2 else 0
+        for at in range(8):
+            yield low * 8 + at, (low + 1) * 8 + (at ^ flip)
 
 
 def swaps(some, others):
@@ -253,46 +239,45 @@
             in_specs=ins + [ANY] * after,
             out_specs=jax.tree.map(lambda _: VMEM, outs),
             scratch_shapes=scratch,
-            compiler_params=pltpu.CompilerParams(vmem_limit_bytes=40 << 20),
+            compiler_params=pltpu.CompilerParams(vmem_limit_bytes=16 << 20),
             cost_estimate=pl.CostEstimate(flops=0, transcendentals=0, bytes_accessed=int(micros * 3.6e6)),
             name=name,
         )
 
-    far_swap = swaps(range(1, slabs - 1, 2), range(2, slabs, 2))
-    near_swap = swaps(range(0, slabs, 2), range(1, slabs, 2))
-    early, late = (STEPS * (2 * WINDOW - 16 - 64 * n) for n in range(2))
+    far_pairs = swaps(*zip(*far_partners(slabs)))
+    near_pairs = swaps(range(0, slabs, 2), range(1, slabs, 2))
+    even_pairs = swaps(SNAKE[0::2], SNAKE[1::2])
+    odd_pairs = swaps(SNAKE[1:-1:2], SNAKE[2::2])
+    series = out(SERIES, NZ)
+    window = out(CX, WINDOW, NZ)
+    work = [taps] + [padded] * 2
+
+    def send(near, far):
+        return lax.ppermute(near, "gx", near_pairs), lax.ppermute(far, ("gx", "ta"), far_pairs)
+
+    def halo(strip):
+        return lax.ppermute(strip, "ta", even_pairs), strip, lax.ppermute(strip, "ta", odd_pairs)
 
     u, r, s = (pltpu.with_memory_space_constraint(a, pltpu.HBM) for a in (u, r, s))
-    wide_work = [buffer(WIDE + 4 * HALO)] * 3 + [buffer(WIDE + 2 * PAD)] * 2 + [buffer(WIDE)] * 2
-    near_a, far_a, kept, start = kernel(
-        first_a_kernel,
-        (out(early, NZ), out(early, NZ), out(3, CX, MIDDLE, NZ), out(CX, WINDOW, NZ)),
-        [HBM] * 3, [taps] + wide_work + [pltpu.SemaphoreType.DMA((3,))], "first_iteration_a", 0.01,
+    near_a, far_a, start, m, q, last = kernel(
+        first_a_kernel, (series, series, window, window, window, out(CX, STRIP, NZ)), [HBM] * 3,
+        [taps] + [buffer(WINDOW + 2 * HALO)] * 3 + [padded] * 2 + [pltpu.SemaphoreType.DMA((3,))], "first_iteration_a", 6.0,
     )(u, r, s)
-    series = out(early + late, NZ)
-    near_b, far_b, state = kernel(
-        first_b_kernel, (series, series, out(CX, WINDOW, NZ)),
-        [VMEM] * 3, [taps] + [buffer(MIDDLE + 2 * PAD)] * 2, "first_iteration_b", 3.0,
-    )(kept, near_a, far_a)
-    near_c, far_c = kernel(
-        first_c_kernel, (series, series), [VMEM, VMEM], [taps] + [padded] * 2, "first_iteration_c", 3.0, 2
-    )(state, kept, near_b, far_b)
-    theirs = [
-        (lax.ppermute(near, "gx", near_swap), lax.ppermute(far, "gx", far_swap))
-        for near, far in ((near_b, far_b), (near_c, far_c))
-    ]
+    theirs_a = send(near_a, far_a)
+    near_b, far_b = kernel(
+        first_b_kernel, (series, series), [VMEM] * 5, work, "first_iteration_b", 3.0, 2
+    )(m, q, *halo(last), near_a, far_a)
+    theirs_b = send(near_b, far_b)
     ends_a = kernel(
-        second_a_kernel, out(4, CX, STRIP, NZ), [VMEM] * 4, [taps] + [padded] * 2, "second_iteration_a", 12.0, 2
-    )(start, kept, *theirs[0], near_c, far_c)
-    last = ends_a[3]
-    even_swap = lax.ppermute(last, "ta", swaps(SNAKE[0::2], SNAKE[1::2]))
-    odd_swap = lax.ppermute(last, "ta", swaps(SNAKE[1:-1:2], SNAKE[2::2]))
+        second_a_kernel, out(4, CX, STRIP, NZ), [VMEM] * 5, work, "second_iteration_a", 12.0, 2
+    )(start, m, q, *theirs_a, near_b, far_b)
     ends_b = kernel(
-        second_b_kernel, out(4, CX, STRIP, NZ), [VMEM] * 6, [taps] + [padded] * 2, "second_iteration_b", 3.0
-    )(kept, *theirs[1], even_swap, last, odd_swap)
+        second_b_kernel, out(4, CX, STRIP, NZ), [VMEM] * 7, work, "second_iteration_b", 3.0
+    )(m, q, *theirs_b, *halo(ends_a[3]))
     ends = jnp.concatenate([ends_a, ends_b], 0)
     strips = lax.all_to_all(ends, "ta", 0, 0, tiled=True)
-    return jnp.concatenate([strips[i] for i in SNAKE], 1)[None]
+    lower = lax.axis_index("gx") < slabs // 2
+    return jnp.concatenate([jnp.where(lower, strips[i], strips[i ^ 4]) for i in SNAKE], 1)[None]
 
 
 def solution(mesh):

time: 76.5 us -> 73.9 us (0.966)
  the two profiles are of different devices: /device:TPU:0 before, /device:TPU:24 now
where the time goes in v4:
time: 73.9 us; the launch traced here: 73.3 us
  Pallas kernels  25.1 us (34%)
  waiting for transfers between devices  24.3 us (33%)
  starting transfers between devices  21.6 us (29%)
  other arithmetic  1.2 us (2%)
  local copies, waits for them, and re-layouts  0.98 us (1%)
    all_to_all x1, waiting for transfers between devices, local(): strips = lax.all_to_all(ends, 'ta', 0, 0, tiled=True)  16.7 us
    all_to_all x1, starting transfers between devices, local(): strips = lax.all_to_all(ends, 'ta', 0, 0, tiled=True)  7.64 us
    pallas_call x1, Pallas kernels, local(): kernel(first_a_kernel, (series, series, window, window, window, out(CX, S...  7.22 us
    pallas_call x1, Pallas kernels, local(): kernel(second_b_kernel, out(4, CX, STRIP, NZ), [VMEM] * 7, work, 'second_...  5.99 us
    pallas_call x1, Pallas kernels, local(): kernel(second_a_kernel, out(4, CX, STRIP, NZ), [VMEM] * 5, work, 'second_...  5.97 us
    pallas_call x1, Pallas kernels, local(): kernel(first_b_kernel, (series, series), [VMEM] * 5, work, 'first_iterati...  5.88 us
    ppermute x2, starting transfers between devices, halo(): lax.ppermute(strip, 'ta', even_pairs)  5.68 us
    ppermute x2, waiting for transfers between devices, halo(): lax.ppermute(strip, 'ta', even_pairs)  5.1 us
  transfers between devices with their start and end apart: 9, of which 4 were waited for; matrix products, arithmetic and copies ran while one was open for 0% of the time, Pallas kernels for 16%

profile of v4, /device:TPU:24, one launch (start us, length us, event | category | flops | bytes accessed | tf_op | source)
XLA Modules:
  0.0 73.3 jit_solution(1886552699261592614)
XLA Ops:
  0.0 7.2 %first_iteration_a.1 = (f32[2304,128]{1,0:T(8,128)S(1)}, f32[2304,128]{1,0:T(8,128)S(1)}, f32[8,96,128]{2,1,0:T(8,128)S(1)}, f32[8,96,128]{2,1,0:T(8,128)S(1)}, ...) custom-call(f32[8,256,128]{2,1,0:T(8,128)} %refs_0_.1, f32[8,256,128]{2,1,0:T(8,128)} %refs_1_.1, f32[8,256,128]{2,1,0:T(8,128)} %refs_2_.1), custom_call_target="tpu_custom_call" | custom-call | bytes 21600000 | tf_op jit(solution)/shard_map/first_iteration_a/pallas_call | solution.py:262
  7.2 0.1 collective-permute-start
  7.3 2.7 %collective-permute-start.1 = (f32[2304,128]{1,0:T(8,128)S(1)}, f32[2304,128]{1,0:T(8,128)S(1)}, u32[]{:S(2)}, u32[]{:S(2)}) collective-permute-start(f32[2304,128]{1,0:T(8,128)S(1)} %get-tuple-element.17.refs_6_), channel_id=1, source_target_pairs={{8,16},{9,17},{10,18},{11,19},{12,20},{13,21},{14,22},{15,23},{24,... | collective-permute-start | bytes 3538952 | tf_op jit(solution)/shard_map/ppermute | solution.py:256
  10.1 1.6 %collective-permute-start.2 = (f32[8,32,128]{2,1,0:T(8,128)S(1)}, f32[8,32,128]{2,1,0:T(8,128)S(1)}, u32[]{:S(2)}, u32[]{:S(2)}) collective-permute-start(f32[8,32,128]{2,1,0:T(8,128)S(1)} %get-tuple-element.18.refs_3_), channel_id=1, source_target_pairs={{0,1},{2,3},{7,6},{5,4},{1,0},{3,2},{6,7},{4,5},{8,9},{10,11},{15,... | collective-permute-start | bytes 393224 | tf_op jit(solution)/shard_map/ppermute | solution.py:259
  11.6 0.7 collective-permute-start.3
  12.3 2.8 %collective-permute-done.2.refs_2_ = f32[8,32,128]{2,1,0:T(8,128)S(1)} collective-permute-done((f32[8,32,128]{2,1,0:T(8,128)S(1)}, f32[8,32,128]{2,1,0:T(8,128)S(1)}, u32[]{:S(2)}, u32[]{:S(2)}) %collective-permute-start.2) | collective-permute-done | bytes 131104 | tf_op jit(solution)/shard_map/ppermute | solution.py:259
  15.1 0.0 collective-permute-done.3.refs_4_
  15.1 5.9 %first_iteration_b.1 = (f32[2304,128]{1,0:T(8,128)S(1)}, f32[2304,128]{1,0:T(8,128)S(1)}) custom-call(f32[8,96,128]{2,1,0:T(8,128)S(1)} %get-tuple-element.14.refs_0_.refs_1_, f32[8,96,128]{2,1,0:T(8,128)S(1)} %get-tuple-element.15.refs_1_.refs_2_, f32[8,32,128]{2,1,0:T(8,128)S(1)} %collective-permute-done.2.refs_2_, ...), custom_call_target="tpu_custom_call" | custom-call | bytes 10800000 | tf_op jit(solution)/shard_map/first_iteration_b/pallas_call | solution.py:267
  21.0 2.2 %collective-permute-start.4 = (f32[2304,128]{1,0:T(8,128)S(1)}, f32[2304,128]{1,0:T(8,128)S(1)}, u32[]{:S(2)}, u32[]{:S(2)}) collective-permute-start(f32[2304,128]{1,0:T(8,128)S(1)} %get-tuple-element.19.refs_5_), channel_id=1, source_target_pairs={{0,8},{16,24},{32,40},{48,56},{64,72},{80,88},{96,104},{112,120},{... | collective-permute-start | bytes 3538952 | tf_op jit(solution)/shard_map/ppermute | solution.py:256
  23.2 1.9 %collective-permute-start.5 = (f32[2304,128]{1,0:T(8,128)S(1)}, f32[2304,128]{1,0:T(8,128)S(1)}, u32[]{:S(2)}, u32[]{:S(2)}) collective-permute-start(f32[2304,128]{1,0:T(8,128)S(1)} %get-tuple-element.20.refs_6_), channel_id=1, source_target_pairs={{8,16},{9,17},{10,18},{11,19},{12,20},{13,21},{14,22},{15,23},{24,... | collective-permute-start | bytes 3538952 | tf_op jit(solution)/shard_map/ppermute | solution.py:256
  25.1 0.0 collective-permute-done.refs_3_
  25.1 0.0 collective-permute-done.1.refs_4_
  25.2 6.0 %second_iteration_a.1 = f32[4,8,32,128]{3,2,1,0:T(8,128)S(1)} custom-call(f32[8,96,128]{2,1,0:T(8,128)S(1)} %get-tuple-element.13.refs_0_, f32[8,96,128]{2,1,0:T(8,128)S(1)} %get-tuple-element.14.refs_0_.refs_1_, f32[8,96,128]{2,1,0:T(8,128)S(1)} %get-tuple-element.15.refs_1_.refs_2_, f32[2304,128]{1,0:T(8,128)S(1)} %collective-permute-done.refs_3_, ...), custom_call_target="tpu_custom_call" | custom-call | bytes 43200000 | tf_op jit(solution)/shard_map/second_iteration_a/pallas_call | solution.py:271
  31.1 4.1 %collective-permute-start.6 = (f32[8,32,128]{2,1,0:T(8,128)S(1)}, f32[8,32,128]{2,1,0:T(8,128)S(1)}, u32[]{:S(2)}, u32[]{:S(2)}) collective-permute-start(f32[8,32,128]{2,1,0:T(8,128)S(1)} %slice_bitcast_fusion.refs_5_), channel_id=1, source_target_pairs={{0,1},{2,3},{7,6},{5,4},{1,0},{3,2},{6,7},{4,5},{8,9},{10,11},{15,... | collective-permute-start | bytes 393224 | tf_op jit(solution)/shard_map/ppermute | solution.py:259
  35.3 0.7 collective-permute-start.7
  35.9 2.3 %collective-permute-done.6.refs_4_ = f32[8,32,128]{2,1,0:T(8,128)S(1)} collective-permute-done((f32[8,32,128]{2,1,0:T(8,128)S(1)}, f32[8,32,128]{2,1,0:T(8,128)S(1)}, u32[]{:S(2)}, u32[]{:S(2)}) %collective-permute-start.6) | collective-permute-done | bytes 131104 | tf_op jit(solution)/shard_map/ppermute | solution.py:259
  38.2 0.0 collective-permute-done.7.refs_6_
  38.2 0.0 collective-permute-done.4.refs_2_
  38.2 2.5 %collective-permute-done.5.refs_3_ = f32[2304,128]{1,0:T(8,128)S(1)} collective-permute-done((f32[2304,128]{1,0:T(8,128)S(1)}, f32[2304,128]{1,0:T(8,128)S(1)}, u32[]{:S(2)}, u32[]{:S(2)}) %collective-permute-start.5) | collective-permute-done | bytes 1179680 | tf_op jit(solution)/shard_map/ppermute | solution.py:256
  40.7 6.0 %second_iteration_b.1 = f32[4,8,32,128]{3,2,1,0:T(8,128)S(1)} custom-call(f32[8,96,128]{2,1,0:T(8,128)S(1)} %get-tuple-element.14.refs_0_.refs_1_, f32[8,96,128]{2,1,0:T(8,128)S(1)} %get-tuple-element.15.refs_1_.refs_2_, f32[2304,128]{1,0:T(8,128)S(1)} %collective-permute-done.4.refs_2_, f32[2304,128]{1,0:T(8,128)S(1)} %collective-permute-done.5.refs_3_, ...), custom_call_target="tpu_custom_call" | custom-call | bytes 10800000 | tf_op jit(solution)/shard_map/second_iteration_b/pallas_call | solution.py:274
  46.7 1.0 %pad_maximum_fusion = f32[8,8,32,128]{3,2,1,0:T(8,128)} fusion(f32[4,8,32,128]{3,2,1,0:T(8,128)S(1)} %second_iteration_b.1, f32[4,8,32,128]{3,2,1,0:T(8,128)S(1)} %second_iteration_a.1), kind=kLoop, calls=%fused_computation | loop fusion | flops 262144 | bytes 2097152 | tf_op jit(solution)/shard_map/concatenate | solution.py:277
  47.8 7.6 %all-to-all-start = ((f32[8,8,32,128]{3,2,1,0:T(8,128)}), f32[8,8,32,128]{3,2,1,0:T(8,128)S(1)}, u32[]{:S(2)}, u32[]{:S(2)}) async-start(f32[8,8,32,128]{3,2,1,0:T(8,128)} %pad_maximum_fusion), calls=%async_computation | async-start | bytes 2097152 | tf_op jit(solution)/shard_map/all_to_all | solution.py:278
  55.4 16.7 %all-to-all-done = f32[8,8,32,128]{3,2,1,0:T(8,128)S(1)} async-done(((f32[8,8,32,128]{3,2,1,0:T(8,128)}), f32[8,8,32,128]{3,2,1,0:T(8,128)S(1)}, u32[]{:S(2)}, u32[]{:S(2)}) %all-to-all-start) | async-done | bytes 1048608 | tf_op jit(solution)/shard_map/all_to_all | solution.py:278
  72.3 0.0 copy-start
  72.3 1.0 %copy-done = f32[8,256,128]{2,1,0:T(8,128)} copy-done((f32[8,256,128]{2,1,0:T(8,128)}, f32[8,256,128]{2,1,0:T(8,128)S(1)}, u32[]{:S(2)}) %copy-start) | copy-done | bytes 1048600
  (9 shorter events, 0.2 us)
Async XLA Ops:
  7.2 17.9 %collective-permute-start = (f32[2304,128]{1,0:T(8,128)S(1)}, f32[2304,128]{1,0:T(8,128)S(1)}, u32[]{:S(2)}, u32[]{:S(2)}) collective-permute-start(f32[2304,128]{1,0:T(8,128)S(1)} %get-tuple-element.16.refs_5_), channel_id=1, source_target_pairs={{0,8},{16,24},{32,40},{48,56},{64,72},{80,88},{96,104},{112,120},{... | collective-permute-start | bytes 3538952 | tf_op jit(solution)/shard_map/ppermute | solution.py:256
  7.3 17.8 %collective-permute-start.1 = (f32[2304,128]{1,0:T(8,128)S(1)}, f32[2304,128]{1,0:T(8,128)S(1)}, u32[]{:S(2)}, u32[]{:S(2)}) collective-permute-start(f32[2304,128]{1,0:T(8,128)S(1)} %get-tuple-element.17.refs_6_), channel_id=1, source_target_pairs={{8,16},{9,17},{10,18},{11,19},{12,20},{13,21},{14,22},{15,23},{24,... | collective-permute-start | bytes 3538952 | tf_op jit(solution)/shard_map/ppermute | solution.py:256
  10.1 5.0 %collective-permute-start.2 = (f32[8,32,128]{2,1,0:T(8,128)S(1)}, f32[8,32,128]{2,1,0:T(8,128)S(1)}, u32[]{:S(2)}, u32[]{:S(2)}) collective-permute-start(f32[8,32,128]{2,1,0:T(8,128)S(1)} %get-tuple-element.18.refs_3_), channel_id=1, source_target_pairs={{0,1},{2,3},{7,6},{5,4},{1,0},{3,2},{6,7},{4,5},{8,9},{10,11},{15,... | collective-permute-start | bytes 393224 | tf_op jit(solution)/shard_map/ppermute | solution.py:259
  11.6 3.5 %collective-permute-start.3 = (f32[8,32,128]{2,1,0:T(8,128)S(1)}, f32[8,32,128]{2,1,0:T(8,128)S(1)}, u32[]{:S(2)}, u32[]{:S(2)}) collective-permute-start(f32[8,32,128]{2,1,0:T(8,128)S(1)} %get-tuple-element.18.refs_3_), channel_id=1, source_target_pairs={{1,2},{3,7},{6,5},{2,1},{7,3},{5,6},{9,10},{11,15},{14,13},{10,9},... | collective-permute-start | bytes 393224 | tf_op jit(solution)/shard_map/ppermute | solution.py:259
  21.0 17.2 %collective-permute-start.4 = (f32[2304,128]{1,0:T(8,128)S(1)}, f32[2304,128]{1,0:T(8,128)S(1)}, u32[]{:S(2)}, u32[]{:S(2)}) collective-permute-start(f32[2304,128]{1,0:T(8,128)S(1)} %get-tuple-element.19.refs_5_), channel_id=1, source_target_pairs={{0,8},{16,24},{32,40},{48,56},{64,72},{80,88},{96,104},{112,120},{... | collective-permute-start | bytes 3538952 | tf_op jit(solution)/shard_map/ppermute | solution.py:256
  23.2 17.5 %collective-permute-start.5 = (f32[2304,128]{1,0:T(8,128)S(1)}, f32[2304,128]{1,0:T(8,128)S(1)}, u32[]{:S(2)}, u32[]{:S(2)}) collective-permute-start(f32[2304,128]{1,0:T(8,128)S(1)} %get-tuple-element.20.refs_6_), channel_id=1, source_target_pairs={{8,16},{9,17},{10,18},{11,19},{12,20},{13,21},{14,22},{15,23},{24,... | collective-permute-start | bytes 3538952 | tf_op jit(solution)/shard_map/ppermute | solution.py:256
  31.1 7.1 %collective-permute-start.6 = (f32[8,32,128]{2,1,0:T(8,128)S(1)}, f32[8,32,128]{2,1,0:T(8,128)S(1)}, u32[]{:S(2)}, u32[]{:S(2)}) collective-permute-start(f32[8,32,128]{2,1,0:T(8,128)S(1)} %slice_bitcast_fusion.refs_5_), channel_id=1, source_target_pairs={{0,1},{2,3},{7,6},{5,4},{1,0},{3,2},{6,7},{4,5},{8,9},{10,11},{15,... | collective-permute-start | bytes 393224 | tf_op jit(solution)/shard_map/ppermute | solution.py:259
  35.3 3.0 %collective-permute-start.7 = (f32[8,32,128]{2,1,0:T(8,128)S(1)}, f32[8,32,128]{2,1,0:T(8,128)S(1)}, u32[]{:S(2)}, u32[]{:S(2)}) collective-permute-start(f32[8,32,128]{2,1,0:T(8,128)S(1)} %slice_bitcast_fusion.refs_5_), channel_id=1, source_target_pairs={{1,2},{3,7},{6,5},{2,1},{7,3},{5,6},{9,10},{11,15},{14,13},{10,9},... | collective-permute-start | bytes 393224 | tf_op jit(solution)/shard_map/ppermute | solution.py:259
  47.8 24.3 %all-to-all-start = ((f32[8,8,32,128]{3,2,1,0:T(8,128)}), f32[8,8,32,128]{3,2,1,0:T(8,128)S(1)}, u32[]{:S(2)}, u32[]{:S(2)}) async-start(f32[8,8,32,128]{3,2,1,0:T(8,128)} %pad_maximum_fusion), calls=%async_computation | async-start | bytes 2097152 | tf_op jit(solution)/shard_map/all_to_all | solution.py:278
  72.3 1.0 %copy-start = (f32[8,256,128]{2,1,0:T(8,128)}, f32[8,256,128]{2,1,0:T(8,128)S(1)}, u32[]{:S(2)}) copy-start(f32[8,256,128]{2,1,0:T(8,128)S(1)} %bitcast_dynamic-update-slice_fusion) | copy-start | bytes 3145732

commit v5 on v4

--- a/solution.py
+++ b/solution.py
@@ -175,7 +175,7 @@
     first_iteration(m, q, near_out, far_out, taps, ua, ub, odd, edges)
 
 
-def second_iteration(m, q, near, far, ends, taps, ua, ub, odd, edges):
+def second_iteration(m, q, near, far, ends, taps, ua, ub, odd, edges, places=range(4)):
     t_matrix = z_matrix(taps)
 
     def step(k, at, n):
@@ -188,7 +188,7 @@
         advance(src, dst, m, q, ghosts, edges, range(k, WINDOW // 8 - k), t_matrix)
 
     for k in phase(step):
-        ends[k] = ua[:, PAD + HALO : PAD + HALO + STRIP, :]
+        ends[places[k]] = ua[:, PAD + HALO : PAD + HALO + STRIP, :]
 
 
 def second_a_kernel(start, m, q, near, far, ends, taps, ua, ub):
@@ -198,11 +198,15 @@
     second_iteration(m, q, near, far, ends, taps, ua, ub, odd, edges)
 
 
-def second_b_kernel(m, q, near, far, even_swap, mid, odd_swap, ends, taps, ua, ub):
+def second_b_kernel(m, q, near, far, even_swap, mid, odd_swap, before, blocks, taps, ua, ub):
     strip, odd, edges = position()
+    lower = lax.axis_index("gx") < lax.axis_size("gx") // 2
     clear_pads((ua, ub), WINDOW)
     join(strip, even_swap, mid, odd_swap, ua)
-    second_iteration(m, q, near, far, ends, taps, ua, ub, odd, edges)
+    for k in range(4):
+        blocks[jnp.where(lower, k, 7 - k)] = before[k]
+    places = [jnp.where(lower, 7 - k, k) for k in range(4)]
+    second_iteration(m, q, near, far, blocks, taps, ua, ub, odd, edges, places)
 
 
 def far_partners(slabs):
@@ -271,13 +275,12 @@
     ends_a = kernel(
         second_a_kernel, out(4, CX, STRIP, NZ), [VMEM] * 5, work, "second_iteration_a", 12.0, 2
     )(start, m, q, *theirs_a, near_b, far_b)
-    ends_b = kernel(
-        second_b_kernel, out(4, CX, STRIP, NZ), [VMEM] * 7, work, "second_iteration_b", 3.0
-    )(m, q, *theirs_b, *halo(ends_a[3]))
-    ends = jnp.concatenate([ends_a, ends_b], 0)
-    strips = lax.all_to_all(ends, "ta", 0, 0, tiled=True)
-    lower = lax.axis_index("gx") < slabs // 2
-    return jnp.concatenate([jnp.where(lower, strips[i], strips[i ^ 4]) for i in SNAKE], 1)[None]
+    blocks = kernel(
+        second_b_kernel, out(8, CX, STRIP, NZ), [VMEM] * 8, work, "second_iteration_b", 3.0
+    )(m, q, *theirs_b, *halo(ends_a[3]), ends_a)
+    groups = [[8 * g + (c if g < slabs // 2 else c ^ 4) for c in SNAKE] for g in range(slabs)]
+    strips = lax.all_to_all(blocks, ("gx", "ta"), 0, 0, axis_index_groups=groups, tiled=True)
+    return strips.transpose(1, 0, 2, 3).reshape(1, CX, -1, NZ)
 
 
 def solution(mesh):

time: 73.9 us -> 72.2 us (0.977)
  the two profiles are of different devices: /device:TPU:24 before, /device:TPU:25 now
where the time goes in v5:
time: 72.2 us; the launch traced here: 72 us
  Pallas kernels  25.1 us (35%)
  blocking collectives  20.7 us (29%)
  starting transfers between devices  16.9 us (23%)
  waiting for transfers between devices  8.2 us (11%)
  local copies, waits for them, and re-layouts  1.07 us (1%)
    all_to_all x1, blocking collectives, local(): lax.all_to_all(blocks, ('gx', 'ta'), 0, 0, axis_index_groups=groups, tile...  20.7 us
    ppermute x2, starting transfers between devices, send(): lax.ppermute(far, ('gx', 'ta'), far_pairs)  10.1 us
    pallas_call x1, Pallas kernels, local(): kernel(first_a_kernel, (series, series, window, window, window, out(CX, S...  7.22 us
    pallas_call x1, Pallas kernels, local(): kernel(second_b_kernel, out(8, CX, STRIP, NZ), [VMEM] * 8, work, 'second_...  6.01 us
    pallas_call x1, Pallas kernels, local(): kernel(second_a_kernel, out(4, CX, STRIP, NZ), [VMEM] * 5, work, 'second_...  5.96 us
    pallas_call x1, Pallas kernels, local(): kernel(first_b_kernel, (series, series), [VMEM] * 5, work, 'first_iterati...  5.88 us
    ppermute x2, starting transfers between devices, halo(): lax.ppermute(strip, 'ta', even_pairs)  4.63 us
    ppermute x2, waiting for transfers between devices, halo(): lax.ppermute(strip, 'ta', even_pairs)  4.23 us
  transfers between devices with their start and end apart: 8, of which 4 were waited for; matrix products, arithmetic and copies ran while one was open for 0% of the time, Pallas kernels for 16%

profile of v5, /device:TPU:25, one launch (start us, length us, event | category | flops | bytes accessed | tf_op | source)
XLA Modules:
  0.0 72.0 jit_solution(961200318080984538)
XLA Ops:
  0.0 7.2 %first_iteration_a.1 = (f32[2304,128]{1,0:T(8,128)S(1)}, f32[2304,128]{1,0:T(8,128)S(1)}, f32[8,96,128]{2,1,0:T(8,128)S(1)}, f32[8,96,128]{2,1,0:T(8,128)S(1)}, ...) custom-call(f32[8,256,128]{2,1,0:T(8,128)} %refs_0_.1, f32[8,256,128]{2,1,0:T(8,128)} %refs_1_.1, f32[8,256,128]{2,1,0:T(8,128)} %refs_2_.1), custom_call_target="tpu_custom_call" | custom-call | bytes 21600000 | tf_op jit(solution)/shard_map/first_iteration_a/pallas_call | solution.py:266
  7.2 0.8 %collective-permute-start.4 = (f32[2304,128]{1,0:T(8,128)S(1)}, f32[2304,128]{1,0:T(8,128)S(1)}, u32[]{:S(2)}, u32[]{:S(2)}) collective-permute-start(f32[2304,128]{1,0:T(8,128)S(1)} %get-tuple-element.16.refs_5_), channel_id=1, source_target_pairs={{0,8},{16,24},{32,40},{48,56},{64,72},{80,88},{96,104},{112,120},{... | collective-permute-start | bytes 3538952 | tf_op jit(solution)/shard_map/ppermute | solution.py:260
  8.0 5.2 %collective-permute-start.5 = (f32[2304,128]{1,0:T(8,128)S(1)}, f32[2304,128]{1,0:T(8,128)S(1)}, u32[]{:S(2)}, u32[]{:S(2)}) collective-permute-start(f32[2304,128]{1,0:T(8,128)S(1)} %get-tuple-element.17.refs_6_), channel_id=1, source_target_pairs={{8,16},{9,17},{10,18},{11,19},{12,20},{13,21},{14,22},{15,23},{24,... | collective-permute-start | bytes 3538952 | tf_op jit(solution)/shard_map/ppermute | solution.py:260
  13.2 1.3 %collective-permute-start = (f32[8,32,128]{2,1,0:T(8,128)S(1)}, f32[8,32,128]{2,1,0:T(8,128)S(1)}, u32[]{:S(2)}, u32[]{:S(2)}) collective-permute-start(f32[8,32,128]{2,1,0:T(8,128)S(1)} %get-tuple-element.15.refs_3_), channel_id=1, source_target_pairs={{0,1},{2,3},{7,6},{5,4},{1,0},{3,2},{6,7},{4,5},{8,9},{10,11},{15,... | collective-permute-start | bytes 393224 | tf_op jit(solution)/shard_map/ppermute | solution.py:263
  14.5 0.7 collective-permute-start.1
  15.2 2.2 %collective-permute-done.refs_2_ = f32[8,32,128]{2,1,0:T(8,128)S(1)} collective-permute-done((f32[8,32,128]{2,1,0:T(8,128)S(1)}, f32[8,32,128]{2,1,0:T(8,128)S(1)}, u32[]{:S(2)}, u32[]{:S(2)}) %collective-permute-start) | collective-permute-done | bytes 131104 | tf_op jit(solution)/shard_map/ppermute | solution.py:263
  17.4 0.0 collective-permute-done.1.refs_4_
  17.4 5.9 %first_iteration_b.1 = (f32[2304,128]{1,0:T(8,128)S(1)}, f32[2304,128]{1,0:T(8,128)S(1)}) custom-call(f32[8,96,128]{2,1,0:T(8,128)S(1)} %get-tuple-element.13.refs_0_.refs_1_, f32[8,96,128]{2,1,0:T(8,128)S(1)} %get-tuple-element.14.refs_1_.refs_2_, f32[8,32,128]{2,1,0:T(8,128)S(1)} %collective-permute-done.refs_2_, ...), custom_call_target="tpu_custom_call" | custom-call | bytes 10800000 | tf_op jit(solution)/shard_map/first_iteration_b/pallas_call | solution.py:271
  23.3 0.1 collective-permute-start.2
  23.4 4.9 %collective-permute-start.3 = (f32[2304,128]{1,0:T(8,128)S(1)}, f32[2304,128]{1,0:T(8,128)S(1)}, u32[]{:S(2)}, u32[]{:S(2)}) collective-permute-start(f32[2304,128]{1,0:T(8,128)S(1)} %get-tuple-element.19.refs_6_), channel_id=1, source_target_pairs={{8,16},{9,17},{10,18},{11,19},{12,20},{13,21},{14,22},{15,23},{24,... | collective-permute-start | bytes 3538952 | tf_op jit(solution)/shard_map/ppermute | solution.py:260
  28.3 0.0 collective-permute-done.4.refs_3_
  28.3 0.5 collective-permute-done.5.refs_4_
  28.8 6.0 %second_iteration_a.1.refs_7_ = f32[4,8,32,128]{3,2,1,0:T(8,128)S(1)} custom-call(f32[8,96,128]{2,1,0:T(8,128)S(1)} %get-tuple-element.20.refs_0_, f32[8,96,128]{2,1,0:T(8,128)S(1)} %get-tuple-element.13.refs_0_.refs_1_, f32[8,96,128]{2,1,0:T(8,128)S(1)} %get-tuple-element.14.refs_1_.refs_2_, f32[2304,128]{1,0:T(8,128)S(1)} %collective-permute-done.4.refs_3_, ...), custom_call_target="tpu_custom_call" | custom-call | bytes 43200000 | tf_op jit(solution)/shard_map/second_iteration_a/pallas_call | solution.py:275
  34.8 3.3 %collective-permute-start.6 = (f32[8,32,128]{2,1,0:T(8,128)S(1)}, f32[8,32,128]{2,1,0:T(8,128)S(1)}, u32[]{:S(2)}, u32[]{:S(2)}) collective-permute-start(f32[8,32,128]{2,1,0:T(8,128)S(1)} %slice_bitcast_fusion.refs_5_), channel_id=1, source_target_pairs={{0,1},{2,3},{7,6},{5,4},{1,0},{3,2},{6,7},{4,5},{8,9},{10,11},{15,... | collective-permute-start | bytes 393224 | tf_op jit(solution)/shard_map/ppermute | solution.py:263
  38.1 0.7 collective-permute-start.7
  38.8 2.0 %collective-permute-done.6.refs_4_ = f32[8,32,128]{2,1,0:T(8,128)S(1)} collective-permute-done((f32[8,32,128]{2,1,0:T(8,128)S(1)}, f32[8,32,128]{2,1,0:T(8,128)S(1)}, u32[]{:S(2)}, u32[]{:S(2)}) %collective-permute-start.6) | collective-permute-done | bytes 131104 | tf_op jit(solution)/shard_map/ppermute | solution.py:263
  40.8 0.0 collective-permute-done.7.refs_6_
  40.8 0.0 collective-permute-done.2.refs_2_
  40.8 3.4 %collective-permute-done.3.refs_3_ = f32[2304,128]{1,0:T(8,128)S(1)} collective-permute-done((f32[2304,128]{1,0:T(8,128)S(1)}, f32[2304,128]{1,0:T(8,128)S(1)}, u32[]{:S(2)}, u32[]{:S(2)}) %collective-permute-start.3) | collective-permute-done | bytes 1179680 | tf_op jit(solution)/shard_map/ppermute | solution.py:260
  44.2 6.0 %second_iteration_b.1 = f32[8,8,32,128]{3,2,1,0:T(8,128)S(1)} custom-call(f32[8,96,128]{2,1,0:T(8,128)S(1)} %get-tuple-element.13.refs_0_.refs_1_, f32[8,96,128]{2,1,0:T(8,128)S(1)} %get-tuple-element.14.refs_1_.refs_2_, f32[2304,128]{1,0:T(8,128)S(1)} %collective-permute-done.2.refs_2_, f32[2304,128]{1,0:T(8,128)S(1)} %collective-permute-done.3.refs_3_, ...), custom_call_target="tpu_custom_call" | custom-call | bytes 10800000 | tf_op jit(solution)/shard_map/second_iteration_b/pallas_call | solution.py:278
  50.2 20.7 %all_to_all.5 = f32[8,8,32,128]{3,2,1,0:T(8,128)S(1)} all-to-all(f32[8,8,32,128]{3,2,1,0:T(8,128)S(1)} %second_iteration_b.1), channel_id=1, replica_groups={{0,1,2,3,7,6,5,4},{8,9,10,11,15,14,13,12},{16,17,18,19,23,22,21,20},{24..., dimensions={0} | all-to-all | bytes 2097152 | tf_op jit(solution)/shard_map/all_to_all | solution.py:282
  70.9 1.1 %copy.4 = f32[8,8,32,128]{3,2,1,0:T(8,128)} copy(f32[8,8,32,128]{3,2,0,1:T(8,128)S(1)} %bitcast.4) | data formatting | bytes 2097152 | tf_op jit(solution)/shard_map/transpose | solution.py:283
  (1 shorter events, 0.0 us)
Async XLA Ops:
  7.2 21.1 %collective-permute-start.4 = (f32[2304,128]{1,0:T(8,128)S(1)}, f32[2304,128]{1,0:T(8,128)S(1)}, u32[]{:S(2)}, u32[]{:S(2)}) collective-permute-start(f32[2304,128]{1,0:T(8,128)S(1)} %get-tuple-element.16.refs_5_), channel_id=1, source_target_pairs={{0,8},{16,24},{32,40},{48,56},{64,72},{80,88},{96,104},{112,120},{... | collective-permute-start | bytes 3538952 | tf_op jit(solution)/shard_map/ppermute | solution.py:260
  8.0 20.8 %collective-permute-start.5 = (f32[2304,128]{1,0:T(8,128)S(1)}, f32[2304,128]{1,0:T(8,128)S(1)}, u32[]{:S(2)}, u32[]{:S(2)}) collective-permute-start(f32[2304,128]{1,0:T(8,128)S(1)} %get-tuple-element.17.refs_6_), channel_id=1, source_target_pairs={{8,16},{9,17},{10,18},{11,19},{12,20},{13,21},{14,22},{15,23},{24,... | collective-permute-start | bytes 3538952 | tf_op jit(solution)/shard_map/ppermute | solution.py:260
  13.2 4.2 %collective-permute-start = (f32[8,32,128]{2,1,0:T(8,128)S(1)}, f32[8,32,128]{2,1,0:T(8,128)S(1)}, u32[]{:S(2)}, u32[]{:S(2)}) collective-permute-start(f32[8,32,128]{2,1,0:T(8,128)S(1)} %get-tuple-element.15.refs_3_), channel_id=1, source_target_pairs={{0,1},{2,3},{7,6},{5,4},{1,0},{3,2},{6,7},{4,5},{8,9},{10,11},{15,... | collective-permute-start | bytes 393224 | tf_op jit(solution)/shard_map/ppermute | solution.py:263
  14.5 2.9 %collective-permute-start.1 = (f32[8,32,128]{2,1,0:T(8,128)S(1)}, f32[8,32,128]{2,1,0:T(8,128)S(1)}, u32[]{:S(2)}, u32[]{:S(2)}) collective-permute-start(f32[8,32,128]{2,1,0:T(8,128)S(1)} %get-tuple-element.15.refs_3_), channel_id=1, source_target_pairs={{1,2},{3,7},{6,5},{2,1},{7,3},{5,6},{9,10},{11,15},{14,13},{10,9},... | collective-permute-start | bytes 393224 | tf_op jit(solution)/shard_map/ppermute | solution.py:263
  23.3 17.5 %collective-permute-start.2 = (f32[2304,128]{1,0:T(8,128)S(1)}, f32[2304,128]{1,0:T(8,128)S(1)}, u32[]{:S(2)}, u32[]{:S(2)}) collective-permute-start(f32[2304,128]{1,0:T(8,128)S(1)} %get-tuple-element.18.refs_5_), channel_id=1, source_target_pairs={{0,8},{16,24},{32,40},{48,56},{64,72},{80,88},{96,104},{112,120},{... | collective-permute-start | bytes 3538952 | tf_op jit(solution)/shard_map/ppermute | solution.py:260
  23.4 20.8 %collective-permute-start.3 = (f32[2304,128]{1,0:T(8,128)S(1)}, f32[2304,128]{1,0:T(8,128)S(1)}, u32[]{:S(2)}, u32[]{:S(2)}) collective-permute-start(f32[2304,128]{1,0:T(8,128)S(1)} %get-tuple-element.19.refs_6_), channel_id=1, source_target_pairs={{8,16},{9,17},{10,18},{11,19},{12,20},{13,21},{14,22},{15,23},{24,... | collective-permute-start | bytes 3538952 | tf_op jit(solution)/shard_map/ppermute | solution.py:260
  34.8 6.0 %collective-permute-start.6 = (f32[8,32,128]{2,1,0:T(8,128)S(1)}, f32[8,32,128]{2,1,0:T(8,128)S(1)}, u32[]{:S(2)}, u32[]{:S(2)}) collective-permute-start(f32[8,32,128]{2,1,0:T(8,128)S(1)} %slice_bitcast_fusion.refs_5_), channel_id=1, source_target_pairs={{0,1},{2,3},{7,6},{5,4},{1,0},{3,2},{6,7},{4,5},{8,9},{10,11},{15,... | collective-permute-start | bytes 393224 | tf_op jit(solution)/shard_map/ppermute | solution.py:263
  38.1 2.7 %collective-permute-start.7 = (f32[8,32,128]{2,1,0:T(8,128)S(1)}, f32[8,32,128]{2,1,0:T(8,128)S(1)}, u32[]{:S(2)}, u32[]{:S(2)}) collective-permute-start(f32[8,32,128]{2,1,0:T(8,128)S(1)} %slice_bitcast_fusion.refs_5_), channel_id=1, source_target_pairs={{1,2},{3,7},{6,5},{2,1},{7,3},{5,6},{9,10},{11,15},{14,13},{10,9},... | collective-permute-start | bytes 393224 | tf_op jit(solution)/shard_map/ppermute | solution.py:263

commit v6 on v5

--- a/solution.py
+++ b/solution.py
@@ -267,10 +267,12 @@
         first_a_kernel, (series, series, window, window, window, out(CX, STRIP, NZ)), [HBM] * 3,
         [taps] + [buffer(WINDOW + 2 * HALO)] * 3 + [padded] * 2 + [pltpu.SemaphoreType.DMA((3,))], "first_iteration_a", 6.0,
     )(u, r, s)
-    theirs_a = send(near_a, far_a)
+    far_a_in = lax.ppermute(far_a, ("gx", "ta"), far_pairs)
     near_b, far_b = kernel(
         first_b_kernel, (series, series), [VMEM] * 5, work, "first_iteration_b", 3.0, 2
     )(m, q, *halo(last), near_a, far_a)
+    near_a, near_b, far_b = lax.optimization_barrier((near_a, near_b, far_b))
+    theirs_a = lax.ppermute(near_a, "gx", near_pairs), far_a_in
     theirs_b = send(near_b, far_b)
     ends_a = kernel(
         second_a_kernel, out(4, CX, STRIP, NZ), [VMEM] * 5, work, "second_iteration_a", 12.0, 2

time: 72.2 us -> 71.7 us (level)
  the two profiles are of different devices: /device:TPU:25 before, /device:TPU:24 now
where the time goes in v6:
time: 71.7 us; the launch traced here: 71.5 us
  Pallas kernels  25.1 us (35%)
  blocking collectives  24.4 us (34%)
  starting transfers between devices  13.6 us (19%)
  waiting for transfers between devices  7.22 us (10%)
  local copies, waits for them, and re-layouts  1.07 us (1%)
    all_to_all x1, blocking collectives, local(): lax.all_to_all(blocks, ('gx', 'ta'), 0, 0, axis_index_groups=groups, tile...  24.4 us
    pallas_call x1, Pallas kernels, local(): kernel(first_a_kernel, (series, series, window, window, window, out(CX, S...  7.22 us
    pallas_call x1, Pallas kernels, local(): kernel(second_b_kernel, out(8, CX, STRIP, NZ), [VMEM] * 8, work, 'second_...  6.01 us
    pallas_call x1, Pallas kernels, local(): kernel(second_a_kernel, out(4, CX, STRIP, NZ), [VMEM] * 5, work, 'second_...  5.97 us
    pallas_call x1, Pallas kernels, local(): kernel(first_b_kernel, (series, series), [VMEM] * 5, work, 'first_iterati...  5.88 us
    ppermute x2, starting transfers between devices, halo(): lax.ppermute(strip, 'ta', even_pairs)  5.58 us
    ppermute x1, waiting for transfers between devices, local(): far_a_in = lax.ppermute(far_a, ('gx', 'ta'), far_pairs)  3.79 us
    ppermute x1, starting transfers between devices, local(): theirs_a = (lax.ppermute(near_a, 'gx', near_pairs), far_a_in)  2.75 us
  transfers between devices with their start and end apart: 8, of which 4 were waited for; matrix products, arithmetic and copies ran while one was open for 0% of the time, Pallas kernels for 17%

profile of v6, /device:TPU:24, one launch (start us, length us, event | category | flops | bytes accessed | tf_op | source)
XLA Modules:
  0.0 71.5 jit_solution(8634426027423590156)
XLA Ops:
  0.0 7.2 %first_iteration_a.1 = (f32[2304,128]{1,0:T(8,128)S(1)}, f32[2304,128]{1,0:T(8,128)S(1)}, f32[8,96,128]{2,1,0:T(8,128)S(1)}, f32[8,96,128]{2,1,0:T(8,128)S(1)}, ...) custom-call(f32[8,256,128]{2,1,0:T(8,128)} %refs_0_.1, f32[8,256,128]{2,1,0:T(8,128)} %refs_1_.1, f32[8,256,128]{2,1,0:T(8,128)} %refs_2_.1), custom_call_target="tpu_custom_call" | custom-call | bytes 21600000 | tf_op jit(solution)/shard_map/first_iteration_a/pallas_call | solution.py:266
  7.2 1.6 %collective-permute-start = (f32[8,32,128]{2,1,0:T(8,128)S(1)}, f32[8,32,128]{2,1,0:T(8,128)S(1)}, u32[]{:S(2)}, u32[]{:S(2)}) collective-permute-start(f32[8,32,128]{2,1,0:T(8,128)S(1)} %get-tuple-element.19.refs_3_), channel_id=1, source_target_pairs={{0,1},{2,3},{7,6},{5,4},{1,0},{3,2},{6,7},{4,5},{8,9},{10,11},{15,... | collective-permute-start | bytes 393224 | tf_op jit(solution)/shard_map/ppermute | solution.py:263
  8.8 0.7 collective-permute-start.1
  9.5 1.9 %collective-permute-start.5 = (f32[2304,128]{1,0:T(8,128)S(1)}, f32[2304,128]{1,0:T(8,128)S(1)}, u32[]{:S(2)}, u32[]{:S(2)}) collective-permute-start(f32[2304,128]{1,0:T(8,128)S(1)} %get-tuple-element.20.refs_6_), channel_id=1, source_target_pairs={{8,16},{9,17},{10,18},{11,19},{12,20},{13,21},{14,22},{15,23},{24,... | collective-permute-start | bytes 3538952 | tf_op jit(solution)/shard_map/ppermute | solution.py:270
  11.4 1.2 %collective-permute-done.refs_2_ = f32[8,32,128]{2,1,0:T(8,128)S(1)} collective-permute-done((f32[8,32,128]{2,1,0:T(8,128)S(1)}, f32[8,32,128]{2,1,0:T(8,128)S(1)}, u32[]{:S(2)}, u32[]{:S(2)}) %collective-permute-start) | collective-permute-done | bytes 131104 | tf_op jit(solution)/shard_map/ppermute | solution.py:263
  12.5 0.0 collective-permute-done.1.refs_4_
  12.6 5.9 %first_iteration_b.1 = (f32[2304,128]{1,0:T(8,128)S(1)}, f32[2304,128]{1,0:T(8,128)S(1)}) custom-call(f32[8,96,128]{2,1,0:T(8,128)S(1)} %get-tuple-element.16.refs_0_.refs_1_, f32[8,96,128]{2,1,0:T(8,128)S(1)} %get-tuple-element.17.refs_1_.refs_2_, f32[8,32,128]{2,1,0:T(8,128)S(1)} %collective-permute-done.refs_2_, ...), custom_call_target="tpu_custom_call" | custom-call | bytes 10800000 | tf_op jit(solution)/shard_map/first_iteration_b/pallas_call | solution.py:271
  18.4 2.8 %collective-permute-start.4 = (f32[2304,128]{1,0:T(8,128)S(1)}, f32[2304,128]{1,0:T(8,128)S(1)}, u32[]{:S(2)}, u32[]{:S(2)}) collective-permute-start(f32[2304,128]{1,0:T(8,128)S(1)} %get-tuple-element.26.refs_5_), channel_id=1, source_target_pairs={{0,8},{16,24},{32,40},{48,56},{64,72},{80,88},{96,104},{112,120},{... | collective-permute-start | bytes 3538952 | tf_op jit(solution)/shard_map/ppermute | solution.py:275
  21.2 0.1 collective-permute-start.2
  21.3 1.9 %collective-permute-start.3 = (f32[2304,128]{1,0:T(8,128)S(1)}, f32[2304,128]{1,0:T(8,128)S(1)}, u32[]{:S(2)}, u32[]{:S(2)}) collective-permute-start(f32[2304,128]{1,0:T(8,128)S(1)} %get-tuple-element.24.refs_6_), channel_id=1, source_target_pairs={{8,16},{9,17},{10,18},{11,19},{12,20},{13,21},{14,22},{15,23},{24,... | collective-permute-start | bytes 3538952 | tf_op jit(solution)/shard_map/ppermute | solution.py:260
  23.2 3.8 %collective-permute-done.5.refs_4_ = f32[2304,128]{1,0:T(8,128)S(1)} collective-permute-done((f32[2304,128]{1,0:T(8,128)S(1)}, f32[2304,128]{1,0:T(8,128)S(1)}, u32[]{:S(2)}, u32[]{:S(2)}) %collective-permute-start.5) | collective-permute-done | bytes 1179680 | tf_op jit(solution)/shard_map/ppermute | solution.py:270
  27.0 0.0 collective-permute-done.4.refs_3_
  27.0 6.0 %second_iteration_a.1.refs_7_ = f32[4,8,32,128]{3,2,1,0:T(8,128)S(1)} custom-call(f32[8,96,128]{2,1,0:T(8,128)S(1)} %get-tuple-element.25.refs_0_, f32[8,96,128]{2,1,0:T(8,128)S(1)} %get-tuple-element.16.refs_0_.refs_1_, f32[8,96,128]{2,1,0:T(8,128)S(1)} %get-tuple-element.17.refs_1_.refs_2_, f32[2304,128]{1,0:T(8,128)S(1)} %collective-permute-done.4.refs_3_, ...), custom_call_target="tpu_custom_call" | custom-call | bytes 43200000 | tf_op jit(solution)/shard_map/second_iteration_a/pallas_call | solution.py:277
  33.0 4.0 %collective-permute-start.6 = (f32[8,32,128]{2,1,0:T(8,128)S(1)}, f32[8,32,128]{2,1,0:T(8,128)S(1)}, u32[]{:S(2)}, u32[]{:S(2)}) collective-permute-start(f32[8,32,128]{2,1,0:T(8,128)S(1)} %slice_bitcast_fusion.refs_5_), channel_id=1, source_target_pairs={{0,1},{2,3},{7,6},{5,4},{1,0},{3,2},{6,7},{4,5},{8,9},{10,11},{15,... | collective-permute-start | bytes 393224 | tf_op jit(solution)/shard_map/ppermute | solution.py:263
  37.0 0.7 collective-permute-start.7
  37.7 0.0 collective-permute-done.2.refs_2_
  37.7 2.0 %collective-permute-done.3.refs_3_ = f32[2304,128]{1,0:T(8,128)S(1)} collective-permute-done((f32[2304,128]{1,0:T(8,128)S(1)}, f32[2304,128]{1,0:T(8,128)S(1)}, u32[]{:S(2)}, u32[]{:S(2)}) %collective-permute-start.3) | collective-permute-done | bytes 1179680 | tf_op jit(solution)/shard_map/ppermute | solution.py:260
  39.6 0.3 collective-permute-done.6.refs_4_
  39.9 0.0 collective-permute-done.7.refs_6_
  39.9 6.0 %second_iteration_b.1 = f32[8,8,32,128]{3,2,1,0:T(8,128)S(1)} custom-call(f32[8,96,128]{2,1,0:T(8,128)S(1)} %get-tuple-element.16.refs_0_.refs_1_, f32[8,96,128]{2,1,0:T(8,128)S(1)} %get-tuple-element.17.refs_1_.refs_2_, f32[2304,128]{1,0:T(8,128)S(1)} %collective-permute-done.2.refs_2_, f32[2304,128]{1,0:T(8,128)S(1)} %collective-permute-done.3.refs_3_, ...), custom_call_target="tpu_custom_call" | custom-call | bytes 10800000 | tf_op jit(solution)/shard_map/second_iteration_b/pallas_call | solution.py:280
  46.0 24.4 %all_to_all.5 = f32[8,8,32,128]{3,2,1,0:T(8,128)S(1)} all-to-all(f32[8,8,32,128]{3,2,1,0:T(8,128)S(1)} %second_iteration_b.1), channel_id=1, replica_groups={{0,1,2,3,7,6,5,4},{8,9,10,11,15,14,13,12},{16,17,18,19,23,22,21,20},{24..., dimensions={0} | all-to-all | bytes 2097152 | tf_op jit(solution)/shard_map/all_to_all | solution.py:284
  70.4 1.1 %copy.4 = f32[8,8,32,128]{3,2,1,0:T(8,128)} copy(f32[8,8,32,128]{3,2,0,1:T(8,128)S(1)} %bitcast.4) | data formatting | bytes 2097152 | tf_op jit(solution)/shard_map/transpose | solution.py:285
  (1 shorter events, 0.0 us)
Async XLA Ops:
  7.2 5.3 %collective-permute-start = (f32[8,32,128]{2,1,0:T(8,128)S(1)}, f32[8,32,128]{2,1,0:T(8,128)S(1)}, u32[]{:S(2)}, u32[]{:S(2)}) collective-permute-start(f32[8,32,128]{2,1,0:T(8,128)S(1)} %get-tuple-element.19.refs_3_), channel_id=1, source_target_pairs={{0,1},{2,3},{7,6},{5,4},{1,0},{3,2},{6,7},{4,5},{8,9},{10,11},{15,... | collective-permute-start | bytes 393224 | tf_op jit(solution)/shard_map/ppermute | solution.py:263
  8.8 3.8 %collective-permute-start.1 = (f32[8,32,128]{2,1,0:T(8,128)S(1)}, f32[8,32,128]{2,1,0:T(8,128)S(1)}, u32[]{:S(2)}, u32[]{:S(2)}) collective-permute-start(f32[8,32,128]{2,1,0:T(8,128)S(1)} %get-tuple-element.19.refs_3_), channel_id=1, source_target_pairs={{1,2},{3,7},{6,5},{2,1},{7,3},{5,6},{9,10},{11,15},{14,13},{10,9},... | collective-permute-start | bytes 393224 | tf_op jit(solution)/shard_map/ppermute | solution.py:263
  9.5 17.5 %collective-permute-start.5 = (f32[2304,128]{1,0:T(8,128)S(1)}, f32[2304,128]{1,0:T(8,128)S(1)}, u32[]{:S(2)}, u32[]{:S(2)}) collective-permute-start(f32[2304,128]{1,0:T(8,128)S(1)} %get-tuple-element.20.refs_6_), channel_id=1, source_target_pairs={{8,16},{9,17},{10,18},{11,19},{12,20},{13,21},{14,22},{15,23},{24,... | collective-permute-start | bytes 3538952 | tf_op jit(solution)/shard_map/ppermute | solution.py:270
  18.4 8.6 %collective-permute-start.4 = (f32[2304,128]{1,0:T(8,128)S(1)}, f32[2304,128]{1,0:T(8,128)S(1)}, u32[]{:S(2)}, u32[]{:S(2)}) collective-permute-start(f32[2304,128]{1,0:T(8,128)S(1)} %get-tuple-element.26.refs_5_), channel_id=1, source_target_pairs={{0,8},{16,24},{32,40},{48,56},{64,72},{80,88},{96,104},{112,120},{... | collective-permute-start | bytes 3538952 | tf_op jit(solution)/shard_map/ppermute | solution.py:275
  21.2 16.5 %collective-permute-start.2 = (f32[2304,128]{1,0:T(8,128)S(1)}, f32[2304,128]{1,0:T(8,128)S(1)}, u32[]{:S(2)}, u32[]{:S(2)}) collective-permute-start(f32[2304,128]{1,0:T(8,128)S(1)} %get-tuple-element.23.refs_5_), channel_id=1, source_target_pairs={{0,8},{16,24},{32,40},{48,56},{64,72},{80,88},{96,104},{112,120},{... | collective-permute-start | bytes 3538952 | tf_op jit(solution)/shard_map/ppermute | solution.py:260
  21.3 18.3 %collective-permute-start.3 = (f32[2304,128]{1,0:T(8,128)S(1)}, f32[2304,128]{1,0:T(8,128)S(1)}, u32[]{:S(2)}, u32[]{:S(2)}) collective-permute-start(f32[2304,128]{1,0:T(8,128)S(1)} %get-tuple-element.24.refs_6_), channel_id=1, source_target_pairs={{8,16},{9,17},{10,18},{11,19},{12,20},{13,21},{14,22},{15,23},{24,... | collective-permute-start | bytes 3538952 | tf_op jit(solution)/shard_map/ppermute | solution.py:260
  33.0 7.0 %collective-permute-start.6 = (f32[8,32,128]{2,1,0:T(8,128)S(1)}, f32[8,32,128]{2,1,0:T(8,128)S(1)}, u32[]{:S(2)}, u32[]{:S(2)}) collective-permute-start(f32[8,32,128]{2,1,0:T(8,128)S(1)} %slice_bitcast_fusion.refs_5_), channel_id=1, source_target_pairs={{0,1},{2,3},{7,6},{5,4},{1,0},{3,2},{6,7},{4,5},{8,9},{10,11},{15,... | collective-permute-start | bytes 393224 | tf_op jit(solution)/shard_map/ppermute | solution.py:263
  37.0 3.0 %collective-permute-start.7 = (f32[8,32,128]{2,1,0:T(8,128)S(1)}, f32[8,32,128]{2,1,0:T(8,128)S(1)}, u32[]{:S(2)}, u32[]{:S(2)}) collective-permute-start(f32[8,32,128]{2,1,0:T(8,128)S(1)} %slice_bitcast_fusion.refs_5_), channel_id=1, source_target_pairs={{1,2},{3,7},{6,5},{2,1},{7,3},{5,6},{9,10},{11,15},{14,13},{10,9},... | collective-permute-start | bytes 393224 | tf_op jit(solution)/shard_map/ppermute | solution.py:263

commit v7 on v6

--- a/solution.py
+++ b/solution.py
@@ -14,7 +14,7 @@
 STEPS = 8
 PAD = 8
 SERIES = STEPS * sum(range(WINDOW, STRIP, -16))
-GROUP = 4
+GROUP = 6
 SNAKE = (0, 1, 2, 3, 7, 6, 5, 4)
 BY_MATRIX = 4
 
@@ -52,8 +52,9 @@
     lane = lax.broadcasted_iota(jnp.int32, (8, NZ), 1)
     not_first, not_last = lane != 0, lane != NZ - 1
     tiles = list(tiles)
-    for begin in range(0, len(tiles), GROUP):
-        group = tiles[begin : begin + GROUP]
+    groups = -(-len(tiles) // GROUP)
+    for n in range(groups):
+        group = tiles[n * len(tiles) // groups : (n + 1) * len(tiles) // groups]
         cells = [[src[x, PAD + 8 * t : PAD + 8 * t + 8, :] for x in range(CX)] for t in group]
         z_all = z_sum(jnp.concatenate([c[x] for c in cells for x in range(BY_MATRIX)], 0), taps)
         for at, t in enumerate(group):

time: 71.7 us -> 71.3 us (level)
  transfers between devices with their start and end apart: 8 -> 8, of which waited for: 4 -> 4; matrix products, arithmetic and copies ran while one was open for 0% -> 0% of each run, Pallas kernels for 17% -> 16%
where the time goes in v7:
time: 71.3 us; the launch traced here: 71.1 us
  Pallas kernels  24.6 us (35%)
  blocking collectives  24.5 us (34%)
  starting transfers between devices  13.6 us (19%)
  waiting for transfers between devices  7.31 us (10%)
  local copies, waits for them, and re-layouts  1.07 us (2%)
    all_to_all x1, blocking collectives, local(): lax.all_to_all(blocks, ('gx', 'ta'), 0, 0, axis_index_groups=groups, tile...  24.5 us
    pallas_call x1, Pallas kernels, local(): kernel(first_a_kernel, (series, series, window, window, window, out(CX, S...  7.12 us
    pallas_call x1, Pallas kernels, local(): kernel(second_b_kernel, out(8, CX, STRIP, NZ), [VMEM] * 8, work, 'second_...  5.88 us
    pallas_call x1, Pallas kernels, local(): kernel(second_a_kernel, out(4, CX, STRIP, NZ), [VMEM] * 5, work, 'second_...  5.83 us
    pallas_call x1, Pallas kernels, local(): kernel(first_b_kernel, (series, series), [VMEM] * 5, work, 'first_iterati...  5.79 us
    ppermute x2, starting transfers between devices, halo(): lax.ppermute(strip, 'ta', even_pairs)  5.58 us
    ppermute x1, waiting for transfers between devices, local(): far_a_in = lax.ppermute(far_a, ('gx', 'ta'), far_pairs)  3.88 us
    ppermute x1, starting transfers between devices, local(): theirs_a = (lax.ppermute(near_a, 'gx', near_pairs), far_a_in)  2.75 us
  transfers between devices with their start and end apart: 8, of which 4 were waited for; matrix products, arithmetic and copies ran while one was open for 0% of the time, Pallas kernels for 16%

profile of v7, /device:TPU:24, one launch (start us, length us, event | category | flops | bytes accessed | tf_op | source)
XLA Modules:
  0.0 71.1 jit_solution(10751769899659999629)
XLA Ops:
  0.0 7.1 %first_iteration_a.1 = (f32[2304,128]{1,0:T(8,128)S(1)}, f32[2304,128]{1,0:T(8,128)S(1)}, f32[8,96,128]{2,1,0:T(8,128)S(1)}, f32[8,96,128]{2,1,0:T(8,128)S(1)}, ...) custom-call(f32[8,256,128]{2,1,0:T(8,128)} %refs_0_.1, f32[8,256,128]{2,1,0:T(8,128)} %refs_1_.1, f32[8,256,128]{2,1,0:T(8,128)} %refs_2_.1), custom_call_target="tpu_custom_call" | custom-call | bytes 21600000 | tf_op jit(solution)/shard_map/first_iteration_a/pallas_call | solution.py:267
  7.1 1.6 %collective-permute-start = (f32[8,32,128]{2,1,0:T(8,128)S(1)}, f32[8,32,128]{2,1,0:T(8,128)S(1)}, u32[]{:S(2)}, u32[]{:S(2)}) collective-permute-start(f32[8,32,128]{2,1,0:T(8,128)S(1)} %get-tuple-element.19.refs_3_), channel_id=1, source_target_pairs={{0,1},{2,3},{7,6},{5,4},{1,0},{3,2},{6,7},{4,5},{8,9},{10,11},{15,... | collective-permute-start | bytes 393224 | tf_op jit(solution)/shard_map/ppermute | solution.py:264
  8.7 0.7 collective-permute-start.1
  9.4 1.9 %collective-permute-start.5 = (f32[2304,128]{1,0:T(8,128)S(1)}, f32[2304,128]{1,0:T(8,128)S(1)}, u32[]{:S(2)}, u32[]{:S(2)}) collective-permute-start(f32[2304,128]{1,0:T(8,128)S(1)} %get-tuple-element.20.refs_6_), channel_id=1, source_target_pairs={{8,16},{9,17},{10,18},{11,19},{12,20},{13,21},{14,22},{15,23},{24,... | collective-permute-start | bytes 3538952 | tf_op jit(solution)/shard_map/ppermute | solution.py:271
  11.3 1.1 %collective-permute-done.refs_2_ = f32[8,32,128]{2,1,0:T(8,128)S(1)} collective-permute-done((f32[8,32,128]{2,1,0:T(8,128)S(1)}, f32[8,32,128]{2,1,0:T(8,128)S(1)}, u32[]{:S(2)}, u32[]{:S(2)}) %collective-permute-start) | collective-permute-done | bytes 131104 | tf_op jit(solution)/shard_map/ppermute | solution.py:264
  12.4 0.0 collective-permute-done.1.refs_4_
  12.5 5.8 %first_iteration_b.1 = (f32[2304,128]{1,0:T(8,128)S(1)}, f32[2304,128]{1,0:T(8,128)S(1)}) custom-call(f32[8,96,128]{2,1,0:T(8,128)S(1)} %get-tuple-element.16.refs_0_.refs_1_, f32[8,96,128]{2,1,0:T(8,128)S(1)} %get-tuple-element.17.refs_1_.refs_2_, f32[8,32,128]{2,1,0:T(8,128)S(1)} %collective-permute-done.refs_2_, ...), custom_call_target="tpu_custom_call" | custom-call | bytes 10800000 | tf_op jit(solution)/shard_map/first_iteration_b/pallas_call | solution.py:272
  18.3 2.8 %collective-permute-start.4 = (f32[2304,128]{1,0:T(8,128)S(1)}, f32[2304,128]{1,0:T(8,128)S(1)}, u32[]{:S(2)}, u32[]{:S(2)}) collective-permute-start(f32[2304,128]{1,0:T(8,128)S(1)} %get-tuple-element.26.refs_5_), channel_id=1, source_target_pairs={{0,8},{16,24},{32,40},{48,56},{64,72},{80,88},{96,104},{112,120},{... | collective-permute-start | bytes 3538952 | tf_op jit(solution)/shard_map/ppermute | solution.py:276
  21.0 0.1 collective-permute-start.2
  21.1 1.9 %collective-permute-start.3 = (f32[2304,128]{1,0:T(8,128)S(1)}, f32[2304,128]{1,0:T(8,128)S(1)}, u32[]{:S(2)}, u32[]{:S(2)}) collective-permute-start(f32[2304,128]{1,0:T(8,128)S(1)} %get-tuple-element.24.refs_6_), channel_id=1, source_target_pairs={{8,16},{9,17},{10,18},{11,19},{12,20},{13,21},{14,22},{15,23},{24,... | collective-permute-start | bytes 3538952 | tf_op jit(solution)/shard_map/ppermute | solution.py:261
  23.0 3.9 %collective-permute-done.5.refs_4_ = f32[2304,128]{1,0:T(8,128)S(1)} collective-permute-done((f32[2304,128]{1,0:T(8,128)S(1)}, f32[2304,128]{1,0:T(8,128)S(1)}, u32[]{:S(2)}, u32[]{:S(2)}) %collective-permute-start.5) | collective-permute-done | bytes 1179680 | tf_op jit(solution)/shard_map/ppermute | solution.py:271
  26.9 0.0 collective-permute-done.4.refs_3_
  26.9 5.8 %second_iteration_a.1.refs_7_ = f32[4,8,32,128]{3,2,1,0:T(8,128)S(1)} custom-call(f32[8,96,128]{2,1,0:T(8,128)S(1)} %get-tuple-element.25.refs_0_, f32[8,96,128]{2,1,0:T(8,128)S(1)} %get-tuple-element.16.refs_0_.refs_1_, f32[8,96,128]{2,1,0:T(8,128)S(1)} %get-tuple-element.17.refs_1_.refs_2_, f32[2304,128]{1,0:T(8,128)S(1)} %collective-permute-done.4.refs_3_, ...), custom_call_target="tpu_custom_call" | custom-call | bytes 43200000 | tf_op jit(solution)/shard_map/second_iteration_a/pallas_call | solution.py:278
  32.8 4.0 %collective-permute-start.6 = (f32[8,32,128]{2,1,0:T(8,128)S(1)}, f32[8,32,128]{2,1,0:T(8,128)S(1)}, u32[]{:S(2)}, u32[]{:S(2)}) collective-permute-start(f32[8,32,128]{2,1,0:T(8,128)S(1)} %slice_bitcast_fusion.refs_5_), channel_id=1, source_target_pairs={{0,1},{2,3},{7,6},{5,4},{1,0},{3,2},{6,7},{4,5},{8,9},{10,11},{15,... | collective-permute-start | bytes 393224 | tf_op jit(solution)/shard_map/ppermute | solution.py:264
  36.8 0.7 collective-permute-start.7
  37.4 0.0 collective-permute-done.2.refs_2_
  37.4 2.1 %collective-permute-done.3.refs_3_ = f32[2304,128]{1,0:T(8,128)S(1)} collective-permute-done((f32[2304,128]{1,0:T(8,128)S(1)}, f32[2304,128]{1,0:T(8,128)S(1)}, u32[]{:S(2)}, u32[]{:S(2)}) %collective-permute-start.3) | collective-permute-done | bytes 1179680 | tf_op jit(solution)/shard_map/ppermute | solution.py:261
  39.5 0.2 collective-permute-done.6.refs_4_
  39.7 0.0 collective-permute-done.7.refs_6_
  39.7 5.9 %second_iteration_b.1 = f32[8,8,32,128]{3,2,1,0:T(8,128)S(1)} custom-call(f32[8,96,128]{2,1,0:T(8,128)S(1)} %get-tuple-element.16.refs_0_.refs_1_, f32[8,96,128]{2,1,0:T(8,128)S(1)} %get-tuple-element.17.refs_1_.refs_2_, f32[2304,128]{1,0:T(8,128)S(1)} %collective-permute-done.2.refs_2_, f32[2304,128]{1,0:T(8,128)S(1)} %collective-permute-done.3.refs_3_, ...), custom_call_target="tpu_custom_call" | custom-call | bytes 10800000 | tf_op jit(solution)/shard_map/second_iteration_b/pallas_call | solution.py:281
  45.6 24.5 %all_to_all.5 = f32[8,8,32,128]{3,2,1,0:T(8,128)S(1)} all-to-all(f32[8,8,32,128]{3,2,1,0:T(8,128)S(1)} %second_iteration_b.1), channel_id=1, replica_groups={{0,1,2,3,7,6,5,4},{8,9,10,11,15,14,13,12},{16,17,18,19,23,22,21,20},{24..., dimensions={0} | all-to-all | bytes 2097152 | tf_op jit(solution)/shard_map/all_to_all | solution.py:285
  70.1 1.1 %copy.4 = f32[8,8,32,128]{3,2,1,0:T(8,128)} copy(f32[8,8,32,128]{3,2,0,1:T(8,128)S(1)} %bitcast.4) | data formatting | bytes 2097152 | tf_op jit(solution)/shard_map/transpose | solution.py:286
  (1 shorter events, 0.0 us)
Async XLA Ops:
  7.1 5.3 %collective-permute-start = (f32[8,32,128]{2,1,0:T(8,128)S(1)}, f32[8,32,128]{2,1,0:T(8,128)S(1)}, u32[]{:S(2)}, u32[]{:S(2)}) collective-permute-start(f32[8,32,128]{2,1,0:T(8,128)S(1)} %get-tuple-element.19.refs_3_), channel_id=1, source_target_pairs={{0,1},{2,3},{7,6},{5,4},{1,0},{3,2},{6,7},{4,5},{8,9},{10,11},{15,... | collective-permute-start | bytes 393224 | tf_op jit(solution)/shard_map/ppermute | solution.py:264
  8.7 3.7 %collective-permute-start.1 = (f32[8,32,128]{2,1,0:T(8,128)S(1)}, f32[8,32,128]{2,1,0:T(8,128)S(1)}, u32[]{:S(2)}, u32[]{:S(2)}) collective-permute-start(f32[8,32,128]{2,1,0:T(8,128)S(1)} %get-tuple-element.19.refs_3_), channel_id=1, source_target_pairs={{1,2},{3,7},{6,5},{2,1},{7,3},{5,6},{9,10},{11,15},{14,13},{10,9},... | collective-permute-start | bytes 393224 | tf_op jit(solution)/shard_map/ppermute | solution.py:264
  9.4 17.5 %collective-permute-start.5 = (f32[2304,128]{1,0:T(8,128)S(1)}, f32[2304,128]{1,0:T(8,128)S(1)}, u32[]{:S(2)}, u32[]{:S(2)}) collective-permute-start(f32[2304,128]{1,0:T(8,128)S(1)} %get-tuple-element.20.refs_6_), channel_id=1, source_target_pairs={{8,16},{9,17},{10,18},{11,19},{12,20},{13,21},{14,22},{15,23},{24,... | collective-permute-start | bytes 3538952 | tf_op jit(solution)/shard_map/ppermute | solution.py:271
  18.3 8.6 %collective-permute-start.4 = (f32[2304,128]{1,0:T(8,128)S(1)}, f32[2304,128]{1,0:T(8,128)S(1)}, u32[]{:S(2)}, u32[]{:S(2)}) collective-permute-start(f32[2304,128]{1,0:T(8,128)S(1)} %get-tuple-element.26.refs_5_), channel_id=1, source_target_pairs={{0,8},{16,24},{32,40},{48,56},{64,72},{80,88},{96,104},{112,120},{... | collective-permute-start | bytes 3538952 | tf_op jit(solution)/shard_map/ppermute | solution.py:276
  21.0 16.4 %collective-permute-start.2 = (f32[2304,128]{1,0:T(8,128)S(1)}, f32[2304,128]{1,0:T(8,128)S(1)}, u32[]{:S(2)}, u32[]{:S(2)}) collective-permute-start(f32[2304,128]{1,0:T(8,128)S(1)} %get-tuple-element.23.refs_5_), channel_id=1, source_target_pairs={{0,8},{16,24},{32,40},{48,56},{64,72},{80,88},{96,104},{112,120},{... | collective-permute-start | bytes 3538952 | tf_op jit(solution)/shard_map/ppermute | solution.py:261
  21.1 18.4 %collective-permute-start.3 = (f32[2304,128]{1,0:T(8,128)S(1)}, f32[2304,128]{1,0:T(8,128)S(1)}, u32[]{:S(2)}, u32[]{:S(2)}) collective-permute-start(f32[2304,128]{1,0:T(8,128)S(1)} %get-tuple-element.24.refs_6_), channel_id=1, source_target_pairs={{8,16},{9,17},{10,18},{11,19},{12,20},{13,21},{14,22},{15,23},{24,... | collective-permute-start | bytes 3538952 | tf_op jit(solution)/shard_map/ppermute | solution.py:261
  32.8 7.0 %collective-permute-start.6 = (f32[8,32,128]{2,1,0:T(8,128)S(1)}, f32[8,32,128]{2,1,0:T(8,128)S(1)}, u32[]{:S(2)}, u32[]{:S(2)}) collective-permute-start(f32[8,32,128]{2,1,0:T(8,128)S(1)} %slice_bitcast_fusion.refs_5_), channel_id=1, source_target_pairs={{0,1},{2,3},{7,6},{5,4},{1,0},{3,2},{6,7},{4,5},{8,9},{10,11},{15,... | collective-permute-start | bytes 393224 | tf_op jit(solution)/shard_map/ppermute | solution.py:264
  36.8 3.0 %collective-permute-start.7 = (f32[8,32,128]{2,1,0:T(8,128)S(1)}, f32[8,32,128]{2,1,0:T(8,128)S(1)}, u32[]{:S(2)}, u32[]{:S(2)}) collective-permute-start(f32[8,32,128]{2,1,0:T(8,128)S(1)} %slice_bitcast_fusion.refs_5_), channel_id=1, source_target_pairs={{1,2},{3,7},{6,5},{2,1},{7,3},{5,6},{9,10},{11,15},{14,13},{10,9},... | collective-permute-start | bytes 393224 | tf_op jit(solution)/shard_map/ppermute | solution.py:264
